TPU v7x, 512 devices: a whole 4x8x8 slice. The times are simulated.
512 devices in a mesh: row: 64 (over x, y_hi, z), col: 8 (over y_lo, core).
Axes of the slice: x: 4, y: 8 (y_hi: 2, y_lo: 4; y = y_hi * 4 + y_lo), z: 8, core: 2. Of those that a mesh axis runs over, the one named last changes fastest.
Arguments:
- features: bfloat16 [8, 512, 256, 128], P(None, 'row', 'col'), may hold values from -6 to 6
- kernel_one: bfloat16 [3, 3, 3, 128, 128], replicated, may hold values from -0.109375 to 0.109375
- projection: bfloat16 [512, 256], replicated, may hold values from -0.25 to 0.25
- kernel_two: bfloat16 [3, 3, 3, 256, 256], replicated, may hold values from -0.078125 to 0.078125
Outputs:
- latent: bfloat16 [8, 256, 128, 256], P(None, 'row', 'col')
All inputs are finite; a program needn't handle non-finite values.
Results may differ from a plain program's by a relative error of at most 0.017.
Values may be sent and summed in bfloat16 or wider, within the bound.
No kernel may reach another device: no remote copies, remote signals or barrier semaphores. Data moves between devices by JAX's collectives and lax.ppermute only.
A program may use at most 128 MiB of HBM per device.

v0:
```python
import jax
import jax.numpy as jnp
from jax import lax
from jax.sharding import PartitionSpec as P

NORM_EPS = 1e-06


def padded_2(block, sides, width):
    for axis, dim in sides:
        count = lax.axis_size(axis)
        forward = [(i, i + 1) for i in range(count - 1)]
        backward = [(target, source) for source, target in forward]
        low = lax.ppermute(
            lax.slice_in_dim(block, block.shape[dim] - width, None, axis=dim), axis, forward
        )
        high = lax.ppermute(lax.slice_in_dim(block, 0, width, axis=dim), axis, backward)
        block = jnp.concatenate([low, block, high], axis=dim)
    return block


def normed_silu(values):
    widened = values.astype(jnp.float32)
    scaled = widened * lax.rsqrt(jnp.mean(widened * widened, axis=-1, keepdims=True) + NORM_EPS)
    return jax.nn.silu(scaled).astype(jnp.bfloat16)


def padded_conv(padded, kernel):
    frame_count = padded.shape[0]
    row_count = padded.shape[1] - 2
    col_count = padded.shape[2] - 2
    channels = padded.shape[3]
    timed = jnp.pad(padded, ((2, 0), (0, 0), (0, 0), (0, 0)))
    summed = jnp.zeros((frame_count * row_count * col_count, kernel.shape[-1]), jnp.float32)
    for tap_t in range(3):
        window = timed[tap_t : tap_t + frame_count]
        stacked = jnp.concatenate(
            [
                window[:, tap_r : tap_r + row_count, tap_c : tap_c + col_count]
                for tap_r in range(3)
                for tap_c in range(3)
            ],
            axis=-1,
        )
        summed = summed + jnp.dot(
            stacked.reshape(-1, 9 * channels),
            kernel[tap_t].reshape(9 * channels, -1),
            preferred_element_type=jnp.float32,
        )
    return summed.reshape(frame_count, row_count, col_count, -1)


def haar_bands(values):
    widened = values.astype(jnp.float32)
    upper = widened[:, 0::2]
    lower = widened[:, 1::2]
    first = upper[:, :, 0::2]
    second = upper[:, :, 1::2]
    third = lower[:, :, 0::2]
    fourth = lower[:, :, 1::2]
    low_pass = (first + second + third + fourth) * 0.5
    across = (first + second - third - fourth) * 0.5
    along = (first - second + third - fourth) * 0.5
    diagonal = (first - second - third + fourth) * 0.5
    return jnp.concatenate([low_pass, across, along, diagonal], axis=-1).astype(jnp.bfloat16)


def level_two_input(bands, projection):
    width_one = bands.shape[-1] // 4
    low_pass = bands[..., :width_one].astype(jnp.float32)
    flat = bands.reshape(-1, bands.shape[-1])
    mixed = jnp.dot(flat, projection, preferred_element_type=jnp.float32)
    mixed = mixed.reshape(bands.shape[:3] + (projection.shape[-1],))
    return (mixed + jnp.concatenate([low_pass, low_pass], axis=-1)).astype(jnp.bfloat16)


def local(features, kernel_one, projection, kernel_two):
    active_one = normed_silu(features)
    around_one = padded_2(active_one, (("row", 1), ("col", 2)), 1)
    level_one = (features.astype(jnp.float32) + padded_conv(around_one, kernel_one)).astype(
        jnp.bfloat16
    )
    bands = haar_bands(level_one)
    level_two = level_two_input(bands, projection)
    active_two = normed_silu(level_two)
    around_two = padded_2(active_two, (("row", 1), ("col", 2)), 1)
    branch = padded_conv(around_two, kernel_two)
    return (level_two.astype(jnp.float32) + branch).astype(jnp.bfloat16)


def solution(mesh):
    return jax.shard_map(
        local,
        mesh=mesh,
        in_specs=(P(None, "row", "col", None), P(), P(), P()),
        out_specs=P(None, "row", "col", None),
        check_vma=False,
    )
```

profile of v0, /device:TPU:7, one launch (start us, length us, event | category | flops | bytes accessed | tf_op | source)
XLA Modules:
  0.0 73.0 jit_solution(3316185929013443973)
XLA Ops:
  0.0 1.5 %fusion.18 = f32[8,8,32]{2,1,0:T(8,128)S(1)} fusion(bf16[8,8,32,128]{3,2,1,0:T(8,128)(2,1)} %param.4), kind=kLoop, calls=%fused_computation.28 | loop fusion | flops 784384 | bytes 532480 | tf_op jit(solution)/shard_map/reduce_sum | solution.py:24
  1.5 1.4 %fusion.17 = bf16[8,8,32,128]{3,2,1,0:T(8,128)(2,1)S(1)} fusion(bf16[8,8,32,128]{3,2,1,0:T(8,128)(2,1)} %param.4, f32[8,8,32]{2,1,0:T(8,128)S(1)} %add_rsqrt_fusion), kind=kLoop, calls=%fused_computation.27 | loop fusion | flops 1835008 | bytes 1056768 | tf_op jit(solution)/shard_map/convert_element_type | solution.py:25
  2.9 4.0 %collective-permute-start = (bf16[8,1,32,128]{3,2,1,0:T(8,128)(2,1)S(1)}, bf16[8,1,32,128]{3,2,1,0:T(8,128)(2,1)S(1)}, u32[]{:S(2)}, u32[]{:S(2)}) collective-permute-start(bf16[8,1,32,128]{3,2,1,0:T(8,128)(2,1)S(1)} %get-tuple-element.57), channel_id=1, source_target_pairs={{0,8},{8,16},{16,24},{24,32},{32,40},{40,48},{48,56},{56,64},{64,7... | collective-permute-start | bytes 196616 | tf_op jit(solution)/shard_map/ppermute | solution.py:14
  6.9 14.1 %collective-permute-start.1 = (bf16[8,1,32,128]{3,2,1,0:T(8,128)(2,1)S(1)}, bf16[8,1,32,128]{3,2,1,0:T(8,128)(2,1)S(1)}, u32[]{:S(2)}, u32[]{:S(2)}) collective-permute-start(bf16[8,1,32,128]{3,2,1,0:T(8,128)(2,1)S(1)} %get-tuple-element.58), channel_id=1, source_target_pairs={{8,0},{16,8},{24,16},{32,24},{40,32},{48,40},{56,48},{64,56},{72,6... | collective-permute-start | bytes 196616 | tf_op jit(solution)/shard_map/ppermute | solution.py:17
  21.1 1.6 %collective-permute-done.1 = bf16[8,1,32,128]{3,2,1,0:T(8,128)(2,1)S(1)} collective-permute-done((bf16[8,1,32,128]{3,2,1,0:T(8,128)(2,1)S(1)}, bf16[8,1,32,128]{3,2,1,0:T(8,128)(2,1)S(1)}, u32[]{:S(2)}, u32[]{:S(2)}) %collective-permute-start.1) | collective-permute-done | bytes 65568 | tf_op jit(solution)/shard_map/ppermute | solution.py:17
  22.7 3.5 %collective-permute-start.2 = (bf16[8,10,1,128]{3,2,1,0:T(2,128)(2,1)S(1)}, bf16[8,10,1,128]{3,2,1,0:T(2,128)(2,1)S(1)}, u32[]{:S(2)}, u32[]{:S(2)}) collective-permute-start(bf16[8,10,1,128]{3,2,1,0:T(2,128)(2,1)S(1)} %get-tuple-element.55), channel_id=1, source_target_pairs={{0,1},{1,2},{2,3},{3,4},{4,5},{5,6},{6,7},{8,9},{9,10},{10,11},{11... | collective-permute-start | bytes 61448 | tf_op jit(solution)/shard_map/ppermute | solution.py:14
  26.2 1.9 %collective-permute-start.3 = (bf16[8,10,1,128]{3,2,1,0:T(2,128)(2,1)S(1)}, bf16[8,10,1,128]{3,2,1,0:T(2,128)(2,1)S(1)}, u32[]{:S(2)}, u32[]{:S(2)}) collective-permute-start(bf16[8,10,1,128]{3,2,1,0:T(2,128)(2,1)S(1)} %get-tuple-element.56), channel_id=1, source_target_pairs={{1,0},{2,1},{3,2},{4,3},{5,4},{6,5},{7,6},{9,8},{10,9},{11,10},{12... | collective-permute-start | bytes 61448 | tf_op jit(solution)/shard_map/ppermute | solution.py:17
  28.2 3.3 %collective-permute-done.3 = bf16[8,10,1,128]{3,2,1,0:T(2,128)(2,1)S(1)} collective-permute-done((bf16[8,10,1,128]{3,2,1,0:T(2,128)(2,1)S(1)}, bf16[8,10,1,128]{3,2,1,0:T(2,128)(2,1)S(1)}, u32[]{:S(2)}, u32[]{:S(2)}) %collective-permute-start.3) | collective-permute-done | bytes 20512 | tf_op jit(solution)/shard_map/ppermute | solution.py:17
  32.2 0.6 pad_maximum_fusion
  33.8 0.5 constant_dynamic-update-slice_fusion
  38.5 1.4 %fusion.47 = f32[2048,128]{1,0:T(8,128)S(1)} fusion(bf16[2048,1152]{1,0:T(8,128)(2,1)S(1)} %bitcast.35, bf16[1152,128]{1,0:T(8,128)(2,1)S(1)} %bitcast.44), kind=kOutput, calls=%fused_computation.130 | convolution fusion | flops 603979776 | bytes 6062080 | tf_op jit(solution)/shard_map/dot_general | solution.py:45
  39.9 1.4 %convolution_add_fusion.1 = f32[2048,128]{1,0:T(8,128)S(1)} fusion(f32[2048,128]{1,0:T(8,128)S(1)} %fusion.47, bf16[2048,1152]{1,0:T(8,128)(2,1)S(1)} %bitcast.33, bf16[1152,128]{1,0:T(8,128)(2,1)S(1)} %bitcast.43), kind=kOutput, calls=%fused_computation.1 | convolution fusion | flops 604241920 | bytes 7110656 | tf_op jit(solution)/shard_map/dot_general | solution.py:45
  41.3 1.4 %convolution_add_fusion = f32[2048,128]{1,0:T(8,128)S(1)} fusion(f32[2048,128]{1,0:T(8,128)S(1)} %convolution_add_fusion.1, bf16[2048,1152]{1,0:T(8,128)(2,1)S(1)} %bitcast.34, bf16[1152,128]{1,0:T(8,128)(2,1)S(1)} %bitcast.42), kind=kOutput, calls=%fused_computation | convolution fusion | flops 604241920 | bytes 7110656 | tf_op jit(solution)/shard_map/dot_general | solution.py:45
  44.6 2.1 %collective-permute-start.4 = (bf16[8,1,16,256]{3,2,1,0:T(8,128)(2,1)S(1)}, bf16[8,1,16,256]{3,2,1,0:T(8,128)(2,1)S(1)}, u32[]{:S(2)}, u32[]{:S(2)}) collective-permute-start(bf16[8,1,16,256]{3,2,1,0:T(8,128)(2,1)S(1)} %get-tuple-element.63), channel_id=1, source_target_pairs={{0,8},{8,16},{16,24},{24,32},{32,40},{40,48},{48,56},{56,64},{64,7... | collective-permute-start | bytes 196616 | tf_op jit(solution)/shard_map/ppermute | solution.py:14
  46.7 11.0 %collective-permute-start.5 = (bf16[8,1,16,256]{3,2,1,0:T(8,128)(2,1)S(1)}, bf16[8,1,16,256]{3,2,1,0:T(8,128)(2,1)S(1)}, u32[]{:S(2)}, u32[]{:S(2)}) collective-permute-start(bf16[8,1,16,256]{3,2,1,0:T(8,128)(2,1)S(1)} %get-tuple-element.64), channel_id=1, source_target_pairs={{8,0},{16,8},{24,16},{32,24},{40,32},{48,40},{56,48},{64,56},{72,6... | collective-permute-start | bytes 196616 | tf_op jit(solution)/shard_map/ppermute | solution.py:17
  57.7 1.1 %collective-permute-done.4 = bf16[8,1,16,256]{3,2,1,0:T(8,128)(2,1)S(1)} collective-permute-done((bf16[8,1,16,256]{3,2,1,0:T(8,128)(2,1)S(1)}, bf16[8,1,16,256]{3,2,1,0:T(8,128)(2,1)S(1)}, u32[]{:S(2)}, u32[]{:S(2)}) %collective-permute-start.4) | collective-permute-done | bytes 65568 | tf_op jit(solution)/shard_map/ppermute | solution.py:14
  58.8 1.3 %collective-permute-done.5 = bf16[8,1,16,256]{3,2,1,0:T(8,128)(2,1)S(1)} collective-permute-done((bf16[8,1,16,256]{3,2,1,0:T(8,128)(2,1)S(1)}, bf16[8,1,16,256]{3,2,1,0:T(8,128)(2,1)S(1)}, u32[]{:S(2)}, u32[]{:S(2)}) %collective-permute-start.5) | collective-permute-done | bytes 65568 | tf_op jit(solution)/shard_map/ppermute | solution.py:17
  60.2 2.1 %collective-permute-start.6 = (bf16[8,6,1,256]{3,2,1,0:T(2,128)(2,1)S(1)}, bf16[8,6,1,256]{3,2,1,0:T(2,128)(2,1)S(1)}, u32[]{:S(2)}, u32[]{:S(2)}) collective-permute-start(bf16[8,6,1,256]{3,2,1,0:T(2,128)(2,1)S(1)} %get-tuple-element.61), channel_id=1, source_target_pairs={{0,1},{1,2},{2,3},{3,4},{4,5},{5,6},{6,7},{8,9},{9,10},{10,11},{11... | collective-permute-start | bytes 73736 | tf_op jit(solution)/shard_map/ppermute | solution.py:14
  62.3 2.4 %collective-permute-start.7 = (bf16[8,6,1,256]{3,2,1,0:T(2,128)(2,1)S(1)}, bf16[8,6,1,256]{3,2,1,0:T(2,128)(2,1)S(1)}, u32[]{:S(2)}, u32[]{:S(2)}) collective-permute-start(bf16[8,6,1,256]{3,2,1,0:T(2,128)(2,1)S(1)} %get-tuple-element.62), channel_id=1, source_target_pairs={{1,0},{2,1},{3,2},{4,3},{5,4},{6,5},{7,6},{9,8},{10,9},{11,10},{12... | collective-permute-start | bytes 73736 | tf_op jit(solution)/shard_map/ppermute | solution.py:17
  65.1 2.6 %collective-permute-done.7 = bf16[8,6,1,256]{3,2,1,0:T(2,128)(2,1)S(1)} collective-permute-done((bf16[8,6,1,256]{3,2,1,0:T(2,128)(2,1)S(1)}, bf16[8,6,1,256]{3,2,1,0:T(2,128)(2,1)S(1)}, u32[]{:S(2)}, u32[]{:S(2)}) %collective-permute-start.7) | collective-permute-done | bytes 24608 | tf_op jit(solution)/shard_map/ppermute | solution.py:17
  69.8 0.8 %fusion.48 = f32[512,256]{1,0:T(8,128)S(1)} fusion(bf16[512,2304]{1,0:T(8,128)(2,1)S(1)} %bitcast.46, bf16[2304,256]{1,0:T(8,128)(2,1)S(1)} %bitcast.45), kind=kOutput, calls=%fused_computation.131 | convolution fusion | flops 603979776 | bytes 4063232 | tf_op jit(solution)/shard_map/dot_general | solution.py:45
  70.6 0.8 %convolution_add_fusion.3 = f32[512,256]{1,0:T(8,128)S(1)} fusion(f32[512,256]{1,0:T(8,128)S(1)} %fusion.48, bf16[512,2304]{1,0:T(8,128)(2,1)S(1)} %bitcast.39, bf16[2304,256]{1,0:T(8,128)(2,1)S(1)} %bitcast.38), kind=kOutput, calls=%fused_computation.20 | convolution fusion | flops 604110848 | bytes 4587520 | tf_op jit(solution)/shard_map/dot_general | solution.py:45
  71.4 0.8 %convolution_add_fusion.2 = f32[512,256]{1,0:T(8,128)S(1)} fusion(f32[512,256]{1,0:T(8,128)S(1)} %convolution_add_fusion.3, bf16[512,2304]{1,0:T(8,128)(2,1)S(1)} %bitcast.40, bf16[2304,256]{1,0:T(8,128)(2,1)S(1)} %bitcast.37), kind=kOutput, calls=%fused_computation.19 | convolution fusion | flops 604110848 | bytes 4587520 | tf_op jit(solution)/shard_map/dot_general | solution.py:45
  72.2 0.8 %add_convert_fusion = bf16[8,4,16,256]{3,2,1,0:T(8,128)(2,1)} fusion(f32[8,4,16,256]{3,2,1,0:T(8,128)S(1)} %get-tuple-element.66, f32[8,4,16,256]{3,2,1,0:T(8,128)S(1)} %bitcast.41), kind=kLoop, calls=%fused_computation.78 | loop fusion | flops 262144 | bytes 1310720 | tf_op jit(solution)/shard_map/convert_element_type | solution.py:88
  (66 shorter events, 10.2 us)
Async XLA Ops:
  0.0 44.0 %copy-start = (bf16[512,256]{1,0:T(8,128)(2,1)S(1)}, bf16[512,256]{1,0:T(8,128)(2,1)}, u32[]{:S(2)}) copy-start(bf16[512,256]{1,0:T(8,128)(2,1)} %param.6) | copy-start | bytes 786436
  0.0 28.2 %copy-start.3 = (bf16[3,3,3,128,128]{4,3,2,1,0:T(8,128)(2,1)S(1)}, bf16[3,3,3,128,128]{4,3,2,1,0:T(8,128)(2,1)}, u32[]{:S(2)}) copy-start(bf16[3,3,3,128,128]{4,3,2,1,0:T(8,128)(2,1)} %param.5) | copy-start | bytes 2654212
  2.9 18.1 %collective-permute-start = (bf16[8,1,32,128]{3,2,1,0:T(8,128)(2,1)S(1)}, bf16[8,1,32,128]{3,2,1,0:T(8,128)(2,1)S(1)}, u32[]{:S(2)}, u32[]{:S(2)}) collective-permute-start(bf16[8,1,32,128]{3,2,1,0:T(8,128)(2,1)S(1)} %get-tuple-element.57), channel_id=1, source_target_pairs={{0,8},{8,16},{16,24},{24,32},{32,40},{40,48},{48,56},{56,64},{64,7... | collective-permute-start | bytes 196616 | tf_op jit(solution)/shard_map/ppermute | solution.py:14
  6.9 15.7 %collective-permute-start.1 = (bf16[8,1,32,128]{3,2,1,0:T(8,128)(2,1)S(1)}, bf16[8,1,32,128]{3,2,1,0:T(8,128)(2,1)S(1)}, u32[]{:S(2)}, u32[]{:S(2)}) collective-permute-start(bf16[8,1,32,128]{3,2,1,0:T(8,128)(2,1)S(1)} %get-tuple-element.58), channel_id=1, source_target_pairs={{8,0},{16,8},{24,16},{32,24},{40,32},{48,40},{56,48},{64,56},{72,6... | collective-permute-start | bytes 196616 | tf_op jit(solution)/shard_map/ppermute | solution.py:17
  22.7 5.5 %collective-permute-start.2 = (bf16[8,10,1,128]{3,2,1,0:T(2,128)(2,1)S(1)}, bf16[8,10,1,128]{3,2,1,0:T(2,128)(2,1)S(1)}, u32[]{:S(2)}, u32[]{:S(2)}) collective-permute-start(bf16[8,10,1,128]{3,2,1,0:T(2,128)(2,1)S(1)} %get-tuple-element.55), channel_id=1, source_target_pairs={{0,1},{1,2},{2,3},{3,4},{4,5},{5,6},{6,7},{8,9},{9,10},{10,11},{11... | collective-permute-start | bytes 61448 | tf_op jit(solution)/shard_map/ppermute | solution.py:14
  26.2 5.3 %collective-permute-start.3 = (bf16[8,10,1,128]{3,2,1,0:T(2,128)(2,1)S(1)}, bf16[8,10,1,128]{3,2,1,0:T(2,128)(2,1)S(1)}, u32[]{:S(2)}, u32[]{:S(2)}) collective-permute-start(bf16[8,10,1,128]{3,2,1,0:T(2,128)(2,1)S(1)} %get-tuple-element.56), channel_id=1, source_target_pairs={{1,0},{2,1},{3,2},{4,3},{5,4},{6,5},{7,6},{9,8},{10,9},{11,10},{12... | collective-permute-start | bytes 61448 | tf_op jit(solution)/shard_map/ppermute | solution.py:17
  32.8 1.0 %copy-start.1 = (bf16[8,8,32,128]{3,2,1,0:T(8,128)(2,1)S(1)}, bf16[8,8,32,128]{3,2,1,0:T(8,128)(2,1)}, u32[]{:S(2)}) copy-start(bf16[8,8,32,128]{3,2,1,0:T(8,128)(2,1)} %param.4) | copy-start | bytes 1572868
  44.0 20.8 %copy-start.2 = (bf16[3,3,3,256,256]{4,3,2,1,0:T(8,128)(2,1)S(1)}, bf16[3,3,3,256,256]{4,3,2,1,0:T(8,128)(2,1)}, u32[]{:S(2)}) copy-start(bf16[3,3,3,256,256]{4,3,2,1,0:T(8,128)(2,1)} %param.7) | copy-start | bytes 10616836
  44.6 14.2 %collective-permute-start.4 = (bf16[8,1,16,256]{3,2,1,0:T(8,128)(2,1)S(1)}, bf16[8,1,16,256]{3,2,1,0:T(8,128)(2,1)S(1)}, u32[]{:S(2)}, u32[]{:S(2)}) collective-permute-start(bf16[8,1,16,256]{3,2,1,0:T(8,128)(2,1)S(1)} %get-tuple-element.63), channel_id=1, source_target_pairs={{0,8},{8,16},{16,24},{24,32},{32,40},{40,48},{48,56},{56,64},{64,7... | collective-permute-start | bytes 196616 | tf_op jit(solution)/shard_map/ppermute | solution.py:14
  46.7 13.4 %collective-permute-start.5 = (bf16[8,1,16,256]{3,2,1,0:T(8,128)(2,1)S(1)}, bf16[8,1,16,256]{3,2,1,0:T(8,128)(2,1)S(1)}, u32[]{:S(2)}, u32[]{:S(2)}) collective-permute-start(bf16[8,1,16,256]{3,2,1,0:T(8,128)(2,1)S(1)} %get-tuple-element.64), channel_id=1, source_target_pairs={{8,0},{16,8},{24,16},{32,24},{40,32},{48,40},{56,48},{64,56},{72,6... | collective-permute-start | bytes 196616 | tf_op jit(solution)/shard_map/ppermute | solution.py:17
  60.2 4.9 %collective-permute-start.6 = (bf16[8,6,1,256]{3,2,1,0:T(2,128)(2,1)S(1)}, bf16[8,6,1,256]{3,2,1,0:T(2,128)(2,1)S(1)}, u32[]{:S(2)}, u32[]{:S(2)}) collective-permute-start(bf16[8,6,1,256]{3,2,1,0:T(2,128)(2,1)S(1)} %get-tuple-element.61), channel_id=1, source_target_pairs={{0,1},{1,2},{2,3},{3,4},{4,5},{5,6},{6,7},{8,9},{9,10},{10,11},{11... | collective-permute-start | bytes 73736 | tf_op jit(solution)/shard_map/ppermute | solution.py:14
  62.3 5.4 %collective-permute-start.7 = (bf16[8,6,1,256]{3,2,1,0:T(2,128)(2,1)S(1)}, bf16[8,6,1,256]{3,2,1,0:T(2,128)(2,1)S(1)}, u32[]{:S(2)}, u32[]{:S(2)}) collective-permute-start(bf16[8,6,1,256]{3,2,1,0:T(2,128)(2,1)S(1)} %get-tuple-element.62), channel_id=1, source_target_pairs={{1,0},{2,1},{3,2},{4,3},{5,4},{6,5},{7,6},{9,8},{10,9},{11,10},{12... | collective-permute-start | bytes 73736 | tf_op jit(solution)/shard_map/ppermute | solution.py:17
where the time goes:
time: 73.4 us; the launch traced here: 73 us
  starting transfers between devices  41.1 us (56%)
  waiting for transfers between devices  9.85 us (13%)
  local copies, waits for them, and re-layouts  7.36 us (10%)
  other arithmetic  7.1 us (10%)
  matrix products  6.95 us (9%)
    ppermute x4, starting transfers between devices, padded_2(): lax.ppermute(lax.slice_in_dim(block, 0, width, axis=dim), axis, backward)  29.5 us
    ppermute x4, starting transfers between devices, padded_2(): lax.ppermute(lax.slice_in_dim(block, block.shape[dim] - width, None, axis...  11.6 us
    ppermute x4, waiting for transfers between devices, padded_2(): lax.ppermute(lax.slice_in_dim(block, 0, width, axis=dim), axis, backward)  8.78 us
    dot_general x6, matrix products, padded_conv(): jnp.dot(stacked.reshape(-1, 9 * channels), kernel[tap_t].reshape(9 * chan...  6.57 us
    unnamed x34, local copies, waits for them, and re-layouts  5.21 us
    concatenate x4, other arithmetic, padded_2(): block = jnp.concatenate([low, block, high], axis=dim)  1.72 us
    convert_element_type x2, other arithmetic, normed_silu(): return jax.nn.silu(scaled).astype(jnp.bfloat16)  1.61 us
    reduce_sum x1, other arithmetic, normed_silu(): jnp.mean(widened * widened, axis=-1, keepdims=True) + NORM_EPS  1.48 us
  transfers between devices with their start and end apart: 8, of which 5 were waited for; matrix products, arithmetic and copies ran while one was open for 1% of the time, Pallas kernels for 0%

commit v1 on v0

v1 whole, which is shorter than its diff:
```python
import jax
import jax.numpy as jnp
from jax import lax
from jax.experimental import pallas as pl
from jax.experimental.pallas import tpu as pltpu
from jax.sharding import PartitionSpec as P

NORM_EPS = 1e-06
FR, RW, CL, C1, C2 = 8, 8, 32, 128, 256
HALO = 3
BF, F32 = jnp.bfloat16, jnp.float32
PITCH = 48
COLS_OF = (1, 2, 0, 3)
VM = pl.BlockSpec(memory_space=pltpu.VMEM)


def dot(a, b):
    return jnp.dot(a, b, preferred_element_type=F32)


def normed_silu(x, ones):
    mean = dot((x * x).astype(BF), ones)
    half = x * (0.5 * lax.rsqrt(mean + NORM_EPS))
    return half + half * jnp.tanh(half)


def mean_matrix(n):
    return jnp.full((n, n), 1.0 / n, BF)


def build_weights(k1, proj, w, m):
    p0, p1, p2, p3 = (proj[i * C1 : (i + 1) * C1].astype(F32) * 0.5 for i in range(4))
    row = lax.broadcasted_iota(jnp.int32, (C1, C2), 0)
    col = lax.broadcasted_iota(jnp.int32, (C1, C2), 1)
    twice = jnp.where((col == row) | (col == row + C1), 0.5, 0.0).astype(F32)
    m[0:C1] = (p0 + p1 + p2 + p3 + twice).astype(BF)
    m[C1 : 2 * C1] = (p0 + p1 - p2 - p3 + twice).astype(BF)
    m[2 * C1 : 3 * C1] = (p0 - p1 + p2 - p3 + twice).astype(BF)
    m[3 * C1 : 4 * C1] = (p0 - p1 - p2 + p3 + twice).astype(BF)
    zero = jnp.zeros((C1, C1), BF)

    def tap(p, q, s):
        return k1[p, q, s] if 0 <= s < 3 else zero

    for p in range(3):
        for dr in range(4):
            pairs = [pr for pr in range(2) if 0 <= dr - pr < 3]
            left = jnp.concatenate(
                [
                    jnp.concatenate([tap(p, dr - pr, dc - pc) for pr in pairs for pc in range(2)], axis=1)
                    for dc in COLS_OF
                ],
                axis=0,
            )
            w[p, dr] = dot(left, m[pairs[0] * 256 : (pairs[-1] + 1) * 256]).astype(BF)


def lay_out(feature, row_of, ones, wide, plain, a, b, c, f):
    rows = len(row_of)
    span = rows * PITCH
    for t in range(2):
        for r, at in enumerate(row_of):
            base = t * span + r * PITCH
            wide[base + 8 : base + 16] = jnp.zeros((8, C1), F32)
            wide[base + 32 : base + 40] = jnp.zeros((8, C1), F32)
            a[t, at] = jnp.zeros((16, C2), BF)
            b[t, at] = jnp.zeros((16, C2), BF)
    for t in range(FR):
        x = feature(t).astype(F32)
        act = normed_silu(x, ones)
        for r, at in enumerate(row_of):
            base = (t + 2) * span + r * PITCH
            wide[base : base + 8] = jnp.zeros((8, C1), F32)
            wide[base + 40 : base + 48] = jnp.zeros((8, C1), F32)
            wide[base + 8 : base + 40] = act[r * CL : (r + 1) * CL]
            own = (t * rows + r) * CL
            plain[own : own + CL] = x[r * CL : (r + 1) * CL]
            a[t + 2, at, :, 0:C1] = wide[pl.ds(base + 8, 16, stride=2), :].astype(BF)
            a[t + 2, at, :, C1:C2] = wide[pl.ds(base + 9, 16, stride=2), :].astype(BF)
            b[t + 2, at, :, 0:C1] = wide[pl.ds(base + 7, 16, stride=2), :].astype(BF)
            b[t + 2, at, :, C1:C2] = wide[pl.ds(base + 10, 16, stride=2), :].astype(BF)
            f[t, at, :, 0:C1] = plain[pl.ds(own, 16, stride=2), :].astype(BF)
            f[t, at, :, C1:C2] = plain[pl.ds(own + 1, 16, stride=2), :].astype(BF)
    zero = jnp.zeros((FR, C1), F32)
    for p in range(3):
        for r, at in enumerate(row_of):
            base = p * span + r * PITCH + 8
            first = wide[pl.ds(base, FR, stride=span), :]
            last = wide[pl.ds(base + CL - 1, FR, stride=span), :]
            c[p, at, :, 0:C1] = jnp.concatenate([zero, last], axis=0).astype(BF)
            c[p, at, :, C1:C2] = jnp.concatenate([first, zero], axis=0).astype(BF)


def contribute(i, have, slot, w, m, a, b, f):
    total = None
    taps = [dr for dr in range(4) if 2 * i + dr in have]
    for p in range(3):
        left = jnp.concatenate(
            [src[p : p + FR, slot(2 * i + dr)].reshape(FR * 16, C2) for dr in taps for src in (a, b)], axis=1
        )
        right = w[p, taps[0] : taps[-1] + 1].reshape(len(taps) * 512, C2)
        got = dot(left, right)
        total = got if total is None else total + got
    for pr in range(2):
        if 2 * i + 1 + pr in have:
            total = total + dot(f[:, slot(2 * i + 1 + pr)].reshape(FR * 16, C2), m[pr * 256 : (pr + 1) * 256])
    return total


def ring(i_rows, have, slot, w, c):
    total = None
    blank = jnp.zeros((16, C2), BF)
    for dr in range(4):
        if not any(2 * i + dr in have for i in i_rows):
            continue
        for p in range(3):
            left = jnp.concatenate([c[p, slot(2 * i + dr)] if 2 * i + dr in have else blank for i in i_rows], axis=0)
            got = dot(left, w[p, dr, 256:512])
            total = got if total is None else total + got
    return total


def put(acc, i, got, old=None):
    for h in range(2):
        new = got[:, h * 128 : (h + 1) * 128].reshape(FR, 16, 128)
        acc[h, :, i] = new if old is None else old[h, :, i] + new


def own_kernel(feat, k1, proj, w, m, acc, edge, wide, plain, a, b, c, f):
    build_weights(k1, proj, w, m)
    ones = mean_matrix(C1)
    lay_out(lambda t: feat[t].reshape(RW * CL, C1), range(RW), ones, wide, plain, a, b, c, f)
    have = range(HALO, HALO + RW)

    def slot(r):
        return r - HALO

    for i in range(6):
        put(acc, i, contribute(i, have, slot, w, m, a, b, f))
    edge[...] = ring(range(6), have, slot, w, c)


HALO_ROWS = (0, 1, 2, 11, 12, 13)


def halo_kernel(place, from_b, from_a, w, m, acc_in, edge_in, acc, edge, to_b, to_a, joined, wide, plain, a, b, c, f):
    odd = place[0] % 2 == 1
    for t in range(FR):
        fb, fa = from_b[t], from_a[t]
        joined[t, 0:HALO] = jnp.where(odd, fa, fb)
        joined[t, HALO : 2 * HALO] = jnp.where(odd, fb, fa)
    ones = mean_matrix(C1)
    lay_out(lambda t: joined[t].reshape(2 * HALO * CL, C1), range(2 * HALO), ones, wide, plain, a, b, c, f)
    slot = HALO_ROWS.index
    for i in range(6):
        if any(2 * i + dr in HALO_ROWS for dr in range(4)):
            put(acc, i, contribute(i, HALO_ROWS, slot, w, m, a, b, f), acc_in)
        else:
            acc[:, :, i] = acc_in[:, :, i]
    edge[...] = edge_in[...] + ring(range(6), HALO_ROWS, slot, w, c)
    odd = place[1] % 2 == 1
    flat = acc.reshape(2 * FR * 6 * 16, 128)

    def column(i, j):
        return jnp.concatenate(
            [flat[pl.ds(h * 768 + i * 16 + j, FR, stride=96), :] for h in range(2)], axis=1
        )

    for i in range(6):
        right = jnp.concatenate([column(i, 15), edge[i * 16 + 8 : i * 16 + 16]], axis=0)
        left = jnp.concatenate([edge[i * 16 : i * 16 + 8], column(i, 0)], axis=0)
        to_b[i] = jnp.where(odd, right, left).astype(BF)
        to_a[i] = jnp.where(odd, left, right).astype(BF)


def final_kernel(last_row, last_col, place, from_b, pair, acc, edge_in, k2, out, lv, edge, wide, a2):
    odd = place[1] % 2 == 1
    for t in range(FR):
        for h in range(2):
            lv[h, t * 96 : (t + 1) * 96] = acc[h, t].reshape(96, 128)
    for i in range(6):
        fb = from_b[i].astype(F32)
        left = jnp.where(odd, pair[0, i].astype(F32), fb)
        right = jnp.where(odd, fb, pair[1, i].astype(F32))
        edge[i * 16 : i * 16 + 8] = edge_in[i * 16 : i * 16 + 8] + left[0:8]
        edge[i * 16 + 8 : i * 16 + 16] = edge_in[i * 16 + 8 : i * 16 + 16] + right[8:16]
        for h in range(2):
            half = slice(h * 128, (h + 1) * 128)
            lv[h, pl.ds(i * 16, FR, stride=96), :] += left[8:16, half]
            lv[h, pl.ds(i * 16 + 15, FR, stride=96), :] += right[0:8, half]
    def level(at, count):
        return jnp.concatenate([lv[0, at : at + count], lv[1, at : at + count]], axis=1)

    ones = mean_matrix(C2)
    keep = [jnp.float32(1.0)] * 6
    keep[0] = jnp.where(place[0] == 0, 0.0, 1.0)
    keep[5] = jnp.where(place[0] == last_row, 0.0, 1.0)
    keep_left = jnp.where(place[1] == 0, 0.0, 1.0)
    keep_right = jnp.where(place[1] == last_col, 0.0, 1.0)
    for t in range(FR):
        act = normed_silu(level(t * 96, 96), ones)
        for i in range(6):
            base = (t * 6 + i) * 32 + 8
            kept = act[i * 16 : (i + 1) * 16] * keep[i]
            for h in range(2):
                wide[h, base : base + 16] = kept[:, h * 128 : (h + 1) * 128]
    act = normed_silu(edge[...], ones)
    for i in range(6):
        for h in range(2):
            half = slice(h * 128, (h + 1) * 128)
            wide[h, pl.ds(i * 32 + 7, FR, stride=192), :] = act[i * 16 : i * 16 + 8, half] * (keep[i] * keep_left)
            wide[h, pl.ds(i * 32 + 24, FR, stride=192), :] = act[i * 16 + 8 : i * 16 + 16, half] * (
                keep[i] * keep_right
            )
    for s in range(3):
        for i in range(6):
            for t in range(2):
                a2[s, t, i] = jnp.zeros((16, C2), BF)
            for t in range(FR):
                base = (t * 6 + i) * 32 + 7 + s
                for h in range(2):
                    a2[s, t + 2, i, :, h * 128 : (h + 1) * 128] = wide[h, base : base + 16].astype(BF)
    for i in range(4):
        total = None
        for p in range(3):
            left = jnp.concatenate(
                [a2[s, p : p + FR, i + q].reshape(FR * 16, C2) for q in range(3) for s in range(3)], axis=1
            )
            got = dot(left, k2[p].reshape(9 * C2, C2))
            total = got if total is None else total + got
        for t in range(FR):
            at = (t * 6 + i + 1) * 16
            out[t, i] = (level(at, 16) + total[t * 16 : (t + 1) * 16]).astype(BF)


def in_vmem(shape, dtype):
    return jax.ShapeDtypeStruct(shape, dtype)


def operands(rows):
    return [
        pltpu.VMEM(((FR + 2) * rows * PITCH, C1), F32),
        pltpu.VMEM((FR * rows * CL, C1), F32),
        pltpu.VMEM((FR + 2, rows, 16, C2), BF),
        pltpu.VMEM((FR + 2, rows, 16, C2), BF),
        pltpu.VMEM((3, rows, 16, C2), BF),
        pltpu.VMEM((FR, rows, 16, C2), BF),
    ]


W_SHAPE = in_vmem((3, 4, 512, C2), BF)
M_SHAPE = in_vmem((512, C2), BF)
ACC_SHAPE = in_vmem((2, FR, 6, 16, 128), F32)
EDGE_SHAPE = in_vmem((96, C2), F32)
STRIP_SHAPE = in_vmem((6, 16, C2), BF)
SMEM = pl.BlockSpec(memory_space=pltpu.SMEM)
PARAMS = pltpu.CompilerParams(vmem_limit_bytes=40 * 2**20)


def own_part(feat, k1, proj):
    return pl.pallas_call(
        own_kernel,
        out_shape=(W_SHAPE, M_SHAPE, ACC_SHAPE, EDGE_SHAPE),
        in_specs=[VM] * 3,
        out_specs=(VM,) * 4,
        scratch_shapes=operands(RW),
        compiler_params=PARAMS,
        name="own_part",
    )(feat, k1, proj)


def halo_part(place, from_b, from_a, w, m, acc, edge):
    return pl.pallas_call(
        halo_kernel,
        out_shape=(ACC_SHAPE, EDGE_SHAPE, STRIP_SHAPE, STRIP_SHAPE),
        in_specs=[SMEM] + [VM] * 6,
        out_specs=(VM,) * 4,
        scratch_shapes=[pltpu.VMEM((FR, 2 * HALO, CL, C1), BF)] + operands(2 * HALO),
        compiler_params=PARAMS,
        name="halo_part",
    )(place, from_b, from_a, w, m, acc, edge)


def final_part(last_row, last_col, place, from_b, pair, acc, edge, k2):
    def kernel(*refs):
        final_kernel(last_row, last_col, *refs)

    return pl.pallas_call(
        kernel,
        out_shape=in_vmem((FR, 4, 16, C2), BF),
        in_specs=[SMEM] + [VM] * 5,
        out_specs=VM,
        scratch_shapes=[
            pltpu.VMEM((2, FR * 6 * 16, 128), F32),
            pltpu.VMEM((96, C2), F32),
            pltpu.VMEM((2, FR * 6 * 32, 128), F32),
            pltpu.VMEM((3, FR + 2, 6, 16, C2), BF),
        ],
        compiler_params=PARAMS,
        name="final_part",
    )(place, from_b, pair, acc, edge, k2)


def pairs(first, count):
    swaps = []
    for i in range(first, count - 1, 2):
        swaps += [(i, i + 1), (i + 1, i)]
    return swaps


def local(features, kernel_one, projection, kernel_two):
    rows, cols = lax.axis_size("row"), lax.axis_size("col")
    row, col = lax.axis_index("row"), lax.axis_index("col")
    place = jnp.stack([row, col]).astype(jnp.int32)
    last = RW - HALO
    odd = row % 2
    send_b = lax.dynamic_slice_in_dim(features, odd * last, HALO, axis=1)
    send_a = lax.dynamic_slice_in_dim(features, (1 - odd) * last, HALO, axis=1)
    from_b = lax.ppermute(send_b, "row", pairs(1, rows))
    from_a = lax.ppermute(send_a, "row", pairs(0, rows))
    w, m, acc, edge = own_part(features, kernel_one, projection)
    acc, edge, to_b, to_a = halo_part(place, from_b, from_a, w, m, acc, edge)
    from_b = lax.ppermute(to_b, "col", pairs(1, cols))
    pair = lax.all_gather(to_a, "col", axis_index_groups=[[i, i + 1] for i in range(0, cols, 2)])
    return final_part(rows - 1, cols - 1, place, from_b, pair, acc, edge, kernel_two)


def solution(mesh):
    return jax.shard_map(
        local,
        mesh=mesh,
        in_specs=(P(None, "row", "col", None), P(), P(), P()),
        out_specs=P(None, "row", "col", None),
        check_vma=False,
    )
```

time: 73.4 us -> 40.7 us (0.55)
  starting transfers between devices: 41.1 us -> 21.5 us
  Pallas kernels: 0 us -> 10.6 us
  waiting for transfers between devices: 9.85 us -> 1.17 us
  other arithmetic: 7.1 us -> 0.08 us
  matrix products: 6.95 us -> 0 us
  local copies, waits for them, and re-layouts: 7.36 us -> 5.09 us
  blocking collectives: 0 us -> 1.88 us
    ppermute x8 -> x3, starting transfers between devices: 41.1 us -> 21.5 us  [the longest x1 14.4 us: local(): from_b = lax.ppermute(send_b, 'row', pairs(1, rows))]
    pallas_call x0 -> x3, Pallas kernels: none -> 10.6 us  [the longest x1 4.15 us: own_part(): pl.pallas_call(own_kernel, out_shape=(W_SHAPE, M_SHAPE, ACC_SHAPE, EDGE_S...]
    ppermute x8 -> x3, waiting for transfers between devices: 9.85 us -> 1.17 us  [the longest x1 0.82 us: local(): from_b = lax.ppermute(send_b, 'row', pairs(1, rows))]
    dot_general x7 -> x0, matrix products: 6.95 us -> none  [the longest x6 6.57 us: padded_conv(): jnp.dot(stacked.reshape(-1, 9 * channels), kernel[tap_t].reshape(9 * chan...]
    convert_element_type x4 -> x0, other arithmetic: 2.56 us -> none  [the longest x2 1.61 us: normed_silu(): return jax.nn.silu(scaled).astype(jnp.bfloat16)]
    unnamed x34 -> x8, local copies, waits for them, and re-layouts: 5.21 us -> 3.16 us
    dynamic_slice x0 -> x1, local copies, waits for them, and re-layouts: none -> 1.93 us  [local(): send_a = lax.dynamic_slice_in_dim(features, (1 - odd) * last, HALO, axis=1)]
    all_gather x0 -> x1, blocking collectives: none -> 1.88 us  [local(): lax.all_gather(to_a, 'col', axis_index_groups=[[i, i + 1] for i in range(...]
  transfers between devices with their start and end apart: 8 -> 3, of which waited for: 5 -> 2; matrix products, arithmetic and copies ran while one was open for 1% -> 0% of each run, Pallas kernels for 0% -> 10%
where the time goes in v1:
time: 40.7 us; the launch traced here: 40.4 us
  starting transfers between devices  21.5 us (53%)
  Pallas kernels  10.6 us (26%)
  local copies, waits for them, and re-layouts  5.09 us (13%)
  blocking collectives  1.88 us (5%)
  waiting for transfers between devices  1.17 us (3%)
    ppermute x1, starting transfers between devices, local(): from_b = lax.ppermute(send_b, 'row', pairs(1, rows))  14.4 us
    pallas_call x1, Pallas kernels, own_part(): pl.pallas_call(own_kernel, out_shape=(W_SHAPE, M_SHAPE, ACC_SHAPE, EDGE_S...  4.15 us
    ppermute x1, starting transfers between devices, local(): from_a = lax.ppermute(send_a, 'row', pairs(0, rows))  3.99 us
    pallas_call x1, Pallas kernels, final_part(): pl.pallas_call(kernel, out_shape=in_vmem((FR, 4, 16, C2), BF), in_specs=[...  3.8 us
    ppermute x1, starting transfers between devices, local(): from_b = lax.ppermute(to_b, 'col', pairs(1, cols))  3.18 us
    unnamed x8, local copies, waits for them, and re-layouts  3.16 us
    pallas_call x1, Pallas kernels, halo_part(): pl.pallas_call(halo_kernel, out_shape=(ACC_SHAPE, EDGE_SHAPE, STRIP_SHAPE...  2.68 us
    dynamic_slice x1, local copies, waits for them, and re-layouts, local(): send_a = lax.dynamic_slice_in_dim(features, (1 - odd) * last, HALO, axis=1)  1.93 us
  transfers between devices with their start and end apart: 3, of which 2 were waited for; matrix products, arithmetic and copies ran while one was open for 0% of the time, Pallas kernels for 10%

profile of v1, /device:TPU:7, one launch (start us, length us, event | category | flops | bytes accessed | tf_op | source)
XLA Modules:
  0.0 40.4 jit_solution(14638745373590224786)
XLA Ops:
  0.0 0.0 copy-start
  0.0 1.9 %constant_dynamic-slice_fusion = (bf16[8,3,32,128]{3,2,1,0:T(8,128)(2,1)}, bf16[8,3,32,128]{3,2,1,0:T(8,128)(2,1)}) fusion(bf16[8,8,32,128]{3,2,1,0:T(8,128)(2,1)} %feat.1, s32[]{:T(128)S(6)} %select_n.15, s32[]{:T(128)S(6)} %select_n.14), kind=kLoop, calls=%fused_computation.1 | loop fusion | bytes 786440 | tf_op jit(solution)/shard_map/dynamic_slice | solution.py:318
  1.9 4.0 %collective-permute-start.1 = (bf16[8,3,32,128]{3,2,1,0:T(8,128)(2,1)}, bf16[8,3,32,128]{3,2,1,0:T(8,128)(2,1)}, u32[]{:S(2)}, u32[]{:S(2)}) collective-permute-start(bf16[8,3,32,128]{3,2,1,0:T(8,128)(2,1)} %get-tuple-element.21), channel_id=1, source_target_pairs={{0,8},{8,0},{16,24},{24,16},{32,40},{40,32},{48,56},{56,48},{64,72... | collective-permute-start | bytes 589832 | tf_op jit(solution)/shard_map/ppermute | solution.py:320
  5.9 14.4 %collective-permute-start = (bf16[8,3,32,128]{3,2,1,0:T(8,128)(2,1)}, bf16[8,3,32,128]{3,2,1,0:T(8,128)(2,1)}, u32[]{:S(2)}, u32[]{:S(2)}) collective-permute-start(bf16[8,3,32,128]{3,2,1,0:T(8,128)(2,1)} %get-tuple-element.22), channel_id=1, source_target_pairs={{8,16},{16,8},{24,32},{32,24},{40,48},{48,40},{56,64},{64,56},{72,... | collective-permute-start | bytes 589832 | tf_op jit(solution)/shard_map/ppermute | solution.py:319
  20.3 0.0 copy-start.1
  20.3 1.0 %copy-done.1 = bf16[8,8,32,128]{3,2,1,0:T(8,128)(2,1)S(1)} copy-done((bf16[8,8,32,128]{3,2,1,0:T(8,128)(2,1)S(1)}, bf16[8,8,32,128]{3,2,1,0:T(8,128)(2,1)}, u32[]{:S(2)}) %copy-start.1) | copy-done | bytes 524312
  21.4 0.0 copy-start.2
  21.4 1.2 %copy-done.2 = bf16[3,3,3,128,128]{4,3,2,1,0:T(8,128)(2,1)S(1)} copy-done((bf16[3,3,3,128,128]{4,3,2,1,0:T(8,128)(2,1)S(1)}, bf16[3,3,3,128,128]{4,3,2,1,0:T(8,128)(2,1)}, u32[]{:S(2)}) %copy-start.2) | copy-done | bytes 884760
  22.5 0.0 copy-start.3
  22.5 0.9 %copy-done.3 = bf16[512,256]{1,0:T(8,128)(2,1)S(1)} copy-done((bf16[512,256]{1,0:T(8,128)(2,1)S(1)}, bf16[512,256]{1,0:T(8,128)(2,1)}, u32[]{:S(2)}) %copy-start.3) | copy-done | bytes 262168
  23.5 4.2 %own_part.1 = (bf16[3,4,512,256]{3,2,1,0:T(8,128)(2,1)S(1)}, bf16[512,256]{1,0:T(8,128)(2,1)S(1)}, f32[2,8,6,16,128]{4,3,2,1,0:T(8,128)S(1)}, f32[96,256]{1,0:T(8,128)S(1)}) custom-call(bf16[8,8,32,128]{3,2,1,0:T(8,128)(2,1)S(1)} %copy-done.1, bf16[3,3,3,128,128]{4,3,2,1,0:T(8,128)(2,1)S(1)} %copy-done.2, bf16[512,256]{1,0:T(8,128)(2,1)S(1)} %copy-done.3), custom_call_target="tpu_custom_call" | custom-call | tf_op jit(solution)/shard_map/own_part/pallas_call | solution.py:261
  27.6 0.1 pad_add_fusion.place.refs_0_
  27.7 0.0 collective-permute-done.1.from_a
  27.7 0.8 %collective-permute-done.from_b = bf16[8,3,32,128]{3,2,1,0:T(8,128)(2,1)} collective-permute-done((bf16[8,3,32,128]{3,2,1,0:T(8,128)(2,1)}, bf16[8,3,32,128]{3,2,1,0:T(8,128)(2,1)}, u32[]{:S(2)}, u32[]{:S(2)}) %collective-permute-start) | collective-permute-done | bytes 196640 | tf_op jit(solution)/shard_map/ppermute | solution.py:319
  28.5 2.7 %halo_part.1 = (f32[2,8,6,16,128]{4,3,2,1,0:T(8,128)S(1)}, f32[96,256]{1,0:T(8,128)S(1)}, bf16[6,16,256]{2,1,0:T(8,128)(2,1)S(1)}, bf16[6,16,256]{2,1,0:T(8,128)(2,1)S(1)}) custom-call(s32[2]{0:T(128)S(1)} %pad_add_fusion.place.refs_0_, bf16[8,3,32,128]{3,2,1,0:T(8,128)(2,1)} %collective-permute-done.from_b, ...), custom_call_target="tpu_custom_call" | custom-call | tf_op jit(solution)/shard_map/halo_part/pallas_call | solution.py:273
  31.2 3.2 %collective-permute-start.2 = (bf16[6,16,256]{2,1,0:T(8,128)(2,1)S(1)}, bf16[6,16,256]{2,1,0:T(8,128)(2,1)S(1)}, u32[]{:S(2)}, u32[]{:S(2)}) collective-permute-start(bf16[6,16,256]{2,1,0:T(8,128)(2,1)S(1)} %get-tuple-element.17), channel_id=1, source_target_pairs={{1,2},{2,1},{3,4},{4,3},{5,6},{6,5},{9,10},{10,9},{11,12},{12,11},... | collective-permute-start | bytes 147464 | tf_op jit(solution)/shard_map/ppermute | solution.py:323
  34.4 1.9 %all-gather = bf16[12,16,256]{2,1,0:T(8,128)(2,1)S(1)} all-gather(bf16[6,16,256]{2,1,0:T(8,128)(2,1)S(1)} %get-tuple-element.18), channel_id=2, replica_groups={{0,1},{2,3},{4,5},{6,7},{8,9},{10,11},{12,13},{14,15},{16,17},{18,19},{..., dimensions={0}, use_global_device_ids=true | all-gather | bytes 147456 | tf_op jit(solution)/shard_map/all_gather | solution.py:324
  36.3 0.3 collective-permute-done.2.refs_1_
  36.6 0.0 copy-done
  36.6 3.8 %final_part.1 = bf16[8,4,16,256]{3,2,1,0:T(8,128)(2,1)} custom-call(s32[2]{0:T(128)S(1)} %pad_add_fusion.place.refs_0_, bf16[6,16,256]{2,1,0:T(8,128)(2,1)S(1)} %collective-permute-done.2.refs_1_, bf16[2,6,16,256]{3,2,1,0:T(8,128)(2,1)S(1)} %bitcast.3, f32[2,8,6,16,128]{4,3,2,1,0:T(8,128)S(1)} %get-tuple-element.19.refs_3_, ...), custom_call_target="tpu_custom_call" | custom-call | tf_op jit(solution)/shard_map/final_part/pallas_call | solution.py:288
Async XLA Ops:
  0.0 36.6 %copy-start = (bf16[3,3,3,256,256]{4,3,2,1,0:T(8,128)(2,1)S(1)}, bf16[3,3,3,256,256]{4,3,2,1,0:T(8,128)(2,1)}, u32[]{:S(2)}) copy-start(bf16[3,3,3,256,256]{4,3,2,1,0:T(8,128)(2,1)} %refs_5_.1) | copy-start | bytes 10616836
  1.9 25.8 %collective-permute-start.1 = (bf16[8,3,32,128]{3,2,1,0:T(8,128)(2,1)}, bf16[8,3,32,128]{3,2,1,0:T(8,128)(2,1)}, u32[]{:S(2)}, u32[]{:S(2)}) collective-permute-start(bf16[8,3,32,128]{3,2,1,0:T(8,128)(2,1)} %get-tuple-element.21), channel_id=1, source_target_pairs={{0,8},{8,0},{16,24},{24,16},{32,40},{40,32},{48,56},{56,48},{64,72... | collective-permute-start | bytes 589832 | tf_op jit(solution)/shard_map/ppermute | solution.py:320
  5.9 22.6 %collective-permute-start = (bf16[8,3,32,128]{3,2,1,0:T(8,128)(2,1)}, bf16[8,3,32,128]{3,2,1,0:T(8,128)(2,1)}, u32[]{:S(2)}, u32[]{:S(2)}) collective-permute-start(bf16[8,3,32,128]{3,2,1,0:T(8,128)(2,1)} %get-tuple-element.22), channel_id=1, source_target_pairs={{8,16},{16,8},{24,32},{32,24},{40,48},{48,40},{56,64},{64,56},{72,... | collective-permute-start | bytes 589832 | tf_op jit(solution)/shard_map/ppermute | solution.py:319
  20.3 1.0 %copy-start.1 = (bf16[8,8,32,128]{3,2,1,0:T(8,128)(2,1)S(1)}, bf16[8,8,32,128]{3,2,1,0:T(8,128)(2,1)}, u32[]{:S(2)}) copy-start(bf16[8,8,32,128]{3,2,1,0:T(8,128)(2,1)} %feat.1) | copy-start | bytes 1572868
  21.4 1.2 %copy-start.2 = (bf16[3,3,3,128,128]{4,3,2,1,0:T(8,128)(2,1)S(1)}, bf16[3,3,3,128,128]{4,3,2,1,0:T(8,128)(2,1)}, u32[]{:S(2)}) copy-start(bf16[3,3,3,128,128]{4,3,2,1,0:T(8,128)(2,1)} %k1.1) | copy-start | bytes 2654212
  22.5 0.9 %copy-start.3 = (bf16[512,256]{1,0:T(8,128)(2,1)S(1)}, bf16[512,256]{1,0:T(8,128)(2,1)}, u32[]{:S(2)}) copy-start(bf16[512,256]{1,0:T(8,128)(2,1)} %proj.1) | copy-start | bytes 786436
  31.2 5.4 %collective-permute-start.2 = (bf16[6,16,256]{2,1,0:T(8,128)(2,1)S(1)}, bf16[6,16,256]{2,1,0:T(8,128)(2,1)S(1)}, u32[]{:S(2)}, u32[]{:S(2)}) collective-permute-start(bf16[6,16,256]{2,1,0:T(8,128)(2,1)S(1)} %get-tuple-element.17), channel_id=1, source_target_pairs={{1,2},{2,1},{3,4},{4,3},{5,6},{6,5},{9,10},{10,9},{11,12},{12,11},... | collective-permute-start | bytes 147464 | tf_op jit(solution)/shard_map/ppermute | solution.py:323

commit v2 on v1

--- a/solution.py
+++ b/solution.py
@@ -257,6 +257,36 @@
 PARAMS = pltpu.CompilerParams(vmem_limit_bytes=40 * 2**20)
 
 
+def stage_kernel(place, feat, k1, proj, send_b, send_a, feat_in, k1_in, proj_in, sems):
+    odd = place[0] % 2
+    last = RW - HALO
+    moves = [
+        (feat.at[:, pl.ds(odd * last, HALO)], send_b),
+        (feat.at[:, pl.ds((1 - odd) * last, HALO)], send_a),
+        (k1, k1_in),
+        (proj, proj_in),
+        (feat, feat_in),
+    ]
+    copies = [pltpu.make_async_copy(src, dst, sems.at[n]) for n, (src, dst) in enumerate(moves)]
+    for copy in copies:
+        copy.start()
+    for copy in copies:
+        copy.wait()
+
+
+def stage(place, feat, k1, proj):
+    strip = in_vmem((FR, HALO, CL, C1), BF)
+    return pl.pallas_call(
+        stage_kernel,
+        out_shape=(strip, strip) + tuple(in_vmem(x.shape, x.dtype) for x in (feat, k1, proj)),
+        in_specs=[SMEM] + [pl.BlockSpec(memory_space=pltpu.HBM)] * 3,
+        out_specs=(VM,) * 5,
+        scratch_shapes=[pltpu.SemaphoreType.DMA((5,))],
+        compiler_params=PARAMS,
+        name="stage",
+    )(place, *(pltpu.with_memory_space_constraint(x, pltpu.HBM) for x in (feat, k1, proj)))
+
+
 def own_part(feat, k1, proj):
     return pl.pallas_call(
         own_kernel,
@@ -312,10 +342,7 @@
     rows, cols = lax.axis_size("row"), lax.axis_size("col")
     row, col = lax.axis_index("row"), lax.axis_index("col")
     place = jnp.stack([row, col]).astype(jnp.int32)
-    last = RW - HALO
-    odd = row % 2
-    send_b = lax.dynamic_slice_in_dim(features, odd * last, HALO, axis=1)
-    send_a = lax.dynamic_slice_in_dim(features, (1 - odd) * last, HALO, axis=1)
+    send_b, send_a, features, kernel_one, projection = stage(place, features, kernel_one, projection)
     from_b = lax.ppermute(send_b, "row", pairs(1, rows))
     from_a = lax.ppermute(send_a, "row", pairs(0, rows))
     w, m, acc, edge = own_part(features, kernel_one, projection)

time: 40.7 us -> 38.2 us (0.939)
  local copies, waits for them, and re-layouts: 5.09 us -> 0.01 us
  Pallas kernels: 10.6 us -> 12.4 us
  starting transfers between devices: 21.5 us -> 22.4 us
    unnamed x8 -> x2, local copies, waits for them, and re-layouts: 3.16 us -> 0.01 us
    pallas_call x0 -> x1, Pallas kernels: none -> 2.18 us  [stage(): pl.pallas_call(stage_kernel, out_shape=(strip, strip) + tuple((in_vmem(x....]
    ppermute x1, starting transfers between devices: 14.4 us -> 16.5 us  [local(): from_b = lax.ppermute(send_b, 'row', pairs(1, rows))]
    ppermute x1, starting transfers between devices: 3.99 us -> 1.92 us  [local(): from_a = lax.ppermute(send_a, 'row', pairs(0, rows))]
    dynamic_slice x1 -> x0, local copies, waits for them, and re-layouts: 1.93 us -> none  [local(): send_a = lax.dynamic_slice_in_dim(features, (1 - odd) * last, HALO, axis=1)]
    ppermute x1, waiting for transfers between devices: 0.01 us -> 1.22 us  [local(): from_a = lax.ppermute(send_a, 'row', pairs(0, rows))]
    ppermute x1, starting transfers between devices: 3.18 us -> 4.05 us  [local(): from_b = lax.ppermute(to_b, 'col', pairs(1, cols))]
    ppermute x1, waiting for transfers between devices: 0.82 us -> 0.01 us  [local(): from_b = lax.ppermute(send_b, 'row', pairs(1, rows))]
  transfers between devices with their start and end apart: 3 -> 3, of which waited for: 2 -> 1; matrix products, arithmetic and copies ran while one was open for 0% -> 0% of each run, Pallas kernels for 10% -> 11%
where the time goes in v2:
time: 38.2 us; the launch traced here: 38.1 us
  starting transfers between devices  22.4 us (59%)
  Pallas kernels  12.4 us (32%)
  blocking collectives  1.88 us (5%)
  waiting for transfers between devices  1.23 us (3%)
    ppermute x1, starting transfers between devices, local(): from_b = lax.ppermute(send_b, 'row', pairs(1, rows))  16.5 us
    pallas_call x1, Pallas kernels, own_part(): pl.pallas_call(own_kernel, out_shape=(W_SHAPE, M_SHAPE, ACC_SHAPE, EDGE_S...  4.18 us
    ppermute x1, starting transfers between devices, local(): from_b = lax.ppermute(to_b, 'col', pairs(1, cols))  4.05 us
    pallas_call x1, Pallas kernels, final_part(): pl.pallas_call(kernel, out_shape=in_vmem((FR, 4, 16, C2), BF), in_specs=[...  3.82 us
    pallas_call x1, Pallas kernels, halo_part(): pl.pallas_call(halo_kernel, out_shape=(ACC_SHAPE, EDGE_SHAPE, STRIP_SHAPE...  2.21 us
    pallas_call x1, Pallas kernels, stage(): pl.pallas_call(stage_kernel, out_shape=(strip, strip) + tuple((in_vmem(x....  2.18 us
    ppermute x1, starting transfers between devices, local(): from_a = lax.ppermute(send_a, 'row', pairs(0, rows))  1.92 us
    all_gather x1, blocking collectives, local(): lax.all_gather(to_a, 'col', axis_index_groups=[[i, i + 1] for i in range(...  1.88 us
  transfers between devices with their start and end apart: 3, of which 1 were waited for; matrix products, arithmetic and copies ran while one was open for 0% of the time, Pallas kernels for 11%

profile of v2, /device:TPU:7, one launch (start us, length us, event | category | flops | bytes accessed | tf_op | source)
XLA Modules:
  0.0 38.1 jit_solution(16963051563680926185)
XLA Ops:
  0.0 0.1 pad_add_fusion.place.refs_0_
  0.1 2.2 %stage.1 = (bf16[8,3,32,128]{3,2,1,0:T(8,128)(2,1)S(1)}, bf16[8,3,32,128]{3,2,1,0:T(8,128)(2,1)S(1)}, bf16[8,8,32,128]{3,2,1,0:T(8,128)(2,1)S(1)}, bf16[3,3,3,12...) custom-call(s32[2]{0:T(128)S(1)} %pad_add_fusion.place.refs_0_, bf16[8,8,32,128]{3,2,1,0:T(8,128)(2,1)} %feat.1, ...), custom_call_target="tpu_custom_call" | custom-call | tf_op jit(solution)/shard_map/stage/pallas_call | solution.py:279
  2.3 0.0 copy-start
  2.3 16.5 %collective-permute-start = (bf16[8,3,32,128]{3,2,1,0:T(8,128)(2,1)S(1)}, bf16[8,3,32,128]{3,2,1,0:T(8,128)(2,1)S(1)}, u32[]{:S(2)}, u32[]{:S(2)}) collective-permute-start(bf16[8,3,32,128]{3,2,1,0:T(8,128)(2,1)S(1)} %get-tuple-element.18), channel_id=1, source_target_pairs={{8,16},{16,8},{24,32},{32,24},{40,48},{48,40},{56,64},{64,56},{72,... | collective-permute-start | bytes 589832 | tf_op jit(solution)/shard_map/ppermute | solution.py:346
  18.7 1.9 %collective-permute-start.1 = (bf16[8,3,32,128]{3,2,1,0:T(8,128)(2,1)S(1)}, bf16[8,3,32,128]{3,2,1,0:T(8,128)(2,1)S(1)}, u32[]{:S(2)}, u32[]{:S(2)}) collective-permute-start(bf16[8,3,32,128]{3,2,1,0:T(8,128)(2,1)S(1)} %get-tuple-element.19), channel_id=1, source_target_pairs={{0,8},{8,0},{16,24},{24,16},{32,40},{40,32},{48,56},{56,48},{64,72... | collective-permute-start | bytes 589832 | tf_op jit(solution)/shard_map/ppermute | solution.py:347
  20.7 4.2 %own_part.1 = (bf16[3,4,512,256]{3,2,1,0:T(8,128)(2,1)S(1)}, bf16[512,256]{1,0:T(8,128)(2,1)S(1)}, f32[2,8,6,16,128]{4,3,2,1,0:T(8,128)S(1)}, f32[96,256]{1,0:T(8,128)S(1)}) custom-call(bf16[8,8,32,128]{3,2,1,0:T(8,128)(2,1)S(1)} %get-tuple-element.20.feat, bf16[3,3,3,128,128]{4,3,2,1,0:T(8,128)(2,1)S(1)} %get-tuple-element.21.k1, ...), custom_call_target="tpu_custom_call" | custom-call | tf_op jit(solution)/shard_map/own_part/pallas_call | solution.py:291
  24.9 0.0 collective-permute-done.from_b
  24.9 1.2 %collective-permute-done.1.from_a = bf16[8,3,32,128]{3,2,1,0:T(8,128)(2,1)S(1)} collective-permute-done((bf16[8,3,32,128]{3,2,1,0:T(8,128)(2,1)S(1)}, bf16[8,3,32,128]{3,2,1,0:T(8,128)(2,1)S(1)}, u32[]{:S(2)}, u32[]{:S(2)}) %collective-permute-start.1) | collective-permute-done | bytes 196640 | tf_op jit(solution)/shard_map/ppermute | solution.py:347
  26.1 2.2 %halo_part.1 = (f32[2,8,6,16,128]{4,3,2,1,0:T(8,128)S(1)}, f32[96,256]{1,0:T(8,128)S(1)}, bf16[6,16,256]{2,1,0:T(8,128)(2,1)S(1)}, bf16[6,16,256]{2,1,0:T(8,128)(2,1)S(1)}) custom-call(s32[2]{0:T(128)S(1)} %pad_add_fusion.place.refs_0_, bf16[8,3,32,128]{3,2,1,0:T(8,128)(2,1)S(1)} %collective-permute-done.from_b, ...), custom_call_target="tpu_custom_call" | custom-call | tf_op jit(solution)/shard_map/halo_part/pallas_call | solution.py:303
  28.3 4.1 %collective-permute-start.2 = (bf16[6,16,256]{2,1,0:T(8,128)(2,1)S(1)}, bf16[6,16,256]{2,1,0:T(8,128)(2,1)S(1)}, u32[]{:S(2)}, u32[]{:S(2)}) collective-permute-start(bf16[6,16,256]{2,1,0:T(8,128)(2,1)S(1)} %get-tuple-element.27), channel_id=1, source_target_pairs={{1,2},{2,1},{3,4},{4,3},{5,6},{6,5},{9,10},{10,9},{11,12},{12,11},... | collective-permute-start | bytes 147464 | tf_op jit(solution)/shard_map/ppermute | solution.py:350
  32.4 1.9 %all-gather = bf16[12,16,256]{2,1,0:T(8,128)(2,1)S(1)} all-gather(bf16[6,16,256]{2,1,0:T(8,128)(2,1)S(1)} %get-tuple-element.28), channel_id=2, replica_groups={{0,1},{2,3},{4,5},{6,7},{8,9},{10,11},{12,13},{14,15},{16,17},{18,19},{..., dimensions={0}, use_global_device_ids=true | all-gather | bytes 147456 | tf_op jit(solution)/shard_map/all_gather | solution.py:351
  34.2 0.0 collective-permute-done.2.refs_1_
  34.2 0.0 copy-done
  34.2 3.8 %final_part.1 = bf16[8,4,16,256]{3,2,1,0:T(8,128)(2,1)} custom-call(s32[2]{0:T(128)S(1)} %pad_add_fusion.place.refs_0_, bf16[6,16,256]{2,1,0:T(8,128)(2,1)S(1)} %collective-permute-done.2.refs_1_, bf16[2,6,16,256]{3,2,1,0:T(8,128)(2,1)S(1)} %bitcast.3, f32[2,8,6,16,128]{4,3,2,1,0:T(8,128)S(1)} %get-tuple-element.29.refs_3_, ...), custom_call_target="tpu_custom_call" | custom-call | tf_op jit(solution)/shard_map/final_part/pallas_call | solution.py:318
Async XLA Ops:
  2.3 32.0 %copy-start = (bf16[3,3,3,256,256]{4,3,2,1,0:T(8,128)(2,1)S(1)}, bf16[3,3,3,256,256]{4,3,2,1,0:T(8,128)(2,1)}, u32[]{:S(2)}) copy-start(bf16[3,3,3,256,256]{4,3,2,1,0:T(8,128)(2,1)} %refs_5_.1) | copy-start | bytes 10616836
  2.3 22.6 %collective-permute-start = (bf16[8,3,32,128]{3,2,1,0:T(8,128)(2,1)S(1)}, bf16[8,3,32,128]{3,2,1,0:T(8,128)(2,1)S(1)}, u32[]{:S(2)}, u32[]{:S(2)}) collective-permute-start(bf16[8,3,32,128]{3,2,1,0:T(8,128)(2,1)S(1)} %get-tuple-element.18), channel_id=1, source_target_pairs={{8,16},{16,8},{24,32},{32,24},{40,48},{48,40},{56,64},{64,56},{72,... | collective-permute-start | bytes 589832 | tf_op jit(solution)/shard_map/ppermute | solution.py:346
  18.7 7.3 %collective-permute-start.1 = (bf16[8,3,32,128]{3,2,1,0:T(8,128)(2,1)S(1)}, bf16[8,3,32,128]{3,2,1,0:T(8,128)(2,1)S(1)}, u32[]{:S(2)}, u32[]{:S(2)}) collective-permute-start(bf16[8,3,32,128]{3,2,1,0:T(8,128)(2,1)S(1)} %get-tuple-element.19), channel_id=1, source_target_pairs={{0,8},{8,0},{16,24},{24,16},{32,40},{40,32},{48,56},{56,48},{64,72... | collective-permute-start | bytes 589832 | tf_op jit(solution)/shard_map/ppermute | solution.py:347
  28.3 5.9 %collective-permute-start.2 = (bf16[6,16,256]{2,1,0:T(8,128)(2,1)S(1)}, bf16[6,16,256]{2,1,0:T(8,128)(2,1)S(1)}, u32[]{:S(2)}, u32[]{:S(2)}) collective-permute-start(bf16[6,16,256]{2,1,0:T(8,128)(2,1)S(1)} %get-tuple-element.27), channel_id=1, source_target_pairs={{1,2},{2,1},{3,4},{4,3},{5,6},{6,5},{9,10},{10,9},{11,12},{12,11},... | collective-permute-start | bytes 147464 | tf_op jit(solution)/shard_map/ppermute | solution.py:350

commit v3 on v1

--- a/solution.py
+++ b/solution.py
@@ -11,7 +11,9 @@
 BF, F32 = jnp.bfloat16, jnp.float32
 PITCH = 48
 COLS_OF = (1, 2, 0, 3)
+FAR = 8
 VM = pl.BlockSpec(memory_space=pltpu.VMEM)
+HBM = pl.BlockSpec(memory_space=pltpu.HBM)
 
 
 def dot(a, b):
@@ -126,10 +128,50 @@
         acc[h, :, i] = new if old is None else old[h, :, i] + new
 
 
-def own_kernel(feat, k1, proj, w, m, acc, edge, wide, plain, a, b, c, f):
-    build_weights(k1, proj, w, m)
+def fetch(sources, targets, sems):
+    copies = [pltpu.make_async_copy(a, b, sems.at[n]) for n, (a, b) in enumerate(zip(sources, targets, strict=True))]
+    for copy in copies:
+        copy.start()
+    for copy in copies:
+        copy.wait()
+
+
+def early():
+    return lax.axis_index("row") % FAR == 0
+
+
+def first_kernel(feat, k1, proj, send_b, send_a, w, m, strip_sems, k1_in, proj_in, sems):
+    last = (lax.axis_index("row") % 2) * (RW - HALO)
+    copies = []
+    for n, (begin, send) in enumerate([(last, send_b), (RW - HALO - last, send_a)]):
+        copies += [
+            pltpu.make_async_copy(feat.at[t, pl.ds(begin, HALO)], send.at[t], strip_sems.at[n, t]) for t in range(FR)
+        ]
+    for copy in copies:
+        copy.start()
+    for copy in copies:
+        copy.wait()
+
+    @pl.when(early())
+    def _():
+        fetch((k1, proj), (k1_in, proj_in), sems)
+        build_weights(k1_in, proj_in, w, m)
+
+
+def own_kernel(
+    feat, k1, proj, w_in, m_in, w, m, acc, edge, k1_in, proj_in, feat_in, sems, feat_sem, wide, plain, a, b, c, f
+):
+    copy = pltpu.make_async_copy(feat, feat_in, feat_sem)
+    copy.start()
+
+    @pl.when(jnp.logical_not(early()))
+    def _():
+        fetch((k1, proj), (k1_in, proj_in), sems)
+        build_weights(k1_in, proj_in, w, m)
+
+    copy.wait()
     ones = mean_matrix(C1)
-    lay_out(lambda t: feat[t].reshape(RW * CL, C1), range(RW), ones, wide, plain, a, b, c, f)
+    lay_out(lambda t: feat_in[t].reshape(RW * CL, C1), range(RW), ones, wide, plain, a, b, c, f)
     have = range(HALO, HALO + RW)
 
     def slot(r):
@@ -140,25 +182,60 @@
     edge[...] = ring(range(6), have, slot, w, c)
 
 
-HALO_ROWS = (0, 1, 2, 11, 12, 13)
-
-
-def halo_kernel(place, from_b, from_a, w, m, acc_in, edge_in, acc, edge, to_b, to_a, joined, wide, plain, a, b, c, f):
-    odd = place[0] % 2 == 1
-    for t in range(FR):
-        fb, fa = from_b[t], from_a[t]
-        joined[t, 0:HALO] = jnp.where(odd, fa, fb)
-        joined[t, HALO : 2 * HALO] = jnp.where(odd, fb, fa)
-    ones = mean_matrix(C1)
-    lay_out(lambda t: joined[t].reshape(2 * HALO * CL, C1), range(2 * HALO), ones, wide, plain, a, b, c, f)
-    slot = HALO_ROWS.index
-    for i in range(6):
-        if any(2 * i + dr in HALO_ROWS for dr in range(4)):
-            put(acc, i, contribute(i, HALO_ROWS, slot, w, m, a, b, f), acc_in)
-        else:
-            acc[:, :, i] = acc_in[:, :, i]
-    edge[...] = edge_in[...] + ring(range(6), HALO_ROWS, slot, w, c)
-    odd = place[1] % 2 == 1
+def add_side(low, got, w, m, acc_in, edge_in, acc, edge, wide, plain, a, b, c, f):
+    lay_out(lambda t: got[t].reshape(HALO * CL, C1), range(HALO), mean_matrix(C1), wide, plain, a, b, c, f)
+    whole, part = 5 * low, 1 + 3 * low
+    one = 2 * (1 - low)
+
+    def lines(src, p, r):
+        return src[p : p + FR, r].reshape(FR * 16, C2)
+
+    blank = jnp.zeros((16, C2), BF)
+    total = beside = None
+    for p in range(3):
+        left = jnp.concatenate(
+            [
+                jnp.concatenate([lines(src, p, r), blank if src is a else c[p, r]], axis=0)
+                for r in range(HALO)
+                for src in (a, b)
+            ],
+            axis=1,
+        )
+        one_left = jnp.concatenate(
+            [jnp.concatenate([lines(src, p, one), blank if src is a else c[p, one]], axis=0) for src in (a, b)], axis=1
+        )
+        here = dot(left, w[p, pl.ds(low, HALO)].reshape(HALO * 512, C2))
+        there = dot(one_left, w[p, 3 * low])
+        total = here if total is None else total + here
+        beside = there if beside is None else beside + there
+    skip = jnp.concatenate([f[:, 1 - low + n].reshape(FR * 16, C2) for n in range(2)], axis=1)
+    main = total[0 : FR * 16] + dot(skip, m[...])
+    for i, sums, rim in ((whole, main, total), (part, beside[0 : FR * 16], beside)):
+        for h in range(2):
+            acc[h, :, i] = acc_in[h, :, i] + sums[:, h * 128 : (h + 1) * 128].reshape(FR, 16, 128)
+        at = pl.ds(pl.multiple_of(i * 16, 16), 16)
+        edge[at] = edge_in[at] + rim[FR * 16 : FR * 16 + 16]
+
+
+def beside_far():
+    return lax.axis_index("row") % FAR < 2
+
+
+def near_kernel(got, w, m, acc_in, edge_in, acc, edge, *scratch):
+    @pl.when(beside_far())
+    def _():
+        add_side(1 - lax.axis_index("row") % 2, got, w, m, acc_in, edge_in, acc, edge, *scratch)
+
+
+def far_kernel(got, got_near, w, m, acc_in, edge_in, acc, edge, to_b, to_a, *scratch):
+    low = lax.axis_index("row") % 2
+
+    @pl.when(jnp.logical_not(beside_far()))
+    def _():
+        add_side(1 - low, got_near, w, m, acc_in, edge_in, acc, edge, *scratch)
+
+    add_side(low, got, w, m, acc_in, edge_in, acc, edge, *scratch)
+    odd = lax.axis_index("col") % 2 == 1
     flat = acc.reshape(2 * FR * 6 * 16, 128)
 
     def column(i, j):
@@ -173,8 +250,9 @@
         to_a[i] = jnp.where(odd, left, right).astype(BF)
 
 
-def final_kernel(last_row, last_col, place, from_b, pair, acc, edge_in, k2, out, lv, edge, wide, a2):
-    odd = place[1] % 2 == 1
+def final_kernel(last_row, last_col, from_b, pair, acc, edge_in, k2, out, lv, edge, wide, a2):
+    row, col = lax.axis_index("row"), lax.axis_index("col")
+    odd = col % 2 == 1
     for t in range(FR):
         for h in range(2):
             lv[h, t * 96 : (t + 1) * 96] = acc[h, t].reshape(96, 128)
@@ -193,10 +271,10 @@
 
     ones = mean_matrix(C2)
     keep = [jnp.float32(1.0)] * 6
-    keep[0] = jnp.where(place[0] == 0, 0.0, 1.0)
-    keep[5] = jnp.where(place[0] == last_row, 0.0, 1.0)
-    keep_left = jnp.where(place[1] == 0, 0.0, 1.0)
-    keep_right = jnp.where(place[1] == last_col, 0.0, 1.0)
+    keep[0] = jnp.where(row == 0, 0.0, 1.0)
+    keep[5] = jnp.where(row == last_row, 0.0, 1.0)
+    keep_left = jnp.where(col == 0, 0.0, 1.0)
+    keep_right = jnp.where(col == last_col, 0.0, 1.0)
     for t in range(FR):
         act = normed_silu(level(t * 96, 96), ones)
         for i in range(6):
@@ -248,47 +326,87 @@
     ]
 
 
+ROWS_SHAPE = in_vmem((FR, HALO, CL, C1), BF)
 W_SHAPE = in_vmem((3, 4, 512, C2), BF)
 M_SHAPE = in_vmem((512, C2), BF)
 ACC_SHAPE = in_vmem((2, FR, 6, 16, 128), F32)
 EDGE_SHAPE = in_vmem((96, C2), F32)
 STRIP_SHAPE = in_vmem((6, 16, C2), BF)
-SMEM = pl.BlockSpec(memory_space=pltpu.SMEM)
-PARAMS = pltpu.CompilerParams(vmem_limit_bytes=40 * 2**20)
-
-
-def own_part(feat, k1, proj):
+PARAMS = pltpu.CompilerParams(vmem_limit_bytes=24 * 2**20)
+
+
+def in_hbm(x):
+    return pltpu.with_memory_space_constraint(x, pltpu.HBM)
+
+
+def weight_scratch():
+    return [
+        pltpu.VMEM((3, 3, 3, C1, C1), BF),
+        pltpu.VMEM((4 * C1, C2), BF),
+    ]
+
+
+def first_part(feat, k1, proj):
+    return pl.pallas_call(
+        first_kernel,
+        out_shape=(ROWS_SHAPE,) * 2 + (W_SHAPE, M_SHAPE),
+        in_specs=[HBM] * 3,
+        out_specs=(VM,) * 4,
+        scratch_shapes=[pltpu.SemaphoreType.DMA((2, FR))] + weight_scratch() + [pltpu.SemaphoreType.DMA((2,))],
+        compiler_params=PARAMS,
+        name="first_part",
+    )(in_hbm(feat), in_hbm(k1), in_hbm(proj))
+
+
+def own_part(feat, k1, proj, w, m):
     return pl.pallas_call(
         own_kernel,
         out_shape=(W_SHAPE, M_SHAPE, ACC_SHAPE, EDGE_SHAPE),
-        in_specs=[VM] * 3,
+        in_specs=[HBM] * 3 + [VM] * 2,
         out_specs=(VM,) * 4,
-        scratch_shapes=operands(RW),
+        scratch_shapes=weight_scratch()
+        + [pltpu.VMEM((FR, RW, CL, C1), BF), pltpu.SemaphoreType.DMA((2,)), pltpu.SemaphoreType.DMA]
+        + operands(RW),
+        input_output_aliases={3: 0, 4: 1},
         compiler_params=PARAMS,
         name="own_part",
-    )(feat, k1, proj)
-
-
-def halo_part(place, from_b, from_a, w, m, acc, edge):
+    )(in_hbm(feat), in_hbm(k1), in_hbm(proj), w, m)
+
+
+def near_part(got, w, m, acc, edge):
     return pl.pallas_call(
-        halo_kernel,
+        near_kernel,
+        out_shape=(ACC_SHAPE, EDGE_SHAPE),
+        in_specs=[VM] * 5,
+        out_specs=(VM,) * 2,
+        scratch_shapes=operands(HALO),
+        input_output_aliases={3: 0, 4: 1},
+        compiler_params=PARAMS,
+        name="near_part",
+    )(got, w, m, acc, edge)
+
+
+def far_part(got, got_near, w, m, acc, edge):
+    return pl.pallas_call(
+        far_kernel,
         out_shape=(ACC_SHAPE, EDGE_SHAPE, STRIP_SHAPE, STRIP_SHAPE),
-        in_specs=[SMEM] + [VM] * 6,
+        in_specs=[VM] * 6,
         out_specs=(VM,) * 4,
-        scratch_shapes=[pltpu.VMEM((FR, 2 * HALO, CL, C1), BF)] + operands(2 * HALO),
+        scratch_shapes=operands(HALO),
+        input_output_aliases={4: 0, 5: 1},
         compiler_params=PARAMS,
-        name="halo_part",
-    )(place, from_b, from_a, w, m, acc, edge)
-
-
-def final_part(last_row, last_col, place, from_b, pair, acc, edge, k2):
+        name="far_part",
+    )(got, got_near, w, m, acc, edge)
+
+
+def final_part(last_row, last_col, from_b, pair, acc, edge, k2):
     def kernel(*refs):
         final_kernel(last_row, last_col, *refs)
 
     return pl.pallas_call(
         kernel,
         out_shape=in_vmem((FR, 4, 16, C2), BF),
-        in_specs=[SMEM] + [VM] * 5,
+        in_specs=[VM] * 5,
         out_specs=VM,
         scratch_shapes=[
             pltpu.VMEM((2, FR * 6 * 16, 128), F32),
@@ -298,7 +416,7 @@
         ],
         compiler_params=PARAMS,
         name="final_part",
-    )(place, from_b, pair, acc, edge, k2)
+    )(from_b, pair, acc, edge, k2)
 
 
 def pairs(first, count):
@@ -310,19 +428,18 @@
 
 def local(features, kernel_one, projection, kernel_two):
     rows, cols = lax.axis_size("row"), lax.axis_size("col")
-    row, col = lax.axis_index("row"), lax.axis_index("col")
-    place = jnp.stack([row, col]).astype(jnp.int32)
-    last = RW - HALO
-    odd = row % 2
-    send_b = lax.dynamic_slice_in_dim(features, odd * last, HALO, axis=1)
-    send_a = lax.dynamic_slice_in_dim(features, (1 - odd) * last, HALO, axis=1)
+    send_b, send_a, w, m = first_part(features, kernel_one, projection)
+    far_side = [(i, j) for i, j in pairs(0, rows) if min(i, j) % FAR == 0]
+    others = [pair for pair in pairs(0, rows) if pair not in far_side]
+    from_a = lax.ppermute(send_a, "row", far_side)
     from_b = lax.ppermute(send_b, "row", pairs(1, rows))
-    from_a = lax.ppermute(send_a, "row", pairs(0, rows))
-    w, m, acc, edge = own_part(features, kernel_one, projection)
-    acc, edge, to_b, to_a = halo_part(place, from_b, from_a, w, m, acc, edge)
+    from_a_too = lax.ppermute(send_a, "row", others)
+    w, m, acc, edge = own_part(features, kernel_one, projection, w, m)
+    acc, edge = near_part(from_a, w, m, acc, edge)
+    acc, edge, to_b, to_a = far_part(from_b, from_a_too, w, m, acc, edge)
     from_b = lax.ppermute(to_b, "col", pairs(1, cols))
     pair = lax.all_gather(to_a, "col", axis_index_groups=[[i, i + 1] for i in range(0, cols, 2)])
-    return final_part(rows - 1, cols - 1, place, from_b, pair, acc, edge, kernel_two)
+    return final_part(rows - 1, cols - 1, from_b, pair, acc, edge, kernel_two)
 
 
 def solution(mesh):

time: 40.7 us -> 39.5 us (0.971)
  local copies, waits for them, and re-layouts: 5.09 us -> 0.01 us
  waiting for transfers between devices: 1.17 us -> 5.3 us
  starting transfers between devices: 21.5 us -> 19.3 us
  Pallas kernels: 10.6 us -> 12.7 us
    ppermute x1, waiting for transfers between devices: 0.82 us -> 4.69 us  [local(): from_b = lax.ppermute(send_b, 'row', pairs(1, rows))]
    unnamed x8 -> x2, local copies, waits for them, and re-layouts: 3.16 us -> 0.01 us
    pallas_call x1 -> x3, Pallas kernels: 2.68 us -> 5.75 us  [the longest x1 3.78 us: first_part(): pl.pallas_call(first_kernel, out_shape=(ROWS_SHAPE,) * 2 + (W_SHAPE, M_SH...]
    dynamic_slice x1 -> x0, local copies, waits for them, and re-layouts: 1.93 us -> none  [local(): send_a = lax.dynamic_slice_in_dim(features, (1 - odd) * last, HALO, axis=1)]
    ppermute x1 -> x2, starting transfers between devices: 3.99 us -> 2.59 us  [the longest x1 1.92 us: local(): from_a = lax.ppermute(send_a, 'row', far_side)]
    ppermute x1, starting transfers between devices: 14.4 us -> 13.8 us  [local(): from_b = lax.ppermute(send_b, 'row', pairs(1, rows))]
    pallas_call x1, Pallas kernels: 3.8 us -> 3.27 us  [final_part(): pl.pallas_call(kernel, out_shape=in_vmem((FR, 4, 16, C2), BF), in_specs=[...]
    pallas_call x1, Pallas kernels: 4.15 us -> 3.65 us  [own_part(): pl.pallas_call(own_kernel, out_shape=(W_SHAPE, M_SHAPE, ACC_SHAPE, EDGE_S...]
  transfers between devices with their start and end apart: 3 -> 4, of which waited for: 2 -> 2; matrix products, arithmetic and copies ran while one was open for 0% -> 0% of each run, Pallas kernels for 10% -> 12%
where the time goes in v3:
time: 39.5 us; the launch traced here: 39.2 us
  starting transfers between devices  19.3 us (49%)
  Pallas kernels  12.7 us (32%)
  waiting for transfers between devices  5.3 us (13%)
  blocking collectives  1.88 us (5%)
    ppermute x1, starting transfers between devices, local(): from_b = lax.ppermute(send_b, 'row', pairs(1, rows))  13.8 us
    ppermute x1, waiting for transfers between devices, local(): from_b = lax.ppermute(send_b, 'row', pairs(1, rows))  4.69 us
    pallas_call x1, Pallas kernels, first_part(): pl.pallas_call(first_kernel, out_shape=(ROWS_SHAPE,) * 2 + (W_SHAPE, M_SH...  3.78 us
    pallas_call x1, Pallas kernels, own_part(): pl.pallas_call(own_kernel, out_shape=(W_SHAPE, M_SHAPE, ACC_SHAPE, EDGE_S...  3.65 us
    pallas_call x1, Pallas kernels, final_part(): pl.pallas_call(kernel, out_shape=in_vmem((FR, 4, 16, C2), BF), in_specs=[...  3.27 us
    ppermute x1, starting transfers between devices, local(): from_b = lax.ppermute(to_b, 'col', pairs(1, cols))  2.91 us
    ppermute x1, starting transfers between devices, local(): from_a = lax.ppermute(send_a, 'row', far_side)  1.92 us
    all_gather x1, blocking collectives, local(): lax.all_gather(to_a, 'col', axis_index_groups=[[i, i + 1] for i in range(...  1.88 us
  transfers between devices with their start and end apart: 4, of which 2 were waited for; matrix products, arithmetic and copies ran while one was open for 0% of the time, Pallas kernels for 12%

profile of v3, /device:TPU:7, one launch (start us, length us, event | category | flops | bytes accessed | tf_op | source)
XLA Modules:
  0.0 39.2 jit_solution(6056232736282983092)
XLA Ops:
  0.0 3.8 %first_part.1 = (bf16[8,3,32,128]{3,2,1,0:T(8,128)(2,1)S(1)}, bf16[8,3,32,128]{3,2,1,0:T(8,128)(2,1)S(1)}, bf16[3,4,512,256]{3,2,1,0:T(8,128)(2,1)S(1)}, bf16[512,256]{1,0:T(8,128)(2,1)S(1)}) custom-call(bf16[8,8,32,128]{3,2,1,0:T(8,128)(2,1)} %feat.3, bf16[3,3,3,128,128]{4,3,2,1,0:T(8,128)(2,1)} %k1.3, bf16[512,256]{1,0:T(8,128)(2,1)} %proj.3), custom_call_target="tpu_custom_call" | custom-call | tf_op jit(solution)/shard_map/first_part/pallas_call | solution.py:350
  3.8 1.9 %collective-permute-start.2 = (bf16[8,3,32,128]{3,2,1,0:T(8,128)(2,1)S(1)}, bf16[8,3,32,128]{3,2,1,0:T(8,128)(2,1)S(1)}, u32[]{:S(2)}, u32[]{:S(2)}) collective-permute-start(bf16[8,3,32,128]{3,2,1,0:T(8,128)(2,1)S(1)} %get-tuple-element.20), channel_id=1, source_target_pairs={{0,8},{8,0},{64,72},{72,64},{128,136},{136,128},{192,200},{200,192... | collective-permute-start | bytes 589832 | tf_op jit(solution)/shard_map/ppermute | solution.py:434
  5.7 0.7 %collective-permute-start.1 = (bf16[8,3,32,128]{3,2,1,0:T(8,128)(2,1)S(1)}, bf16[8,3,32,128]{3,2,1,0:T(8,128)(2,1)S(1)}, u32[]{:S(2)}, u32[]{:S(2)}) collective-permute-start(bf16[8,3,32,128]{3,2,1,0:T(8,128)(2,1)S(1)} %get-tuple-element.20), channel_id=1, source_target_pairs={{16,24},{24,16},{32,40},{40,32},{48,56},{56,48},{80,88},{88,80},{9... | collective-permute-start | bytes 589832 | tf_op jit(solution)/shard_map/ppermute | solution.py:436
  6.4 13.8 %collective-permute-start = (bf16[8,3,32,128]{3,2,1,0:T(8,128)(2,1)S(1)}, bf16[8,3,32,128]{3,2,1,0:T(8,128)(2,1)S(1)}, u32[]{:S(2)}, u32[]{:S(2)}) collective-permute-start(bf16[8,3,32,128]{3,2,1,0:T(8,128)(2,1)S(1)} %get-tuple-element.19), channel_id=1, source_target_pairs={{8,16},{16,8},{24,32},{32,24},{40,48},{48,40},{56,64},{64,56},{72,... | collective-permute-start | bytes 589832 | tf_op jit(solution)/shard_map/ppermute | solution.py:435
  20.2 3.6 %own_part.1 = (bf16[3,4,512,256]{3,2,1,0:T(8,128)(2,1)S(1)}, bf16[512,256]{1,0:T(8,128)(2,1)S(1)}, f32[2,8,6,16,128]{4,3,2,1,0:T(8,128)S(1)}, f32[96,256]{1,0:T(8,128)S(1)}) custom-call(bf16[8,8,32,128]{3,2,1,0:T(8,128)(2,1)} %feat.3, bf16[3,3,3,128,128]{4,3,2,1,0:T(8,128)(2,1)} %k1.3, ...), custom_call_target="tpu_custom_call", output_to_operand_aliasing={{0}: (3, {}), {1}: (4, {})} | custom-call | tf_op jit(solution)/shard_map/own_part/pallas_call | solution.py:362
  23.8 0.0 collective-permute-done.2.got
  23.8 0.9 %near_part.1 = (f32[2,8,6,16,128]{4,3,2,1,0:T(8,128)S(1)}, f32[96,256]{1,0:T(8,128)S(1)}) custom-call(bf16[8,3,32,128]{3,2,1,0:T(8,128)(2,1)S(1)} %collective-permute-done.2.got, bf16[3,4,512,256]{3,2,1,0:T(8,128)(2,1)S(1)} %get-tuple-element.23.w, bf16[512,256]{1,0:T(8,128)(2,1)S(1)} %get-tuple-element.24.m, ...), custom_call_target="tpu_custom_call", output_to_operand_aliasing={{0}: (3, {}), {1}: (4, {})} | custom-call | tf_op jit(solution)/shard_map/near_part/pallas_call | solution.py:377
  24.8 0.0 copy-start
  24.8 0.0 collective-permute-done.1.got_near
  24.8 4.7 %collective-permute-done.got = bf16[8,3,32,128]{3,2,1,0:T(8,128)(2,1)S(1)} collective-permute-done((bf16[8,3,32,128]{3,2,1,0:T(8,128)(2,1)S(1)}, bf16[8,3,32,128]{3,2,1,0:T(8,128)(2,1)S(1)}, u32[]{:S(2)}, u32[]{:S(2)}) %collective-permute-start) | collective-permute-done | bytes 196640 | tf_op jit(solution)/shard_map/ppermute | solution.py:435
  29.5 1.0 %far_part.1 = (f32[2,8,6,16,128]{4,3,2,1,0:T(8,128)S(1)}, f32[96,256]{1,0:T(8,128)S(1)}, bf16[6,16,256]{2,1,0:T(8,128)(2,1)S(1)}, bf16[6,16,256]{2,1,0:T(8,128)(2,1)S(1)}) custom-call(bf16[8,3,32,128]{3,2,1,0:T(8,128)(2,1)S(1)} %collective-permute-done.got, ...), custom_call_target="tpu_custom_call", output_to_operand_aliasing={{0}: (4, {}), {1}: (5, {})} | custom-call | tf_op jit(solution)/shard_map/far_part/pallas_call | solution.py:390
  30.5 2.9 %collective-permute-start.3 = (bf16[6,16,256]{2,1,0:T(8,128)(2,1)S(1)}, bf16[6,16,256]{2,1,0:T(8,128)(2,1)S(1)}, u32[]{:S(2)}, u32[]{:S(2)}) collective-permute-start(bf16[6,16,256]{2,1,0:T(8,128)(2,1)S(1)} %get-tuple-element.29), channel_id=1, source_target_pairs={{1,2},{2,1},{3,4},{4,3},{5,6},{6,5},{9,10},{10,9},{11,12},{12,11},... | collective-permute-start | bytes 147464 | tf_op jit(solution)/shard_map/ppermute | solution.py:440
  33.5 1.9 %all-gather = bf16[12,16,256]{2,1,0:T(8,128)(2,1)S(1)} all-gather(bf16[6,16,256]{2,1,0:T(8,128)(2,1)S(1)} %get-tuple-element.30), channel_id=2, replica_groups={{0,1},{2,3},{4,5},{6,7},{8,9},{10,11},{12,13},{14,15},{16,17},{18,19},{..., dimensions={0}, use_global_device_ids=true | all-gather | bytes 147456 | tf_op jit(solution)/shard_map/all_gather | solution.py:441
  35.3 0.6 %collective-permute-done.3.refs_0_ = bf16[6,16,256]{2,1,0:T(8,128)(2,1)S(1)} collective-permute-done((bf16[6,16,256]{2,1,0:T(8,128)(2,1)S(1)}, bf16[6,16,256]{2,1,0:T(8,128)(2,1)S(1)}, u32[]{:S(2)}, u32[]{:S(2)}) %collective-permute-start.3) | collective-permute-done | bytes 49184 | tf_op jit(solution)/shard_map/ppermute | solution.py:440
  35.9 0.0 copy-done
  35.9 3.3 %final_part.1 = bf16[8,4,16,256]{3,2,1,0:T(8,128)(2,1)} custom-call(bf16[6,16,256]{2,1,0:T(8,128)(2,1)S(1)} %collective-permute-done.3.refs_0_, bf16[2,6,16,256]{3,2,1,0:T(8,128)(2,1)S(1)} %bitcast.1, f32[2,8,6,16,128]{4,3,2,1,0:T(8,128)S(1)} %get-tuple-element.31.refs_2_, f32[96,256]{1,0:T(8,128)S(1)} %get-tuple-element.32.refs_3_, ...), custom_call_target="tpu_custom_call" | custom-call | tf_op jit(solution)/shard_map/final_part/pallas_call | solution.py:406
Async XLA Ops:
  3.8 20.0 %collective-permute-start.2 = (bf16[8,3,32,128]{3,2,1,0:T(8,128)(2,1)S(1)}, bf16[8,3,32,128]{3,2,1,0:T(8,128)(2,1)S(1)}, u32[]{:S(2)}, u32[]{:S(2)}) collective-permute-start(bf16[8,3,32,128]{3,2,1,0:T(8,128)(2,1)S(1)} %get-tuple-element.20), channel_id=1, source_target_pairs={{0,8},{8,0},{64,72},{72,64},{128,136},{136,128},{192,200},{200,192... | collective-permute-start | bytes 589832 | tf_op jit(solution)/shard_map/ppermute | solution.py:434
  5.7 19.1 %collective-permute-start.1 = (bf16[8,3,32,128]{3,2,1,0:T(8,128)(2,1)S(1)}, bf16[8,3,32,128]{3,2,1,0:T(8,128)(2,1)S(1)}, u32[]{:S(2)}, u32[]{:S(2)}) collective-permute-start(bf16[8,3,32,128]{3,2,1,0:T(8,128)(2,1)S(1)} %get-tuple-element.20), channel_id=1, source_target_pairs={{16,24},{24,16},{32,40},{40,32},{48,56},{56,48},{80,88},{88,80},{9... | collective-permute-start | bytes 589832 | tf_op jit(solution)/shard_map/ppermute | solution.py:436
  6.4 23.1 %collective-permute-start = (bf16[8,3,32,128]{3,2,1,0:T(8,128)(2,1)S(1)}, bf16[8,3,32,128]{3,2,1,0:T(8,128)(2,1)S(1)}, u32[]{:S(2)}, u32[]{:S(2)}) collective-permute-start(bf16[8,3,32,128]{3,2,1,0:T(8,128)(2,1)S(1)} %get-tuple-element.19), channel_id=1, source_target_pairs={{8,16},{16,8},{24,32},{32,24},{40,48},{48,40},{56,64},{64,56},{72,... | collective-permute-start | bytes 589832 | tf_op jit(solution)/shard_map/ppermute | solution.py:435
  24.8 11.1 %copy-start = (bf16[3,3,3,256,256]{4,3,2,1,0:T(8,128)(2,1)S(1)}, bf16[3,3,3,256,256]{4,3,2,1,0:T(8,128)(2,1)}, u32[]{:S(2)}) copy-start(bf16[3,3,3,256,256]{4,3,2,1,0:T(8,128)(2,1)} %refs_4_.1) | copy-start | bytes 10616836
  30.5 5.4 %collective-permute-start.3 = (bf16[6,16,256]{2,1,0:T(8,128)(2,1)S(1)}, bf16[6,16,256]{2,1,0:T(8,128)(2,1)S(1)}, u32[]{:S(2)}, u32[]{:S(2)}) collective-permute-start(bf16[6,16,256]{2,1,0:T(8,128)(2,1)S(1)} %get-tuple-element.29), channel_id=1, source_target_pairs={{1,2},{2,1},{3,4},{4,3},{5,6},{6,5},{9,10},{10,9},{11,12},{12,11},... | collective-permute-start | bytes 147464 | tf_op jit(solution)/shard_map/ppermute | solution.py:440

commit v4 on v3

--- a/solution.py
+++ b/solution.py
@@ -140,10 +140,10 @@
     return lax.axis_index("row") % FAR == 0
 
 
-def first_kernel(feat, k1, proj, send_b, send_a, w, m, strip_sems, k1_in, proj_in, sems):
+def first_kernel(feat, k1, proj, send_b, send_a, send_a_too, w, m, strip_sems, k1_in, proj_in, sems):
     last = (lax.axis_index("row") % 2) * (RW - HALO)
     copies = []
-    for n, (begin, send) in enumerate([(last, send_b), (RW - HALO - last, send_a)]):
+    for n, (begin, send) in enumerate([(last, send_b), (RW - HALO - last, send_a), (RW - HALO - last, send_a_too)]):
         copies += [
             pltpu.make_async_copy(feat.at[t, pl.ds(begin, HALO)], send.at[t], strip_sems.at[n, t]) for t in range(FR)
         ]
@@ -349,10 +349,10 @@
 def first_part(feat, k1, proj):
     return pl.pallas_call(
         first_kernel,
-        out_shape=(ROWS_SHAPE,) * 2 + (W_SHAPE, M_SHAPE),
+        out_shape=(ROWS_SHAPE,) * 3 + (W_SHAPE, M_SHAPE),
         in_specs=[HBM] * 3,
-        out_specs=(VM,) * 4,
-        scratch_shapes=[pltpu.SemaphoreType.DMA((2, FR))] + weight_scratch() + [pltpu.SemaphoreType.DMA((2,))],
+        out_specs=(VM,) * 5,
+        scratch_shapes=[pltpu.SemaphoreType.DMA((3, FR))] + weight_scratch() + [pltpu.SemaphoreType.DMA((2,))],
         compiler_params=PARAMS,
         name="first_part",
     )(in_hbm(feat), in_hbm(k1), in_hbm(proj))
@@ -428,12 +428,12 @@
 
 def local(features, kernel_one, projection, kernel_two):
     rows, cols = lax.axis_size("row"), lax.axis_size("col")
-    send_b, send_a, w, m = first_part(features, kernel_one, projection)
+    send_b, send_a, send_a_too, w, m = first_part(features, kernel_one, projection)
     far_side = [(i, j) for i, j in pairs(0, rows) if min(i, j) % FAR == 0]
     others = [pair for pair in pairs(0, rows) if pair not in far_side]
     from_a = lax.ppermute(send_a, "row", far_side)
     from_b = lax.ppermute(send_b, "row", pairs(1, rows))
-    from_a_too = lax.ppermute(send_a, "row", others)
+    from_a_too = lax.ppermute(send_a_too, "row", others)
     w, m, acc, edge = own_part(features, kernel_one, projection, w, m)
     acc, edge = near_part(from_a, w, m, acc, edge)
     acc, edge, to_b, to_a = far_part(from_b, from_a_too, w, m, acc, edge)

time: 39.5 us -> 37 us (0.937)
  waiting for transfers between devices: 5.3 us -> 3.62 us
  starting transfers between devices: 19.3 us -> 18.3 us
    ppermute x1, starting transfers between devices: 13.8 us -> 12.3 us  [local(): from_b = lax.ppermute(send_b, 'row', pairs(1, rows))]
    ppermute x1, waiting for transfers between devices: 4.69 us -> 3.51 us  [local(): from_b = lax.ppermute(send_b, 'row', pairs(1, rows))]
    ppermute x1, starting transfers between devices: 2.91 us -> 3.42 us  [local(): from_b = lax.ppermute(to_b, 'col', pairs(1, cols))]
    ppermute x1, waiting for transfers between devices: 0.61 us -> 0.1 us  [local(): from_b = lax.ppermute(to_b, 'col', pairs(1, cols))]
  transfers between devices with their start and end apart: 4 -> 4, of which waited for: 2 -> 2; matrix products, arithmetic and copies ran while one was open for 0% -> 0% of each run, Pallas kernels for 12% -> 13%
where the time goes in v4:
time: 37 us; the launch traced here: 36.7 us
  starting transfers between devices  18.3 us (49%)
  Pallas kernels  12.8 us (35%)
  waiting for transfers between devices  3.62 us (10%)
  blocking collectives  1.88 us (5%)
    ppermute x1, starting transfers between devices, local(): from_b = lax.ppermute(send_b, 'row', pairs(1, rows))  12.3 us
    pallas_call x1, Pallas kernels, first_part(): pl.pallas_call(first_kernel, out_shape=(ROWS_SHAPE,) * 3 + (W_SHAPE, M_SH...  3.93 us
    pallas_call x1, Pallas kernels, own_part(): pl.pallas_call(own_kernel, out_shape=(W_SHAPE, M_SHAPE, ACC_SHAPE, EDGE_S...  3.65 us
    ppermute x1, waiting for transfers between devices, local(): from_b = lax.ppermute(send_b, 'row', pairs(1, rows))  3.51 us
    ppermute x1, starting transfers between devices, local(): from_b = lax.ppermute(to_b, 'col', pairs(1, cols))  3.42 us
    pallas_call x1, Pallas kernels, final_part(): pl.pallas_call(kernel, out_shape=in_vmem((FR, 4, 16, C2), BF), in_specs=[...  3.26 us
    ppermute x1, starting transfers between devices, local(): from_a = lax.ppermute(send_a, 'row', far_side)  1.92 us
    all_gather x1, blocking collectives, local(): lax.all_gather(to_a, 'col', axis_index_groups=[[i, i + 1] for i in range(...  1.88 us
  transfers between devices with their start and end apart: 4, of which 2 were waited for; matrix products, arithmetic and copies ran while one was open for 0% of the time, Pallas kernels for 13%

profile of v4, /device:TPU:7, one launch (start us, length us, event | category | flops | bytes accessed | tf_op | source)
XLA Modules:
  0.0 36.7 jit_solution(9703309988684924263)
XLA Ops:
  0.0 3.9 %first_part.1 = (bf16[8,3,32,128]{3,2,1,0:T(8,128)(2,1)S(1)}, bf16[8,3,32,128]{3,2,1,0:T(8,128)(2,1)S(1)}, bf16[8,3,32,128]{3,2,1,0:T(8,128)(2,1)S(1)}, bf16[3,4...) custom-call(bf16[8,8,32,128]{3,2,1,0:T(8,128)(2,1)} %feat.3, bf16[3,3,3,128,128]{4,3,2,1,0:T(8,128)(2,1)} %k1.3, ...), custom_call_target="tpu_custom_call" | custom-call | tf_op jit(solution)/shard_map/first_part/pallas_call | solution.py:350
  3.9 1.9 %collective-permute-start.2 = (bf16[8,3,32,128]{3,2,1,0:T(8,128)(2,1)S(1)}, bf16[8,3,32,128]{3,2,1,0:T(8,128)(2,1)S(1)}, u32[]{:S(2)}, u32[]{:S(2)}) collective-permute-start(bf16[8,3,32,128]{3,2,1,0:T(8,128)(2,1)S(1)} %get-tuple-element.26), channel_id=1, source_target_pairs={{0,8},{8,0},{64,72},{72,64},{128,136},{136,128},{192,200},{200,192... | collective-permute-start | bytes 589832 | tf_op jit(solution)/shard_map/ppermute | solution.py:434
  5.9 12.3 %collective-permute-start = (bf16[8,3,32,128]{3,2,1,0:T(8,128)(2,1)S(1)}, bf16[8,3,32,128]{3,2,1,0:T(8,128)(2,1)S(1)}, u32[]{:S(2)}, u32[]{:S(2)}) collective-permute-start(bf16[8,3,32,128]{3,2,1,0:T(8,128)(2,1)S(1)} %get-tuple-element.20), channel_id=1, source_target_pairs={{8,16},{16,8},{24,32},{32,24},{40,48},{48,40},{56,64},{64,56},{72,... | collective-permute-start | bytes 589832 | tf_op jit(solution)/shard_map/ppermute | solution.py:435
  18.1 0.7 %collective-permute-start.1 = (bf16[8,3,32,128]{3,2,1,0:T(8,128)(2,1)S(1)}, bf16[8,3,32,128]{3,2,1,0:T(8,128)(2,1)S(1)}, u32[]{:S(2)}, u32[]{:S(2)}) collective-permute-start(bf16[8,3,32,128]{3,2,1,0:T(8,128)(2,1)S(1)} %get-tuple-element.21), channel_id=1, source_target_pairs={{16,24},{24,16},{32,40},{40,32},{48,56},{56,48},{80,88},{88,80},{9... | collective-permute-start | bytes 589832 | tf_op jit(solution)/shard_map/ppermute | solution.py:436
  18.8 3.6 %own_part.1 = (bf16[3,4,512,256]{3,2,1,0:T(8,128)(2,1)S(1)}, bf16[512,256]{1,0:T(8,128)(2,1)S(1)}, f32[2,8,6,16,128]{4,3,2,1,0:T(8,128)S(1)}, f32[96,256]{1,0:T(8,128)S(1)}) custom-call(bf16[8,8,32,128]{3,2,1,0:T(8,128)(2,1)} %feat.3, bf16[3,3,3,128,128]{4,3,2,1,0:T(8,128)(2,1)} %k1.3, ...), custom_call_target="tpu_custom_call", output_to_operand_aliasing={{0}: (3, {}), {1}: (4, {})} | custom-call | tf_op jit(solution)/shard_map/own_part/pallas_call | solution.py:362
  22.5 0.0 collective-permute-done.2.got
  22.5 1.0 %near_part.1 = (f32[2,8,6,16,128]{4,3,2,1,0:T(8,128)S(1)}, f32[96,256]{1,0:T(8,128)S(1)}) custom-call(bf16[8,3,32,128]{3,2,1,0:T(8,128)(2,1)S(1)} %collective-permute-done.2.got, bf16[3,4,512,256]{3,2,1,0:T(8,128)(2,1)S(1)} %get-tuple-element.24.w, bf16[512,256]{1,0:T(8,128)(2,1)S(1)} %get-tuple-element.25.m, ...), custom_call_target="tpu_custom_call", output_to_operand_aliasing={{0}: (3, {}), {1}: (4, {})} | custom-call | tf_op jit(solution)/shard_map/near_part/pallas_call | solution.py:377
  23.4 0.0 copy-start
  23.4 3.5 %collective-permute-done.got = bf16[8,3,32,128]{3,2,1,0:T(8,128)(2,1)S(1)} collective-permute-done((bf16[8,3,32,128]{3,2,1,0:T(8,128)(2,1)S(1)}, bf16[8,3,32,128]{3,2,1,0:T(8,128)(2,1)S(1)}, u32[]{:S(2)}, u32[]{:S(2)}) %collective-permute-start) | collective-permute-done | bytes 196640 | tf_op jit(solution)/shard_map/ppermute | solution.py:435
  27.0 0.0 collective-permute-done.1.got_near
  27.0 1.0 %far_part.1 = (f32[2,8,6,16,128]{4,3,2,1,0:T(8,128)S(1)}, f32[96,256]{1,0:T(8,128)S(1)}, bf16[6,16,256]{2,1,0:T(8,128)(2,1)S(1)}, bf16[6,16,256]{2,1,0:T(8,128)(2,1)S(1)}) custom-call(bf16[8,3,32,128]{3,2,1,0:T(8,128)(2,1)S(1)} %collective-permute-done.got, ...), custom_call_target="tpu_custom_call", output_to_operand_aliasing={{0}: (4, {}), {1}: (5, {})} | custom-call | tf_op jit(solution)/shard_map/far_part/pallas_call | solution.py:390
  28.0 3.4 %collective-permute-start.3 = (bf16[6,16,256]{2,1,0:T(8,128)(2,1)S(1)}, bf16[6,16,256]{2,1,0:T(8,128)(2,1)S(1)}, u32[]{:S(2)}, u32[]{:S(2)}) collective-permute-start(bf16[6,16,256]{2,1,0:T(8,128)(2,1)S(1)} %get-tuple-element.31), channel_id=1, source_target_pairs={{1,2},{2,1},{3,4},{4,3},{5,6},{6,5},{9,10},{10,9},{11,12},{12,11},... | collective-permute-start | bytes 147464 | tf_op jit(solution)/shard_map/ppermute | solution.py:440
  31.4 1.9 %all-gather = bf16[12,16,256]{2,1,0:T(8,128)(2,1)S(1)} all-gather(bf16[6,16,256]{2,1,0:T(8,128)(2,1)S(1)} %get-tuple-element.32), channel_id=2, replica_groups={{0,1},{2,3},{4,5},{6,7},{8,9},{10,11},{12,13},{14,15},{16,17},{18,19},{..., dimensions={0}, use_global_device_ids=true | all-gather | bytes 147456 | tf_op jit(solution)/shard_map/all_gather | solution.py:441
  33.3 0.1 collective-permute-done.3.refs_0_
  33.4 0.0 copy-done
  33.4 3.3 %final_part.1 = bf16[8,4,16,256]{3,2,1,0:T(8,128)(2,1)} custom-call(bf16[6,16,256]{2,1,0:T(8,128)(2,1)S(1)} %collective-permute-done.3.refs_0_, bf16[2,6,16,256]{3,2,1,0:T(8,128)(2,1)S(1)} %bitcast.1, f32[2,8,6,16,128]{4,3,2,1,0:T(8,128)S(1)} %get-tuple-element.33.refs_2_, f32[96,256]{1,0:T(8,128)S(1)} %get-tuple-element.34.refs_3_, ...), custom_call_target="tpu_custom_call" | custom-call | tf_op jit(solution)/shard_map/final_part/pallas_call | solution.py:406
Async XLA Ops:
  3.9 18.5 %collective-permute-start.2 = (bf16[8,3,32,128]{3,2,1,0:T(8,128)(2,1)S(1)}, bf16[8,3,32,128]{3,2,1,0:T(8,128)(2,1)S(1)}, u32[]{:S(2)}, u32[]{:S(2)}) collective-permute-start(bf16[8,3,32,128]{3,2,1,0:T(8,128)(2,1)S(1)} %get-tuple-element.26), channel_id=1, source_target_pairs={{0,8},{8,0},{64,72},{72,64},{128,136},{136,128},{192,200},{200,192... | collective-permute-start | bytes 589832 | tf_op jit(solution)/shard_map/ppermute | solution.py:434
  5.9 21.1 %collective-permute-start = (bf16[8,3,32,128]{3,2,1,0:T(8,128)(2,1)S(1)}, bf16[8,3,32,128]{3,2,1,0:T(8,128)(2,1)S(1)}, u32[]{:S(2)}, u32[]{:S(2)}) collective-permute-start(bf16[8,3,32,128]{3,2,1,0:T(8,128)(2,1)S(1)} %get-tuple-element.20), channel_id=1, source_target_pairs={{8,16},{16,8},{24,32},{32,24},{40,48},{48,40},{56,64},{64,56},{72,... | collective-permute-start | bytes 589832 | tf_op jit(solution)/shard_map/ppermute | solution.py:435
  18.1 8.8 %collective-permute-start.1 = (bf16[8,3,32,128]{3,2,1,0:T(8,128)(2,1)S(1)}, bf16[8,3,32,128]{3,2,1,0:T(8,128)(2,1)S(1)}, u32[]{:S(2)}, u32[]{:S(2)}) collective-permute-start(bf16[8,3,32,128]{3,2,1,0:T(8,128)(2,1)S(1)} %get-tuple-element.21), channel_id=1, source_target_pairs={{16,24},{24,16},{32,40},{40,32},{48,56},{56,48},{80,88},{88,80},{9... | collective-permute-start | bytes 589832 | tf_op jit(solution)/shard_map/ppermute | solution.py:436
  23.4 10.0 %copy-start = (bf16[3,3,3,256,256]{4,3,2,1,0:T(8,128)(2,1)S(1)}, bf16[3,3,3,256,256]{4,3,2,1,0:T(8,128)(2,1)}, u32[]{:S(2)}) copy-start(bf16[3,3,3,256,256]{4,3,2,1,0:T(8,128)(2,1)} %refs_4_.1) | copy-start | bytes 10616836
  28.0 5.4 %collective-permute-start.3 = (bf16[6,16,256]{2,1,0:T(8,128)(2,1)S(1)}, bf16[6,16,256]{2,1,0:T(8,128)(2,1)S(1)}, u32[]{:S(2)}, u32[]{:S(2)}) collective-permute-start(bf16[6,16,256]{2,1,0:T(8,128)(2,1)S(1)} %get-tuple-element.31), channel_id=1, source_target_pairs={{1,2},{2,1},{3,4},{4,3},{5,6},{6,5},{9,10},{10,9},{11,12},{12,11},... | collective-permute-start | bytes 147464 | tf_op jit(solution)/shard_map/ppermute | solution.py:440

commit v5 on v4

--- a/solution.py
+++ b/solution.py
@@ -11,7 +11,7 @@
 BF, F32 = jnp.bfloat16, jnp.float32
 PITCH = 48
 COLS_OF = (1, 2, 0, 3)
-FAR = 8
+FAR = 16
 VM = pl.BlockSpec(memory_space=pltpu.VMEM)
 HBM = pl.BlockSpec(memory_space=pltpu.HBM)
 
@@ -142,14 +142,26 @@
 
 def first_kernel(feat, k1, proj, send_b, send_a, send_a_too, w, m, strip_sems, k1_in, proj_in, sems):
     last = (lax.axis_index("row") % 2) * (RW - HALO)
-    copies = []
-    for n, (begin, send) in enumerate([(last, send_b), (RW - HALO - last, send_a), (RW - HALO - last, send_a_too)]):
-        copies += [
+
+    def strips(n, begin, send):
+        return [
             pltpu.make_async_copy(feat.at[t, pl.ds(begin, HALO)], send.at[t], strip_sems.at[n, t]) for t in range(FR)
         ]
-    for copy in copies:
+
+    far = strips(0, last, send_b)
+    for copy in far:
         copy.start()
-    for copy in copies:
+    for wanted, send in ((beside_far(), send_a), (jnp.logical_not(beside_far()), send_a_too)):
+
+        @pl.when(wanted)
+        def _(send=send):
+            near = strips(1, RW - HALO - last, send)
+            for copy in near:
+                copy.start()
+            for copy in near:
+                copy.wait()
+
+    for copy in far:
         copy.wait()
 
     @pl.when(early())
@@ -352,7 +364,7 @@
         out_shape=(ROWS_SHAPE,) * 3 + (W_SHAPE, M_SHAPE),
         in_specs=[HBM] * 3,
         out_specs=(VM,) * 5,
-        scratch_shapes=[pltpu.SemaphoreType.DMA((3, FR))] + weight_scratch() + [pltpu.SemaphoreType.DMA((2,))],
+        scratch_shapes=[pltpu.SemaphoreType.DMA((2, FR))] + weight_scratch() + [pltpu.SemaphoreType.DMA((2,))],
         compiler_params=PARAMS,
         name="first_part",
     )(in_hbm(feat), in_hbm(k1), in_hbm(proj))

time: 37 us -> 35.4 us (0.957)
  waiting for transfers between devices: 3.62 us -> 0.01 us
  starting transfers between devices: 18.3 us -> 20.1 us
    ppermute x1, waiting for transfers between devices: 3.51 us -> 0.01 us  [local(): from_b = lax.ppermute(send_b, 'row', pairs(1, rows))]
    ppermute x1, starting transfers between devices: 3.42 us -> 5.21 us  [local(): from_b = lax.ppermute(to_b, 'col', pairs(1, cols))]
  transfers between devices with their start and end apart: 4 -> 4, of which waited for: 2 -> 0; matrix products, arithmetic and copies ran while one was open for 0% -> 0% of each run, Pallas kernels for 13% -> 13%
where the time goes in v5:
time: 35.4 us; the launch traced here: 34.8 us
  starting transfers between devices  20.1 us (57%)
  Pallas kernels  12.7 us (36%)
  blocking collectives  1.88 us (5%)
    ppermute x1, starting transfers between devices, local(): from_b = lax.ppermute(send_b, 'row', pairs(1, rows))  12.3 us
    ppermute x1, starting transfers between devices, local(): from_b = lax.ppermute(to_b, 'col', pairs(1, cols))  5.21 us
    pallas_call x1, Pallas kernels, first_part(): pl.pallas_call(first_kernel, out_shape=(ROWS_SHAPE,) * 3 + (W_SHAPE, M_SH...  3.79 us
    pallas_call x1, Pallas kernels, own_part(): pl.pallas_call(own_kernel, out_shape=(W_SHAPE, M_SHAPE, ACC_SHAPE, EDGE_S...  3.65 us
    pallas_call x1, Pallas kernels, final_part(): pl.pallas_call(kernel, out_shape=in_vmem((FR, 4, 16, C2), BF), in_specs=[...  3.27 us
    ppermute x1, starting transfers between devices, local(): from_a = lax.ppermute(send_a, 'row', far_side)  1.92 us
    all_gather x1, blocking collectives, local(): lax.all_gather(to_a, 'col', axis_index_groups=[[i, i + 1] for i in range(...  1.88 us
    pallas_call x1, Pallas kernels, far_part(): pl.pallas_call(far_kernel, out_shape=(ACC_SHAPE, EDGE_SHAPE, STRIP_SHAPE,...  1.04 us
  transfers between devices with their start and end apart: 4, of which 0 were waited for; matrix products, arithmetic and copies ran while one was open for 0% of the time, Pallas kernels for 13%

profile of v5, /device:TPU:7, one launch (start us, length us, event | category | flops | bytes accessed | tf_op | source)
XLA Modules:
  0.0 34.8 jit_solution(3836736111116481644)
XLA Ops:
  0.0 3.8 %first_part.1 = (bf16[8,3,32,128]{3,2,1,0:T(8,128)(2,1)S(1)}, bf16[8,3,32,128]{3,2,1,0:T(8,128)(2,1)S(1)}, bf16[8,3,32,128]{3,2,1,0:T(8,128)(2,1)S(1)}, bf16[3,4...) custom-call(bf16[8,8,32,128]{3,2,1,0:T(8,128)(2,1)} %feat.3, bf16[3,3,3,128,128]{4,3,2,1,0:T(8,128)(2,1)} %k1.3, ...), custom_call_target="tpu_custom_call" | custom-call | tf_op jit(solution)/shard_map/first_part/pallas_call | solution.py:362
  3.8 1.9 %collective-permute-start.2 = (bf16[8,3,32,128]{3,2,1,0:T(8,128)(2,1)S(1)}, bf16[8,3,32,128]{3,2,1,0:T(8,128)(2,1)S(1)}, u32[]{:S(2)}, u32[]{:S(2)}) collective-permute-start(bf16[8,3,32,128]{3,2,1,0:T(8,128)(2,1)S(1)} %get-tuple-element.26), channel_id=1, source_target_pairs={{0,8},{8,0},{128,136},{136,128},{256,264},{264,256},{384,392},{392... | collective-permute-start | bytes 589832 | tf_op jit(solution)/shard_map/ppermute | solution.py:446
  5.7 12.3 %collective-permute-start = (bf16[8,3,32,128]{3,2,1,0:T(8,128)(2,1)S(1)}, bf16[8,3,32,128]{3,2,1,0:T(8,128)(2,1)S(1)}, u32[]{:S(2)}, u32[]{:S(2)}) collective-permute-start(bf16[8,3,32,128]{3,2,1,0:T(8,128)(2,1)S(1)} %get-tuple-element.20), channel_id=1, source_target_pairs={{8,16},{16,8},{24,32},{32,24},{40,48},{48,40},{56,64},{64,56},{72,... | collective-permute-start | bytes 589832 | tf_op jit(solution)/shard_map/ppermute | solution.py:447
  18.0 0.7 %collective-permute-start.1 = (bf16[8,3,32,128]{3,2,1,0:T(8,128)(2,1)S(1)}, bf16[8,3,32,128]{3,2,1,0:T(8,128)(2,1)S(1)}, u32[]{:S(2)}, u32[]{:S(2)}) collective-permute-start(bf16[8,3,32,128]{3,2,1,0:T(8,128)(2,1)S(1)} %get-tuple-element.21), channel_id=1, source_target_pairs={{16,24},{24,16},{32,40},{40,32},{48,56},{56,48},{64,72},{72,64},{8... | collective-permute-start | bytes 589832 | tf_op jit(solution)/shard_map/ppermute | solution.py:448
  18.7 3.6 %own_part.1 = (bf16[3,4,512,256]{3,2,1,0:T(8,128)(2,1)S(1)}, bf16[512,256]{1,0:T(8,128)(2,1)S(1)}, f32[2,8,6,16,128]{4,3,2,1,0:T(8,128)S(1)}, f32[96,256]{1,0:T(8,128)S(1)}) custom-call(bf16[8,8,32,128]{3,2,1,0:T(8,128)(2,1)} %feat.3, bf16[3,3,3,128,128]{4,3,2,1,0:T(8,128)(2,1)} %k1.3, ...), custom_call_target="tpu_custom_call", output_to_operand_aliasing={{0}: (3, {}), {1}: (4, {})} | custom-call | tf_op jit(solution)/shard_map/own_part/pallas_call | solution.py:374
  22.3 0.0 collective-permute-done.2.got
  22.3 1.0 %near_part.1 = (f32[2,8,6,16,128]{4,3,2,1,0:T(8,128)S(1)}, f32[96,256]{1,0:T(8,128)S(1)}) custom-call(bf16[8,3,32,128]{3,2,1,0:T(8,128)(2,1)S(1)} %collective-permute-done.2.got, bf16[3,4,512,256]{3,2,1,0:T(8,128)(2,1)S(1)} %get-tuple-element.24.w, bf16[512,256]{1,0:T(8,128)(2,1)S(1)} %get-tuple-element.25.m, ...), custom_call_target="tpu_custom_call", output_to_operand_aliasing={{0}: (3, {}), {1}: (4, {})} | custom-call | tf_op jit(solution)/shard_map/near_part/pallas_call | solution.py:389
  23.3 0.0 copy-start
  23.3 0.0 collective-permute-done.got
  23.3 0.0 collective-permute-done.1.got_near
  23.3 1.0 %far_part.1 = (f32[2,8,6,16,128]{4,3,2,1,0:T(8,128)S(1)}, f32[96,256]{1,0:T(8,128)S(1)}, bf16[6,16,256]{2,1,0:T(8,128)(2,1)S(1)}, bf16[6,16,256]{2,1,0:T(8,128)(2,1)S(1)}) custom-call(bf16[8,3,32,128]{3,2,1,0:T(8,128)(2,1)S(1)} %collective-permute-done.got, ...), custom_call_target="tpu_custom_call", output_to_operand_aliasing={{0}: (4, {}), {1}: (5, {})} | custom-call | tf_op jit(solution)/shard_map/far_part/pallas_call | solution.py:402
  24.4 5.2 %collective-permute-start.3 = (bf16[6,16,256]{2,1,0:T(8,128)(2,1)S(1)}, bf16[6,16,256]{2,1,0:T(8,128)(2,1)S(1)}, u32[]{:S(2)}, u32[]{:S(2)}) collective-permute-start(bf16[6,16,256]{2,1,0:T(8,128)(2,1)S(1)} %get-tuple-element.31), channel_id=1, source_target_pairs={{1,2},{2,1},{3,4},{4,3},{5,6},{6,5},{9,10},{10,9},{11,12},{12,11},... | collective-permute-start | bytes 147464 | tf_op jit(solution)/shard_map/ppermute | solution.py:452
  29.6 1.9 %all-gather = bf16[12,16,256]{2,1,0:T(8,128)(2,1)S(1)} all-gather(bf16[6,16,256]{2,1,0:T(8,128)(2,1)S(1)} %get-tuple-element.32), channel_id=2, replica_groups={{0,1},{2,3},{4,5},{6,7},{8,9},{10,11},{12,13},{14,15},{16,17},{18,19},{..., dimensions={0}, use_global_device_ids=true | all-gather | bytes 147456 | tf_op jit(solution)/shard_map/all_gather | solution.py:453
  31.5 0.0 collective-permute-done.3.refs_0_
  31.5 0.0 copy-done
  31.5 3.3 %final_part.1 = bf16[8,4,16,256]{3,2,1,0:T(8,128)(2,1)} custom-call(bf16[6,16,256]{2,1,0:T(8,128)(2,1)S(1)} %collective-permute-done.3.refs_0_, bf16[2,6,16,256]{3,2,1,0:T(8,128)(2,1)S(1)} %bitcast.1, f32[2,8,6,16,128]{4,3,2,1,0:T(8,128)S(1)} %get-tuple-element.33.refs_2_, f32[96,256]{1,0:T(8,128)S(1)} %get-tuple-element.34.refs_3_, ...), custom_call_target="tpu_custom_call" | custom-call | tf_op jit(solution)/shard_map/final_part/pallas_call | solution.py:418
Async XLA Ops:
  3.8 18.5 %collective-permute-start.2 = (bf16[8,3,32,128]{3,2,1,0:T(8,128)(2,1)S(1)}, bf16[8,3,32,128]{3,2,1,0:T(8,128)(2,1)S(1)}, u32[]{:S(2)}, u32[]{:S(2)}) collective-permute-start(bf16[8,3,32,128]{3,2,1,0:T(8,128)(2,1)S(1)} %get-tuple-element.26), channel_id=1, source_target_pairs={{0,8},{8,0},{128,136},{136,128},{256,264},{264,256},{384,392},{392... | collective-permute-start | bytes 589832 | tf_op jit(solution)/shard_map/ppermute | solution.py:446
  5.7 17.6 %collective-permute-start = (bf16[8,3,32,128]{3,2,1,0:T(8,128)(2,1)S(1)}, bf16[8,3,32,128]{3,2,1,0:T(8,128)(2,1)S(1)}, u32[]{:S(2)}, u32[]{:S(2)}) collective-permute-start(bf16[8,3,32,128]{3,2,1,0:T(8,128)(2,1)S(1)} %get-tuple-element.20), channel_id=1, source_target_pairs={{8,16},{16,8},{24,32},{32,24},{40,48},{48,40},{56,64},{64,56},{72,... | collective-permute-start | bytes 589832 | tf_op jit(solution)/shard_map/ppermute | solution.py:447
  18.0 5.3 %collective-permute-start.1 = (bf16[8,3,32,128]{3,2,1,0:T(8,128)(2,1)S(1)}, bf16[8,3,32,128]{3,2,1,0:T(8,128)(2,1)S(1)}, u32[]{:S(2)}, u32[]{:S(2)}) collective-permute-start(bf16[8,3,32,128]{3,2,1,0:T(8,128)(2,1)S(1)} %get-tuple-element.21), channel_id=1, source_target_pairs={{16,24},{24,16},{32,40},{40,32},{48,56},{56,48},{64,72},{72,64},{8... | collective-permute-start | bytes 589832 | tf_op jit(solution)/shard_map/ppermute | solution.py:448
  23.3 8.2 %copy-start = (bf16[3,3,3,256,256]{4,3,2,1,0:T(8,128)(2,1)S(1)}, bf16[3,3,3,256,256]{4,3,2,1,0:T(8,128)(2,1)}, u32[]{:S(2)}) copy-start(bf16[3,3,3,256,256]{4,3,2,1,0:T(8,128)(2,1)} %refs_4_.1) | copy-start | bytes 10616836
  24.4 7.1 %collective-permute-start.3 = (bf16[6,16,256]{2,1,0:T(8,128)(2,1)S(1)}, bf16[6,16,256]{2,1,0:T(8,128)(2,1)S(1)}, u32[]{:S(2)}, u32[]{:S(2)}) collective-permute-start(bf16[6,16,256]{2,1,0:T(8,128)(2,1)S(1)} %get-tuple-element.31), channel_id=1, source_target_pairs={{1,2},{2,1},{3,4},{4,3},{5,6},{6,5},{9,10},{10,9},{11,12},{12,11},... | collective-permute-start | bytes 147464 | tf_op jit(solution)/shard_map/ppermute | solution.py:452

commit v6 on v5

--- a/solution.py
+++ b/solution.py
@@ -11,6 +11,7 @@
 BF, F32 = jnp.bfloat16, jnp.float32
 PITCH = 48
 COLS_OF = (1, 2, 0, 3)
+NEXT = 8
 FAR = 16
 VM = pl.BlockSpec(memory_space=pltpu.VMEM)
 HBM = pl.BlockSpec(memory_space=pltpu.HBM)
@@ -30,7 +31,7 @@
     return jnp.full((n, n), 1.0 / n, BF)
 
 
-def build_weights(k1, proj, w, m):
+def build_maps(proj, m):
     p0, p1, p2, p3 = (proj[i * C1 : (i + 1) * C1].astype(F32) * 0.5 for i in range(4))
     row = lax.broadcasted_iota(jnp.int32, (C1, C2), 0)
     col = lax.broadcasted_iota(jnp.int32, (C1, C2), 1)
@@ -39,12 +40,15 @@
     m[C1 : 2 * C1] = (p0 + p1 - p2 - p3 + twice).astype(BF)
     m[2 * C1 : 3 * C1] = (p0 - p1 + p2 - p3 + twice).astype(BF)
     m[3 * C1 : 4 * C1] = (p0 - p1 - p2 + p3 + twice).astype(BF)
+
+
+def build_weights(frames, k1, w, m):
     zero = jnp.zeros((C1, C1), BF)
 
     def tap(p, q, s):
         return k1[p, q, s] if 0 <= s < 3 else zero
 
-    for p in range(3):
+    for p in frames:
         for dr in range(4):
             pairs = [pr for pr in range(2) if 0 <= dr - pr < 3]
             left = jnp.concatenate(
@@ -128,19 +132,17 @@
         acc[h, :, i] = new if old is None else old[h, :, i] + new
 
 
-def fetch(sources, targets, sems):
-    copies = [pltpu.make_async_copy(a, b, sems.at[n]) for n, (a, b) in enumerate(zip(sources, targets, strict=True))]
-    for copy in copies:
-        copy.start()
-    for copy in copies:
-        copy.wait()
-
-
 def early():
     return lax.axis_index("row") % FAR == 0
 
 
-def first_kernel(feat, k1, proj, send_b, send_a, send_a_too, w, m, strip_sems, k1_in, proj_in, sems):
+def waits():
+    return lax.axis_index("row") % NEXT == 0
+
+
+def first_kernel(
+    feat, k1, proj, send_b, send_a, send_a_too, w, m, feat_in, k1_in, strip_sems, feat_sem, proj_in, sems
+):
     last = (lax.axis_index("row") % 2) * (RW - HALO)
 
     def strips(n, begin, send):
@@ -151,6 +153,18 @@
     far = strips(0, last, send_b)
     for copy in far:
         copy.start()
+
+    @pl.when(waits())
+    def _():
+        pltpu.make_async_copy(feat, feat_in, feat_sem).start()
+
+    weights = [pltpu.make_async_copy(x, y, sems.at[n]) for n, (x, y) in enumerate([(k1, k1_in), (proj, proj_in)])]
+
+    @pl.when(early())
+    def _():
+        for copy in weights:
+            copy.start()
+
     for wanted, send in ((beside_far(), send_a), (jnp.logical_not(beside_far()), send_a_too)):
 
         @pl.when(wanted)
@@ -164,24 +178,91 @@
     for copy in far:
         copy.wait()
 
+    @pl.when(waits())
+    def _():
+        pltpu.make_async_copy(feat, feat_in, feat_sem).wait()
+
     @pl.when(early())
     def _():
-        fetch((k1, proj), (k1_in, proj_in), sems)
-        build_weights(k1_in, proj_in, w, m)
+        for copy in weights:
+            copy.wait()
+        build_maps(proj_in, m)
+        build_weights((0,), k1_in, w, m)
+
+
+def middle_columns(acc, tall, act_in):
+    x = jnp.concatenate([acc[h, :, 2:4].reshape(FR * 2 * 16, 128) for h in range(2)], axis=1)
+    column = lax.broadcasted_iota(jnp.int32, (FR * 2 * 16, C2), 0) % 16
+    inner = jnp.where((column > 0) & (column < 15), 1.0, 0.0).astype(F32)
+    act = normed_silu(x, mean_matrix(C2)) * inner
+    for n in range(2 * FR):
+        for h in range(2):
+            tall[h, n * 32 : n * 32 + 8] = jnp.zeros((8, 128), F32)
+            tall[h, n * 32 + 24 : n * 32 + 32] = jnp.zeros((8, 128), F32)
+            tall[h, n * 32 + 8 : n * 32 + 24] = act[n * 16 : (n + 1) * 16, h * 128 : (h + 1) * 128]
+    for s in range(3):
+        for n in range(2):
+            for t in range(2):
+                act_in[s, t, n] = jnp.zeros((16, C2), BF)
+            for t in range(FR):
+                base = (t * 2 + n) * 32 + 7 + s
+                for h in range(2):
+                    act_in[s, t + 2, n, :, h * 128 : (h + 1) * 128] = tall[h, base : base + 16].astype(BF)
+
+
+def middle(k2, mid, act_in):
+    for i in range(4):
+        taps = [q for q in range(3) if i + q in (2, 3)]
+        total = None
+        for p in range(3):
+            left = jnp.concatenate(
+                [act_in[s, p : p + FR, i + q - 2].reshape(FR * 16, C2) for q in taps for s in range(3)], axis=1
+            )
+            got = dot(left, k2[p, taps[0] : taps[-1] + 1].reshape(len(taps) * 3 * C2, C2))
+            total = got if total is None else total + got
+        for h in range(2):
+            mid[h, i * FR * 16 : (i + 1) * FR * 16] = total[:, h * 128 : (h + 1) * 128]
 
 
 def own_kernel(
-    feat, k1, proj, w_in, m_in, w, m, acc, edge, k1_in, proj_in, feat_in, sems, feat_sem, wide, plain, a, b, c, f
+    feat, k1, proj, k2_far, w_in, m_in, feat_here, k1_here,
+    w, m, feat_in, k1_in, acc, edge, k2, mid,
+    proj_in, sems, late_sems, tall, act_in, wide, plain, a, b, c, f,
 ):
-    copy = pltpu.make_async_copy(feat, feat_in, feat_sem)
-    copy.start()
-
-    @pl.when(jnp.logical_not(early()))
-    def _():
-        fetch((k1, proj), (k1_in, proj_in), sems)
-        build_weights(k1_in, proj_in, w, m)
-
-    copy.wait()
+    copy = pltpu.make_async_copy(feat, feat_in, late_sems.at[0])
+
+    @pl.when(jnp.logical_not(waits()))
+    def _():
+        copy.start()
+
+    make = jnp.logical_not(early())
+    sources = [
+        pltpu.make_async_copy(x, y, sems.at[n]) for n, (x, y) in enumerate([(k1, k1_in), (proj, proj_in)])
+    ]
+
+    @pl.when(make)
+    def _():
+        for source in sources:
+            source.start()
+
+    @pl.when(jnp.logical_not(waits()))
+    def _():
+        copy.wait()
+
+    @pl.when(make)
+    def _():
+        for source in sources:
+            source.wait()
+
+    copy_k2 = pltpu.make_async_copy(k2_far, k2, late_sems.at[1])
+    copy_k2.start()
+
+    @pl.when(make)
+    def _():
+        build_maps(proj_in, m)
+        build_weights((0,), k1_in, w, m)
+
+    build_weights((1, 2), k1_in, w, m)
     ones = mean_matrix(C1)
     lay_out(lambda t: feat_in[t].reshape(RW * CL, C1), range(RW), ones, wide, plain, a, b, c, f)
     have = range(HALO, HALO + RW)
@@ -189,9 +270,14 @@
     def slot(r):
         return r - HALO
 
-    for i in range(6):
+    for i in (2, 3):
+        put(acc, i, contribute(i, have, slot, w, m, a, b, f))
+    middle_columns(acc, tall, act_in)
+    for i in (0, 1, 4, 5):
         put(acc, i, contribute(i, have, slot, w, m, a, b, f))
     edge[...] = ring(range(6), have, slot, w, c)
+    copy_k2.wait()
+    middle(k2, mid, act_in)
 
 
 def add_side(low, got, w, m, acc_in, edge_in, acc, edge, wide, plain, a, b, c, f):
@@ -241,12 +327,20 @@
 
 def far_kernel(got, got_near, w, m, acc_in, edge_in, acc, edge, to_b, to_a, *scratch):
     low = lax.axis_index("row") % 2
+    half = len(scratch) // 2
+
+    def far():
+        add_side(low, got, w, m, acc_in, edge_in, acc, edge, *scratch[:half])
+
+    @pl.when(beside_far())
+    def _():
+        far()
 
     @pl.when(jnp.logical_not(beside_far()))
     def _():
-        add_side(1 - low, got_near, w, m, acc_in, edge_in, acc, edge, *scratch)
-
-    add_side(low, got, w, m, acc_in, edge_in, acc, edge, *scratch)
+        add_side(1 - low, got_near, w, m, acc_in, edge_in, acc, edge, *scratch[half:])
+        far()
+
     odd = lax.axis_index("col") % 2 == 1
     flat = acc.reshape(2 * FR * 6 * 16, 128)
 
@@ -262,7 +356,11 @@
         to_a[i] = jnp.where(odd, left, right).astype(BF)
 
 
-def final_kernel(last_row, last_col, from_b, pair, acc, edge_in, k2, out, lv, edge, wide, a2):
+OUTER = (0, 1, 4, 5)
+FIXED = (0, 1, 14, 15)
+
+
+def final_kernel(last_row, last_col, from_b, pair, acc, edge_in, k2, mid_in, out, mid, lv, edge, wide, a2, beside):
     row, col = lax.axis_index("row"), lax.axis_index("col")
     odd = col % 2 == 1
     for t in range(FR):
@@ -278,49 +376,100 @@
             half = slice(h * 128, (h + 1) * 128)
             lv[h, pl.ds(i * 16, FR, stride=96), :] += left[8:16, half]
             lv[h, pl.ds(i * 16 + 15, FR, stride=96), :] += right[0:8, half]
+
     def level(at, count):
         return jnp.concatenate([lv[0, at : at + count], lv[1, at : at + count]], axis=1)
 
     ones = mean_matrix(C2)
-    keep = [jnp.float32(1.0)] * 6
+    keep = {i: jnp.float32(1.0) for i in range(6)}
     keep[0] = jnp.where(row == 0, 0.0, 1.0)
     keep[5] = jnp.where(row == last_row, 0.0, 1.0)
     keep_left = jnp.where(col == 0, 0.0, 1.0)
     keep_right = jnp.where(col == last_col, 0.0, 1.0)
     for t in range(FR):
-        act = normed_silu(level(t * 96, 96), ones)
-        for i in range(6):
-            base = (t * 6 + i) * 32 + 8
-            kept = act[i * 16 : (i + 1) * 16] * keep[i]
+        act = normed_silu(jnp.concatenate([level(t * 96, 32), level(t * 96 + 64, 32)], axis=0), ones)
+        for k, i in enumerate(OUTER):
+            base = (t * 4 + k) * 32 + 8
+            kept = act[k * 16 : (k + 1) * 16] * keep[i]
             for h in range(2):
                 wide[h, base : base + 16] = kept[:, h * 128 : (h + 1) * 128]
-    act = normed_silu(edge[...], ones)
-    for i in range(6):
+
+    def column(i, j):
+        return jnp.concatenate([lv[h, pl.ds(i * 16 + j, FR, stride=96), :] for h in range(2)], axis=1)
+
+    act = normed_silu(
+        jnp.concatenate([edge[...]] + [column(i, j) for i in (2, 3) for j in (0, 15)], axis=0), ones
+    )
+    for k, i in enumerate(OUTER):
         for h in range(2):
             half = slice(h * 128, (h + 1) * 128)
-            wide[h, pl.ds(i * 32 + 7, FR, stride=192), :] = act[i * 16 : i * 16 + 8, half] * (keep[i] * keep_left)
-            wide[h, pl.ds(i * 32 + 24, FR, stride=192), :] = act[i * 16 + 8 : i * 16 + 16, half] * (
+            wide[h, pl.ds(k * 32 + 7, FR, stride=128), :] = act[i * 16 : i * 16 + 8, half] * (keep[i] * keep_left)
+            wide[h, pl.ds(k * 32 + 24, FR, stride=128), :] = act[i * 16 + 8 : i * 16 + 16, half] * (
                 keep[i] * keep_right
             )
+    for n, i in enumerate((2, 3)):
+        four = (
+            act[i * 16 : i * 16 + 8] * keep_left,
+            act[96 + n * 16 : 96 + n * 16 + 8],
+            act[96 + n * 16 + 8 : 96 + n * 16 + 16],
+            act[i * 16 + 8 : i * 16 + 16] * keep_right,
+        )
+        for v, value in enumerate(four):
+            for h in range(2):
+                beside[h, n, v, 0:8] = jnp.zeros((8, 128), F32)
+                beside[h, n, v, 8:16] = value[:, h * 128 : (h + 1) * 128]
     for s in range(3):
-        for i in range(6):
+        for k in range(4):
             for t in range(2):
-                a2[s, t, i] = jnp.zeros((16, C2), BF)
+                a2[s, t, k] = jnp.zeros((16, C2), BF)
             for t in range(FR):
-                base = (t * 6 + i) * 32 + 7 + s
+                base = (t * 4 + k) * 32 + 7 + s
                 for h in range(2):
-                    a2[s, t + 2, i, :, h * 128 : (h + 1) * 128] = wide[h, base : base + 16].astype(BF)
-    for i in range(4):
-        total = None
-        for p in range(3):
-            left = jnp.concatenate(
-                [a2[s, p : p + FR, i + q].reshape(FR * 16, C2) for q in range(3) for s in range(3)], axis=1
-            )
-            got = dot(left, k2[p].reshape(9 * C2, C2))
-            total = got if total is None else total + got
-        for t in range(FR):
+                    a2[s, t + 2, k, :, h * 128 : (h + 1) * 128] = wide[h, base : base + 16].astype(BF)
+
+    blank = jnp.zeros((FR, C2), F32)
+
+    def fix(n, p, s):
+        def at(v):
+            return jnp.concatenate([beside[h, n, v, 6 + p : 14 + p] for h in range(2)], axis=1)
+
+        rows = ((at(0), at(1), blank, blank), (at(1), blank, blank, at(2)), (blank, blank, at(2), at(3)))[s]
+        return jnp.concatenate(rows, axis=0).astype(BF)
+
+    for q in range(3):
+        whole = [(i, OUTER.index(i + q)) for i in range(4) if i + q in OUTER]
+        left = jnp.concatenate(
+            [
+                jnp.concatenate(
+                    [a2[s, p : p + FR, k].reshape(FR * 16, C2) for _, k in whole] + [fix(n, p, s) for n in range(2)],
+                    axis=0,
+                )
+                for p in range(3)
+                for s in range(3)
+            ],
+            axis=1,
+        )
+        right = jnp.concatenate([k2[p, q].reshape(3 * C2, C2) for p in range(3)], axis=0)
+        got = dot(left, right)
+        for h in range(2):
+            half = slice(h * 128, (h + 1) * 128)
+            for n, (i, _) in enumerate(whole):
+                mid[h, i * 128 : (i + 1) * 128] = (mid_in if q == 0 else mid)[h, i * 128 : (i + 1) * 128] + got[
+                    n * 128 : (n + 1) * 128, half
+                ]
+            if q == 0:
+                for i in range(4):
+                    if i not in [i for i, _ in whole]:
+                        mid[h, i * 128 : (i + 1) * 128] = mid_in[h, i * 128 : (i + 1) * 128]
+            for n in range(2):
+                for v, j in enumerate(FIXED):
+                    at = pl.ds((2 - q + n) * 128 + j, FR, stride=16)
+                    mid[h, at, :] += got[256 + n * 32 + v * 8 : 256 + n * 32 + v * 8 + 8, half]
+    for t in range(FR):
+        for i in range(4):
             at = (t * 6 + i + 1) * 16
-            out[t, i] = (level(at, 16) + total[t * 16 : (t + 1) * 16]).astype(BF)
+            sums = jnp.concatenate([mid[h, i * 128 + t * 16 : i * 128 + t * 16 + 16] for h in range(2)], axis=1)
+            out[t, i] = (level(at, 16) + sums).astype(BF)
 
 
 def in_vmem(shape, dtype):
@@ -342,6 +491,7 @@
 W_SHAPE = in_vmem((3, 4, 512, C2), BF)
 M_SHAPE = in_vmem((512, C2), BF)
 ACC_SHAPE = in_vmem((2, FR, 6, 16, 128), F32)
+MID_SHAPE = in_vmem((2, 4 * FR * 16, 128), F32)
 EDGE_SHAPE = in_vmem((96, C2), F32)
 STRIP_SHAPE = in_vmem((6, 16, C2), BF)
 PARAMS = pltpu.CompilerParams(vmem_limit_bytes=24 * 2**20)
@@ -351,38 +501,43 @@
     return pltpu.with_memory_space_constraint(x, pltpu.HBM)
 
 
-def weight_scratch():
-    return [
-        pltpu.VMEM((3, 3, 3, C1, C1), BF),
-        pltpu.VMEM((4 * C1, C2), BF),
-    ]
-
-
 def first_part(feat, k1, proj):
     return pl.pallas_call(
         first_kernel,
-        out_shape=(ROWS_SHAPE,) * 3 + (W_SHAPE, M_SHAPE),
+        out_shape=(ROWS_SHAPE,) * 3 + (W_SHAPE, M_SHAPE) + tuple(in_vmem(x.shape, x.dtype) for x in (feat, k1)),
         in_specs=[HBM] * 3,
-        out_specs=(VM,) * 5,
-        scratch_shapes=[pltpu.SemaphoreType.DMA((2, FR))] + weight_scratch() + [pltpu.SemaphoreType.DMA((2,))],
+        out_specs=(VM,) * 7,
+        scratch_shapes=[
+            pltpu.SemaphoreType.DMA((2, FR)),
+            pltpu.SemaphoreType.DMA,
+            pltpu.VMEM(proj.shape, proj.dtype),
+            pltpu.SemaphoreType.DMA((2,)),
+        ],
         compiler_params=PARAMS,
         name="first_part",
     )(in_hbm(feat), in_hbm(k1), in_hbm(proj))
 
 
-def own_part(feat, k1, proj, w, m):
+def own_part(feat, k1, proj, k2, w, m, feat_in, k1_in):
     return pl.pallas_call(
         own_kernel,
-        out_shape=(W_SHAPE, M_SHAPE, ACC_SHAPE, EDGE_SHAPE),
-        in_specs=[HBM] * 3 + [VM] * 2,
-        out_specs=(VM,) * 4,
-        scratch_shapes=weight_scratch()
-        + [pltpu.VMEM((FR, RW, CL, C1), BF), pltpu.SemaphoreType.DMA((2,)), pltpu.SemaphoreType.DMA]
+        out_shape=(W_SHAPE, M_SHAPE)
+        + tuple(in_vmem(x.shape, x.dtype) for x in (feat, k1))
+        + (ACC_SHAPE, EDGE_SHAPE, in_vmem(k2.shape, k2.dtype), MID_SHAPE),
+        in_specs=[HBM] * 4 + [VM] * 4,
+        out_specs=(VM,) * 8,
+        scratch_shapes=[
+            pltpu.VMEM(proj.shape, proj.dtype),
+            pltpu.SemaphoreType.DMA((2,)),
+            pltpu.SemaphoreType.DMA((2,)),
+            pltpu.VMEM((2, FR * 2 * 32, 128), F32),
+            pltpu.VMEM((3, FR + 2, 2, 16, C2), BF),
+        ]
         + operands(RW),
-        input_output_aliases={3: 0, 4: 1},
+        input_output_aliases={4: 0, 5: 1, 6: 2, 7: 3},
         compiler_params=PARAMS,
         name="own_part",
-    )(in_hbm(feat), in_hbm(k1), in_hbm(proj), w, m)
+    )(in_hbm(feat), in_hbm(k1), in_hbm(proj), in_hbm(k2), w, m, feat_in, k1_in)
 
 
 def near_part(got, w, m, acc, edge):
@@ -404,31 +559,33 @@
         out_shape=(ACC_SHAPE, EDGE_SHAPE, STRIP_SHAPE, STRIP_SHAPE),
         in_specs=[VM] * 6,
         out_specs=(VM,) * 4,
-        scratch_shapes=operands(HALO),
+        scratch_shapes=operands(HALO) + operands(HALO),
         input_output_aliases={4: 0, 5: 1},
         compiler_params=PARAMS,
         name="far_part",
     )(got, got_near, w, m, acc, edge)
 
 
-def final_part(last_row, last_col, from_b, pair, acc, edge, k2):
+def final_part(last_row, last_col, from_b, pair, acc, edge, k2, mid):
     def kernel(*refs):
         final_kernel(last_row, last_col, *refs)
 
     return pl.pallas_call(
         kernel,
         out_shape=in_vmem((FR, 4, 16, C2), BF),
-        in_specs=[VM] * 5,
+        in_specs=[VM] * 6,
         out_specs=VM,
         scratch_shapes=[
+            pltpu.VMEM(MID_SHAPE.shape, F32),
             pltpu.VMEM((2, FR * 6 * 16, 128), F32),
             pltpu.VMEM((96, C2), F32),
-            pltpu.VMEM((2, FR * 6 * 32, 128), F32),
-            pltpu.VMEM((3, FR + 2, 6, 16, C2), BF),
+            pltpu.VMEM((2, FR * 4 * 32, 128), F32),
+            pltpu.VMEM((3, FR + 2, 4, 16, C2), BF),
+            pltpu.VMEM((2, 2, 4, 16, 128), F32),
         ],
         compiler_params=PARAMS,
         name="final_part",
-    )(from_b, pair, acc, edge, k2)
+    )(from_b, pair, acc, edge, k2, mid)
 
 
 def pairs(first, count):
@@ -440,18 +597,18 @@
 
 def local(features, kernel_one, projection, kernel_two):
     rows, cols = lax.axis_size("row"), lax.axis_size("col")
-    send_b, send_a, send_a_too, w, m = first_part(features, kernel_one, projection)
+    send_b, send_a, send_a_too, w, m, *here = first_part(features, kernel_one, projection)
     far_side = [(i, j) for i, j in pairs(0, rows) if min(i, j) % FAR == 0]
     others = [pair for pair in pairs(0, rows) if pair not in far_side]
     from_a = lax.ppermute(send_a, "row", far_side)
     from_b = lax.ppermute(send_b, "row", pairs(1, rows))
     from_a_too = lax.ppermute(send_a_too, "row", others)
-    w, m, acc, edge = own_part(features, kernel_one, projection, w, m)
+    w, m, _, _, acc, edge, kernel_two, mid = own_part(features, kernel_one, projection, kernel_two, w, m, *here)
     acc, edge = near_part(from_a, w, m, acc, edge)
     acc, edge, to_b, to_a = far_part(from_b, from_a_too, w, m, acc, edge)
     from_b = lax.ppermute(to_b, "col", pairs(1, cols))
     pair = lax.all_gather(to_a, "col", axis_index_groups=[[i, i + 1] for i in range(0, cols, 2)])
-    return final_part(rows - 1, cols - 1, from_b, pair, acc, edge, kernel_two)
+    return final_part(rows - 1, cols - 1, from_b, pair, acc, edge, kernel_two, mid)
 
 
 def solution(mesh):

time: 35.4 us -> 34.7 us (0.980)
  Pallas kernels: 12.7 us -> 12.1 us
    pallas_call x1, Pallas kernels: 3.65 us -> 5.18 us  [own_part(): pl.pallas_call(own_kernel, out_shape=(W_SHAPE, M_SHAPE) + tuple((in_vmem(...]
    ppermute x1, starting transfers between devices: 5.21 us -> 3.81 us  [local(): from_b = lax.ppermute(to_b, 'col', pairs(1, cols))]
    pallas_call x1, Pallas kernels: 3.79 us -> 2.41 us  [first_part(): pl.pallas_call(first_kernel, out_shape=(ROWS_SHAPE,) * 3 + (W_SHAPE, M_SH...]
    ppermute x1, starting transfers between devices: 1.92 us -> 2.71 us  [local(): from_a = lax.ppermute(send_a, 'row', far_side)]
    pallas_call x1, Pallas kernels: 3.27 us -> 2.58 us  [final_part(): pl.pallas_call(kernel, out_shape=in_vmem((FR, 4, 16, C2), BF), in_specs=[...]
    ppermute x1, starting transfers between devices: 12.3 us -> 12.9 us  [local(): from_b = lax.ppermute(send_b, 'row', pairs(1, rows))]
  transfers between devices with their start and end apart: 4 -> 4, of which waited for: 0 -> 0; matrix products, arithmetic and copies ran while one was open for 0% -> 0% of each run, Pallas kernels for 13% -> 18%
where the time goes in v6:
time: 34.7 us; the launch traced here: 34.2 us
  starting transfers between devices  20.1 us (58%)
  Pallas kernels  12.1 us (35%)
  blocking collectives  1.88 us (5%)
    ppermute x1, starting transfers between devices, local(): from_b = lax.ppermute(send_b, 'row', pairs(1, rows))  12.9 us
    pallas_call x1, Pallas kernels, own_part(): pl.pallas_call(own_kernel, out_shape=(W_SHAPE, M_SHAPE) + tuple((in_vmem(...  5.18 us
    ppermute x1, starting transfers between devices, local(): from_b = lax.ppermute(to_b, 'col', pairs(1, cols))  3.81 us
    ppermute x1, starting transfers between devices, local(): from_a = lax.ppermute(send_a, 'row', far_side)  2.71 us
    pallas_call x1, Pallas kernels, final_part(): pl.pallas_call(kernel, out_shape=in_vmem((FR, 4, 16, C2), BF), in_specs=[...  2.58 us
    pallas_call x1, Pallas kernels, first_part(): pl.pallas_call(first_kernel, out_shape=(ROWS_SHAPE,) * 3 + (W_SHAPE, M_SH...  2.41 us
    all_gather x1, blocking collectives, local(): lax.all_gather(to_a, 'col', axis_index_groups=[[i, i + 1] for i in range(...  1.88 us
    pallas_call x1, Pallas kernels, far_part(): pl.pallas_call(far_kernel, out_shape=(ACC_SHAPE, EDGE_SHAPE, STRIP_SHAPE,...  1.02 us
  transfers between devices with their start and end apart: 4, of which 0 were waited for; matrix products, arithmetic and copies ran while one was open for 0% of the time, Pallas kernels for 18%

profile of v6, /device:TPU:7, one launch (start us, length us, event | category | flops | bytes accessed | tf_op | source)
XLA Modules:
  0.0 34.2 jit_solution(4049248472824048683)
XLA Ops:
  0.0 2.4 %first_part.1 = (bf16[8,3,32,128]{3,2,1,0:T(8,128)(2,1)S(1)}, bf16[8,3,32,128]{3,2,1,0:T(8,128)(2,1)S(1)}, bf16[8,3,32,128]{3,2,1,0:T(8,128)(2,1)S(1)}, bf16[3,4...) custom-call(bf16[8,8,32,128]{3,2,1,0:T(8,128)(2,1)} %feat.3, ...), custom_call_target="tpu_custom_call" | custom-call | tf_op jit(solution)/shard_map/first_part/pallas_call | solution.py:505
  2.4 2.7 %collective-permute-start.2 = (bf16[8,3,32,128]{3,2,1,0:T(8,128)(2,1)S(1)}, bf16[8,3,32,128]{3,2,1,0:T(8,128)(2,1)S(1)}, u32[]{:S(2)}, u32[]{:S(2)}) collective-permute-start(bf16[8,3,32,128]{3,2,1,0:T(8,128)(2,1)S(1)} %get-tuple-element.32), channel_id=1, source_target_pairs={{0,8},{8,0},{128,136},{136,128},{256,264},{264,256},{384,392},{392... | collective-permute-start | bytes 589832 | tf_op jit(solution)/shard_map/ppermute | solution.py:603
  5.1 12.9 %collective-permute-start = (bf16[8,3,32,128]{3,2,1,0:T(8,128)(2,1)S(1)}, bf16[8,3,32,128]{3,2,1,0:T(8,128)(2,1)S(1)}, u32[]{:S(2)}, u32[]{:S(2)}) collective-permute-start(bf16[8,3,32,128]{3,2,1,0:T(8,128)(2,1)S(1)} %get-tuple-element.24), channel_id=1, source_target_pairs={{8,16},{16,8},{24,32},{32,24},{40,48},{48,40},{56,64},{64,56},{72,... | collective-permute-start | bytes 589832 | tf_op jit(solution)/shard_map/ppermute | solution.py:604
  18.0 0.7 %collective-permute-start.1 = (bf16[8,3,32,128]{3,2,1,0:T(8,128)(2,1)S(1)}, bf16[8,3,32,128]{3,2,1,0:T(8,128)(2,1)S(1)}, u32[]{:S(2)}, u32[]{:S(2)}) collective-permute-start(bf16[8,3,32,128]{3,2,1,0:T(8,128)(2,1)S(1)} %get-tuple-element.25), channel_id=1, source_target_pairs={{16,24},{24,16},{32,40},{40,32},{48,56},{56,48},{64,72},{72,64},{8... | collective-permute-start | bytes 589832 | tf_op jit(solution)/shard_map/ppermute | solution.py:605
  18.7 5.2 %own_part.1 = (bf16[3,4,512,256]{3,2,1,0:T(8,128)(2,1)S(1)}, bf16[512,256]{1,0:T(8,128)(2,1)S(1)}, bf16[8,8,32,128]{3,2,1,0:T(8,128)(2,1)S(1)}, bf16[3,3,3,128,1...) custom-call(bf16[8,8,32,128]{3,2,1,0:T(8,128)(2,1)} %feat.3, ...), custom_call_target="tpu_custom_call", output_to_operand_aliasing={{0}: (4, {}), {1}: (5, {}), {2}: (6, {}), {3}: (7, {})} | custom-call | tf_op jit(solution)/shard_map/own_part/pallas_call | solution.py:522
  23.9 0.0 collective-permute-done.2.got
  23.9 1.0 %near_part.1 = (f32[2,8,6,16,128]{4,3,2,1,0:T(8,128)S(1)}, f32[96,256]{1,0:T(8,128)S(1)}) custom-call(bf16[8,3,32,128]{3,2,1,0:T(8,128)(2,1)S(1)} %collective-permute-done.2.got, bf16[3,4,512,256]{3,2,1,0:T(8,128)(2,1)S(1)} %get-tuple-element.30.w, bf16[512,256]{1,0:T(8,128)(2,1)S(1)} %get-tuple-element.31.m, ...), custom_call_target="tpu_custom_call", output_to_operand_aliasing={{0}: (3, {}), {1}: (4, {})} | custom-call | tf_op jit(solution)/shard_map/near_part/pallas_call | solution.py:544
  24.8 0.0 collective-permute-done.got
  24.9 0.0 collective-permute-done.1.got_near
  24.9 1.0 %far_part.1 = (f32[2,8,6,16,128]{4,3,2,1,0:T(8,128)S(1)}, f32[96,256]{1,0:T(8,128)S(1)}, bf16[6,16,256]{2,1,0:T(8,128)(2,1)S(1)}, bf16[6,16,256]{2,1,0:T(8,128)(2,1)S(1)}) custom-call(bf16[8,3,32,128]{3,2,1,0:T(8,128)(2,1)S(1)} %collective-permute-done.got, ...), custom_call_target="tpu_custom_call", output_to_operand_aliasing={{0}: (4, {}), {1}: (5, {})} | custom-call | tf_op jit(solution)/shard_map/far_part/pallas_call | solution.py:557
  25.9 3.8 %collective-permute-start.3 = (bf16[6,16,256]{2,1,0:T(8,128)(2,1)S(1)}, bf16[6,16,256]{2,1,0:T(8,128)(2,1)S(1)}, u32[]{:S(2)}, u32[]{:S(2)}) collective-permute-start(bf16[6,16,256]{2,1,0:T(8,128)(2,1)S(1)} %get-tuple-element.37), channel_id=1, source_target_pairs={{1,2},{2,1},{3,4},{4,3},{5,6},{6,5},{9,10},{10,9},{11,12},{12,11},... | collective-permute-start | bytes 147464 | tf_op jit(solution)/shard_map/ppermute | solution.py:609
  29.7 1.9 %all-gather = bf16[12,16,256]{2,1,0:T(8,128)(2,1)S(1)} all-gather(bf16[6,16,256]{2,1,0:T(8,128)(2,1)S(1)} %get-tuple-element.38), channel_id=2, replica_groups={{0,1},{2,3},{4,5},{6,7},{8,9},{10,11},{12,13},{14,15},{16,17},{18,19},{..., dimensions={0}, use_global_device_ids=true | all-gather | bytes 147456 | tf_op jit(solution)/shard_map/all_gather | solution.py:610
  31.6 0.0 collective-permute-done.3.refs_0_
  31.6 2.6 %final_part.1 = bf16[8,4,16,256]{3,2,1,0:T(8,128)(2,1)} custom-call(bf16[6,16,256]{2,1,0:T(8,128)(2,1)S(1)} %collective-permute-done.3.refs_0_, bf16[2,6,16,256]{3,2,1,0:T(8,128)(2,1)S(1)} %bitcast.1, f32[2,8,6,16,128]{4,3,2,1,0:T(8,128)S(1)} %get-tuple-element.39.refs_2_, f32[96,256]{1,0:T(8,128)S(1)} %get-tuple-element.40.refs_3_, ...), custom_call_target="tpu_custom_call" | custom-call | tf_op jit(solution)/shard_map/final_part/pallas_call | solution.py:573
Async XLA Ops:
  2.4 21.5 %collective-permute-start.2 = (bf16[8,3,32,128]{3,2,1,0:T(8,128)(2,1)S(1)}, bf16[8,3,32,128]{3,2,1,0:T(8,128)(2,1)S(1)}, u32[]{:S(2)}, u32[]{:S(2)}) collective-permute-start(bf16[8,3,32,128]{3,2,1,0:T(8,128)(2,1)S(1)} %get-tuple-element.32), channel_id=1, source_target_pairs={{0,8},{8,0},{128,136},{136,128},{256,264},{264,256},{384,392},{392... | collective-permute-start | bytes 589832 | tf_op jit(solution)/shard_map/ppermute | solution.py:603
  5.1 19.7 %collective-permute-start = (bf16[8,3,32,128]{3,2,1,0:T(8,128)(2,1)S(1)}, bf16[8,3,32,128]{3,2,1,0:T(8,128)(2,1)S(1)}, u32[]{:S(2)}, u32[]{:S(2)}) collective-permute-start(bf16[8,3,32,128]{3,2,1,0:T(8,128)(2,1)S(1)} %get-tuple-element.24), channel_id=1, source_target_pairs={{8,16},{16,8},{24,32},{32,24},{40,48},{48,40},{56,64},{64,56},{72,... | collective-permute-start | bytes 589832 | tf_op jit(solution)/shard_map/ppermute | solution.py:604
  18.0 6.9 %collective-permute-start.1 = (bf16[8,3,32,128]{3,2,1,0:T(8,128)(2,1)S(1)}, bf16[8,3,32,128]{3,2,1,0:T(8,128)(2,1)S(1)}, u32[]{:S(2)}, u32[]{:S(2)}) collective-permute-start(bf16[8,3,32,128]{3,2,1,0:T(8,128)(2,1)S(1)} %get-tuple-element.25), channel_id=1, source_target_pairs={{16,24},{24,16},{32,40},{40,32},{48,56},{56,48},{64,72},{72,64},{8... | collective-permute-start | bytes 589832 | tf_op jit(solution)/shard_map/ppermute | solution.py:605
  25.9 5.7 %collective-permute-start.3 = (bf16[6,16,256]{2,1,0:T(8,128)(2,1)S(1)}, bf16[6,16,256]{2,1,0:T(8,128)(2,1)S(1)}, u32[]{:S(2)}, u32[]{:S(2)}) collective-permute-start(bf16[6,16,256]{2,1,0:T(8,128)(2,1)S(1)} %get-tuple-element.37), channel_id=1, source_target_pairs={{1,2},{2,1},{3,4},{4,3},{5,6},{6,5},{9,10},{10,9},{11,12},{12,11},... | collective-permute-start | bytes 147464 | tf_op jit(solution)/shard_map/ppermute | solution.py:609

commit v7 on v6

--- a/solution.py
+++ b/solution.py
@@ -360,12 +360,16 @@
 FIXED = (0, 1, 14, 15)
 
 
-def final_kernel(last_row, last_col, from_b, pair, acc, edge_in, k2, mid_in, out, mid, lv, edge, wide, a2, beside):
+def final_kernel(
+    last_row, last_col, from_b, pair, acc_in, edge_in, k2, mid_in, out, acc, mid, edge, wide, a2, beside
+):
     row, col = lax.axis_index("row"), lax.axis_index("col")
     odd = col % 2 == 1
-    for t in range(FR):
-        for h in range(2):
-            lv[h, t * 96 : (t + 1) * 96] = acc[h, t].reshape(96, 128)
+    flat = acc.reshape(2 * FR * 6 * 16, 128)
+
+    def lines(h, i, j):
+        return pl.ds(h * FR * 96 + i * 16 + j, FR, stride=96)
+
     for i in range(6):
         fb = from_b[i].astype(F32)
         left = jnp.where(odd, pair[0, i].astype(F32), fb)
@@ -374,11 +378,8 @@
         edge[i * 16 + 8 : i * 16 + 16] = edge_in[i * 16 + 8 : i * 16 + 16] + right[8:16]
         for h in range(2):
             half = slice(h * 128, (h + 1) * 128)
-            lv[h, pl.ds(i * 16, FR, stride=96), :] += left[8:16, half]
-            lv[h, pl.ds(i * 16 + 15, FR, stride=96), :] += right[0:8, half]
-
-    def level(at, count):
-        return jnp.concatenate([lv[0, at : at + count], lv[1, at : at + count]], axis=1)
+            flat[lines(h, i, 0), :] += left[8:16, half]
+            flat[lines(h, i, 15), :] += right[0:8, half]
 
     ones = mean_matrix(C2)
     keep = {i: jnp.float32(1.0) for i in range(6)}
@@ -386,40 +387,39 @@
     keep[5] = jnp.where(row == last_row, 0.0, 1.0)
     keep_left = jnp.where(col == 0, 0.0, 1.0)
     keep_right = jnp.where(col == last_col, 0.0, 1.0)
-    for t in range(FR):
-        act = normed_silu(jnp.concatenate([level(t * 96, 32), level(t * 96 + 64, 32)], axis=0), ones)
-        for k, i in enumerate(OUTER):
-            base = (t * 4 + k) * 32 + 8
-            kept = act[k * 16 : (k + 1) * 16] * keep[i]
-            for h in range(2):
-                wide[h, base : base + 16] = kept[:, h * 128 : (h + 1) * 128]
 
     def column(i, j):
-        return jnp.concatenate([lv[h, pl.ds(i * 16 + j, FR, stride=96), :] for h in range(2)], axis=1)
-
-    act = normed_silu(
+        return jnp.concatenate([flat[lines(h, i, j), :] for h in range(2)], axis=1)
+
+    rim = normed_silu(
         jnp.concatenate([edge[...]] + [column(i, j) for i in (2, 3) for j in (0, 15)], axis=0), ones
     )
-    for k, i in enumerate(OUTER):
-        for h in range(2):
-            half = slice(h * 128, (h + 1) * 128)
-            wide[h, pl.ds(k * 32 + 7, FR, stride=128), :] = act[i * 16 : i * 16 + 8, half] * (keep[i] * keep_left)
-            wide[h, pl.ds(k * 32 + 24, FR, stride=128), :] = act[i * 16 + 8 : i * 16 + 16, half] * (
-                keep[i] * keep_right
-            )
     for n, i in enumerate((2, 3)):
         four = (
-            act[i * 16 : i * 16 + 8] * keep_left,
-            act[96 + n * 16 : 96 + n * 16 + 8],
-            act[96 + n * 16 + 8 : 96 + n * 16 + 16],
-            act[i * 16 + 8 : i * 16 + 16] * keep_right,
+            rim[i * 16 : i * 16 + 8] * keep_left,
+            rim[96 + n * 16 : 96 + n * 16 + 8],
+            rim[96 + n * 16 + 8 : 96 + n * 16 + 16],
+            rim[i * 16 + 8 : i * 16 + 16] * keep_right,
         )
         for v, value in enumerate(four):
             for h in range(2):
                 beside[h, n, v, 0:8] = jnp.zeros((8, 128), F32)
                 beside[h, n, v, 8:16] = value[:, h * 128 : (h + 1) * 128]
-    for s in range(3):
-        for k in range(4):
+
+    def activate(k):
+        i = OUTER[k]
+        x = jnp.concatenate([acc[h, :, i].reshape(FR * 16, 128) for h in range(2)], axis=1)
+        act = normed_silu(x, ones) * keep[i]
+        for h in range(2):
+            half = slice(h * 128, (h + 1) * 128)
+            for t in range(FR):
+                base = (t * 4 + k) * 32 + 8
+                wide[h, base : base + 16] = act[t * 16 : (t + 1) * 16, half]
+            wide[h, pl.ds(k * 32 + 7, FR, stride=128), :] = rim[i * 16 : i * 16 + 8, half] * (keep[i] * keep_left)
+            wide[h, pl.ds(k * 32 + 24, FR, stride=128), :] = rim[i * 16 + 8 : i * 16 + 16, half] * (
+                keep[i] * keep_right
+            )
+        for s in range(3):
             for t in range(2):
                 a2[s, t, k] = jnp.zeros((16, C2), BF)
             for t in range(FR):
@@ -436,7 +436,7 @@
         rows = ((at(0), at(1), blank, blank), (at(1), blank, blank, at(2)), (blank, blank, at(2), at(3)))[s]
         return jnp.concatenate(rows, axis=0).astype(BF)
 
-    for q in range(3):
+    def convolve(q):
         whole = [(i, OUTER.index(i + q)) for i in range(4) if i + q in OUTER]
         left = jnp.concatenate(
             [
@@ -454,22 +454,25 @@
         for h in range(2):
             half = slice(h * 128, (h + 1) * 128)
             for n, (i, _) in enumerate(whole):
-                mid[h, i * 128 : (i + 1) * 128] = (mid_in if q == 0 else mid)[h, i * 128 : (i + 1) * 128] + got[
-                    n * 128 : (n + 1) * 128, half
-                ]
-            if q == 0:
-                for i in range(4):
-                    if i not in [i for i, _ in whole]:
-                        mid[h, i * 128 : (i + 1) * 128] = mid_in[h, i * 128 : (i + 1) * 128]
+                mid[h, i * 128 : (i + 1) * 128] += got[n * 128 : (n + 1) * 128, half]
             for n in range(2):
                 for v, j in enumerate(FIXED):
                     at = pl.ds((2 - q + n) * 128 + j, FR, stride=16)
                     mid[h, at, :] += got[256 + n * 32 + v * 8 : 256 + n * 32 + v * 8 + 8, half]
+
+    activate(0)
+    activate(1)
+    convolve(0)
+    activate(2)
+    activate(3)
+    convolve(2)
+    convolve(1)
     for t in range(FR):
         for i in range(4):
-            at = (t * 6 + i + 1) * 16
-            sums = jnp.concatenate([mid[h, i * 128 + t * 16 : i * 128 + t * 16 + 16] for h in range(2)], axis=1)
-            out[t, i] = (level(at, 16) + sums).astype(BF)
+            sums = jnp.concatenate(
+                [acc[h, t, i + 1] + mid[h, i * 128 + t * 16 : i * 128 + t * 16 + 16] for h in range(2)], axis=1
+            )
+            out[t, i] = sums.astype(BF)
 
 
 def in_vmem(shape, dtype):
@@ -499,6 +502,10 @@
 
 def in_hbm(x):
     return pltpu.with_memory_space_constraint(x, pltpu.HBM)
+
+
+def held(*xs):
+    return tuple(pltpu.with_memory_space_constraint(x, pltpu.VMEM) for x in xs)
 
 
 def first_part(feat, k1, proj):
@@ -537,7 +544,7 @@
         input_output_aliases={4: 0, 5: 1, 6: 2, 7: 3},
         compiler_params=PARAMS,
         name="own_part",
-    )(in_hbm(feat), in_hbm(k1), in_hbm(proj), in_hbm(k2), w, m, feat_in, k1_in)
+    )(in_hbm(feat), in_hbm(k1), in_hbm(proj), in_hbm(k2), *held(w, m, feat_in, k1_in))
 
 
 def near_part(got, w, m, acc, edge):
@@ -550,7 +557,7 @@
         input_output_aliases={3: 0, 4: 1},
         compiler_params=PARAMS,
         name="near_part",
-    )(got, w, m, acc, edge)
+    )(got, w, m, *held(acc, edge))
 
 
 def far_part(got, got_near, w, m, acc, edge):
@@ -563,7 +570,7 @@
         input_output_aliases={4: 0, 5: 1},
         compiler_params=PARAMS,
         name="far_part",
-    )(got, got_near, w, m, acc, edge)
+    )(got, got_near, w, m, *held(acc, edge))
 
 
 def final_part(last_row, last_col, from_b, pair, acc, edge, k2, mid):
@@ -572,20 +579,19 @@
 
     return pl.pallas_call(
         kernel,
-        out_shape=in_vmem((FR, 4, 16, C2), BF),
+        out_shape=(in_vmem((FR, 4, 16, C2), BF), ACC_SHAPE, MID_SHAPE),
         in_specs=[VM] * 6,
-        out_specs=VM,
+        out_specs=(VM,) * 3,
         scratch_shapes=[
-            pltpu.VMEM(MID_SHAPE.shape, F32),
-            pltpu.VMEM((2, FR * 6 * 16, 128), F32),
             pltpu.VMEM((96, C2), F32),
             pltpu.VMEM((2, FR * 4 * 32, 128), F32),
             pltpu.VMEM((3, FR + 2, 4, 16, C2), BF),
             pltpu.VMEM((2, 2, 4, 16, 128), F32),
         ],
+        input_output_aliases={2: 1, 5: 2},
         compiler_params=PARAMS,
         name="final_part",
-    )(from_b, pair, acc, edge, k2, mid)
+    )(from_b, pair, *held(acc), edge, k2, *held(mid))[0]
 
 
 def pairs(first, count):

time: 34.7 us -> 34.6 us (level)
  no operation moved by 1% of the time
where the time goes in v7:
time: 34.6 us; the launch traced here: 34.1 us
  starting transfers between devices  20.1 us (58%)
  Pallas kernels  12.1 us (35%)
  blocking collectives  1.88 us (5%)
    ppermute x1, starting transfers between devices, local(): from_b = lax.ppermute(send_b, 'row', pairs(1, rows))  12.9 us
    pallas_call x1, Pallas kernels, own_part(): pl.pallas_call(own_kernel, out_shape=(W_SHAPE, M_SHAPE) + tuple((in_vmem(...  5.18 us
    ppermute x1, starting transfers between devices, local(): from_b = lax.ppermute(to_b, 'col', pairs(1, cols))  3.81 us
    ppermute x1, starting transfers between devices, local(): from_a = lax.ppermute(send_a, 'row', far_side)  2.71 us
    pallas_call x1, Pallas kernels, final_part(): pl.pallas_call(kernel, out_shape=(in_vmem((FR, 4, 16, C2), BF), ACC_SHAPE...  2.51 us
    pallas_call x1, Pallas kernels, first_part(): pl.pallas_call(first_kernel, out_shape=(ROWS_SHAPE,) * 3 + (W_SHAPE, M_SH...  2.41 us
    all_gather x1, blocking collectives, local(): lax.all_gather(to_a, 'col', axis_index_groups=[[i, i + 1] for i in range(...  1.88 us
    pallas_call x1, Pallas kernels, far_part(): pl.pallas_call(far_kernel, out_shape=(ACC_SHAPE, EDGE_SHAPE, STRIP_SHAPE,...  1.02 us
  transfers between devices with their start and end apart: 4, of which 0 were waited for; matrix products, arithmetic and copies ran while one was open for 0% of the time, Pallas kernels for 18%

profile of v7, /device:TPU:7, one launch (start us, length us, event | category | flops | bytes accessed | tf_op | source)
XLA Modules:
  0.0 34.1 jit_solution(1086534000376758050)
XLA Ops:
  0.0 2.4 %first_part.1 = (bf16[8,3,32,128]{3,2,1,0:T(8,128)(2,1)S(1)}, bf16[8,3,32,128]{3,2,1,0:T(8,128)(2,1)S(1)}, bf16[8,3,32,128]{3,2,1,0:T(8,128)(2,1)S(1)}, bf16[3,4...) custom-call(bf16[8,8,32,128]{3,2,1,0:T(8,128)(2,1)} %feat.3, ...), custom_call_target="tpu_custom_call" | custom-call | tf_op jit(solution)/shard_map/first_part/pallas_call | solution.py:512
  2.4 2.7 %collective-permute-start.2 = (bf16[8,3,32,128]{3,2,1,0:T(8,128)(2,1)S(1)}, bf16[8,3,32,128]{3,2,1,0:T(8,128)(2,1)S(1)}, u32[]{:S(2)}, u32[]{:S(2)}) collective-permute-start(bf16[8,3,32,128]{3,2,1,0:T(8,128)(2,1)S(1)} %get-tuple-element.33), channel_id=1, source_target_pairs={{0,8},{8,0},{128,136},{136,128},{256,264},{264,256},{384,392},{392... | collective-permute-start | bytes 589832 | tf_op jit(solution)/shard_map/ppermute | solution.py:609
  5.1 12.9 %collective-permute-start = (bf16[8,3,32,128]{3,2,1,0:T(8,128)(2,1)S(1)}, bf16[8,3,32,128]{3,2,1,0:T(8,128)(2,1)S(1)}, u32[]{:S(2)}, u32[]{:S(2)}) collective-permute-start(bf16[8,3,32,128]{3,2,1,0:T(8,128)(2,1)S(1)} %get-tuple-element.25), channel_id=1, source_target_pairs={{8,16},{16,8},{24,32},{32,24},{40,48},{48,40},{56,64},{64,56},{72,... | collective-permute-start | bytes 589832 | tf_op jit(solution)/shard_map/ppermute | solution.py:610
  18.0 0.7 %collective-permute-start.1 = (bf16[8,3,32,128]{3,2,1,0:T(8,128)(2,1)S(1)}, bf16[8,3,32,128]{3,2,1,0:T(8,128)(2,1)S(1)}, u32[]{:S(2)}, u32[]{:S(2)}) collective-permute-start(bf16[8,3,32,128]{3,2,1,0:T(8,128)(2,1)S(1)} %get-tuple-element.26), channel_id=1, source_target_pairs={{16,24},{24,16},{32,40},{40,32},{48,56},{56,48},{64,72},{72,64},{8... | collective-permute-start | bytes 589832 | tf_op jit(solution)/shard_map/ppermute | solution.py:611
  18.7 5.2 %own_part.1 = (bf16[3,4,512,256]{3,2,1,0:T(8,128)(2,1)S(1)}, bf16[512,256]{1,0:T(8,128)(2,1)S(1)}, bf16[8,8,32,128]{3,2,1,0:T(8,128)(2,1)S(1)}, bf16[3,3,3,128,1...) custom-call(bf16[8,8,32,128]{3,2,1,0:T(8,128)(2,1)} %feat.3, ...), custom_call_target="tpu_custom_call", output_to_operand_aliasing={{0}: (4, {}), {1}: (5, {}), {2}: (6, {}), {3}: (7, {})} | custom-call | tf_op jit(solution)/shard_map/own_part/pallas_call | solution.py:529
  23.9 0.0 collective-permute-done.2.got
  23.9 1.0 %near_part.1 = (f32[2,8,6,16,128]{4,3,2,1,0:T(8,128)S(1)}, f32[96,256]{1,0:T(8,128)S(1)}) custom-call(bf16[8,3,32,128]{3,2,1,0:T(8,128)(2,1)S(1)} %collective-permute-done.2.got, bf16[3,4,512,256]{3,2,1,0:T(8,128)(2,1)S(1)} %get-tuple-element.31.w, bf16[512,256]{1,0:T(8,128)(2,1)S(1)} %get-tuple-element.32.m, ...), custom_call_target="tpu_custom_call", output_to_operand_aliasing={{0}: (3, {}), {1}: (4, {})} | custom-call | tf_op jit(solution)/shard_map/near_part/pallas_call | solution.py:551
  24.8 0.0 collective-permute-done.got
  24.9 0.0 collective-permute-done.1.got_near
  24.9 1.0 %far_part.1 = (f32[2,8,6,16,128]{4,3,2,1,0:T(8,128)S(1)}, f32[96,256]{1,0:T(8,128)S(1)}, bf16[6,16,256]{2,1,0:T(8,128)(2,1)S(1)}, bf16[6,16,256]{2,1,0:T(8,128)(2,1)S(1)}) custom-call(bf16[8,3,32,128]{3,2,1,0:T(8,128)(2,1)S(1)} %collective-permute-done.got, ...), custom_call_target="tpu_custom_call", output_to_operand_aliasing={{0}: (4, {}), {1}: (5, {})} | custom-call | tf_op jit(solution)/shard_map/far_part/pallas_call | solution.py:564
  25.9 3.8 %collective-permute-start.3 = (bf16[6,16,256]{2,1,0:T(8,128)(2,1)S(1)}, bf16[6,16,256]{2,1,0:T(8,128)(2,1)S(1)}, u32[]{:S(2)}, u32[]{:S(2)}) collective-permute-start(bf16[6,16,256]{2,1,0:T(8,128)(2,1)S(1)} %get-tuple-element.38), channel_id=1, source_target_pairs={{1,2},{2,1},{3,4},{4,3},{5,6},{6,5},{9,10},{10,9},{11,12},{12,11},... | collective-permute-start | bytes 147464 | tf_op jit(solution)/shard_map/ppermute | solution.py:615
  29.7 1.9 %all-gather = bf16[12,16,256]{2,1,0:T(8,128)(2,1)S(1)} all-gather(bf16[6,16,256]{2,1,0:T(8,128)(2,1)S(1)} %get-tuple-element.39), channel_id=2, replica_groups={{0,1},{2,3},{4,5},{6,7},{8,9},{10,11},{12,13},{14,15},{16,17},{18,19},{..., dimensions={0}, use_global_device_ids=true | all-gather | bytes 147456 | tf_op jit(solution)/shard_map/all_gather | solution.py:616
  31.6 0.0 collective-permute-done.3.refs_0_
  31.6 2.5 %final_part.1 = (bf16[8,4,16,256]{3,2,1,0:T(8,128)(2,1)}, f32[2,8,6,16,128]{4,3,2,1,0:T(8,128)S(1)}, f32[2,512,128]{2,1,0:T(8,128)S(1)}) custom-call(bf16[6,16,256]{2,1,0:T(8,128)(2,1)S(1)} %collective-permute-done.3.refs_0_, bf16[2,6,16,256]{3,2,1,0:T(8,128)(2,1)S(1)} %bitcast.1, ...), custom_call_target="tpu_custom_call", output_to_operand_aliasing={{1}: (2, {}), {2}: (5, {})} | custom-call | tf_op jit(solution)/shard_map/final_part/pallas_call | solution.py:580
Async XLA Ops:
  2.4 21.5 %collective-permute-start.2 = (bf16[8,3,32,128]{3,2,1,0:T(8,128)(2,1)S(1)}, bf16[8,3,32,128]{3,2,1,0:T(8,128)(2,1)S(1)}, u32[]{:S(2)}, u32[]{:S(2)}) collective-permute-start(bf16[8,3,32,128]{3,2,1,0:T(8,128)(2,1)S(1)} %get-tuple-element.33), channel_id=1, source_target_pairs={{0,8},{8,0},{128,136},{136,128},{256,264},{264,256},{384,392},{392... | collective-permute-start | bytes 589832 | tf_op jit(solution)/shard_map/ppermute | solution.py:609
  5.1 19.7 %collective-permute-start = (bf16[8,3,32,128]{3,2,1,0:T(8,128)(2,1)S(1)}, bf16[8,3,32,128]{3,2,1,0:T(8,128)(2,1)S(1)}, u32[]{:S(2)}, u32[]{:S(2)}) collective-permute-start(bf16[8,3,32,128]{3,2,1,0:T(8,128)(2,1)S(1)} %get-tuple-element.25), channel_id=1, source_target_pairs={{8,16},{16,8},{24,32},{32,24},{40,48},{48,40},{56,64},{64,56},{72,... | collective-permute-start | bytes 589832 | tf_op jit(solution)/shard_map/ppermute | solution.py:610
  18.0 6.9 %collective-permute-start.1 = (bf16[8,3,32,128]{3,2,1,0:T(8,128)(2,1)S(1)}, bf16[8,3,32,128]{3,2,1,0:T(8,128)(2,1)S(1)}, u32[]{:S(2)}, u32[]{:S(2)}) collective-permute-start(bf16[8,3,32,128]{3,2,1,0:T(8,128)(2,1)S(1)} %get-tuple-element.26), channel_id=1, source_target_pairs={{16,24},{24,16},{32,40},{40,32},{48,56},{56,48},{64,72},{72,64},{8... | collective-permute-start | bytes 589832 | tf_op jit(solution)/shard_map/ppermute | solution.py:611
  25.9 5.7 %collective-permute-start.3 = (bf16[6,16,256]{2,1,0:T(8,128)(2,1)S(1)}, bf16[6,16,256]{2,1,0:T(8,128)(2,1)S(1)}, u32[]{:S(2)}, u32[]{:S(2)}) collective-permute-start(bf16[6,16,256]{2,1,0:T(8,128)(2,1)S(1)} %get-tuple-element.38), channel_id=1, source_target_pairs={{1,2},{2,1},{3,4},{4,3},{5,6},{6,5},{9,10},{10,9},{11,12},{12,11},... | collective-permute-start | bytes 147464 | tf_op jit(solution)/shard_map/ppermute | solution.py:615

commit v8 on v7

--- a/solution.py
+++ b/solution.py
@@ -187,7 +187,7 @@
         for copy in weights:
             copy.wait()
         build_maps(proj_in, m)
-        build_weights((0,), k1_in, w, m)
+        build_weights((0, 1), k1_in, w, m)
 
 
 def middle_columns(acc, tall, act_in):
@@ -249,35 +249,37 @@
     def _():
         copy.wait()
 
+    copy_k2 = pltpu.make_async_copy(k2_far, k2, late_sems.at[1])
+
+    def rest(frames):
+        copy_k2.start()
+        build_weights(frames, k1_in, w, m)
+        ones = mean_matrix(C1)
+        lay_out(lambda t: feat_in[t].reshape(RW * CL, C1), range(RW), ones, wide, plain, a, b, c, f)
+        have = range(HALO, HALO + RW)
+
+        def slot(r):
+            return r - HALO
+
+        for i in (2, 3):
+            put(acc, i, contribute(i, have, slot, w, m, a, b, f))
+        middle_columns(acc, tall, act_in)
+        for i in (0, 1, 4, 5):
+            put(acc, i, contribute(i, have, slot, w, m, a, b, f))
+        edge[...] = ring(range(6), have, slot, w, c)
+        copy_k2.wait()
+        middle(k2, mid, act_in)
+
     @pl.when(make)
     def _():
         for source in sources:
             source.wait()
-
-    copy_k2 = pltpu.make_async_copy(k2_far, k2, late_sems.at[1])
-    copy_k2.start()
-
-    @pl.when(make)
-    def _():
         build_maps(proj_in, m)
-        build_weights((0,), k1_in, w, m)
-
-    build_weights((1, 2), k1_in, w, m)
-    ones = mean_matrix(C1)
-    lay_out(lambda t: feat_in[t].reshape(RW * CL, C1), range(RW), ones, wide, plain, a, b, c, f)
-    have = range(HALO, HALO + RW)
-
-    def slot(r):
-        return r - HALO
-
-    for i in (2, 3):
-        put(acc, i, contribute(i, have, slot, w, m, a, b, f))
-    middle_columns(acc, tall, act_in)
-    for i in (0, 1, 4, 5):
-        put(acc, i, contribute(i, have, slot, w, m, a, b, f))
-    edge[...] = ring(range(6), have, slot, w, c)
-    copy_k2.wait()
-    middle(k2, mid, act_in)
+        rest((0, 1, 2))
+
+    @pl.when(early())
+    def _():
+        rest((2,))
 
 
 def add_side(low, got, w, m, acc_in, edge_in, acc, edge, wide, plain, a, b, c, f):

time: 34.6 us -> 34.6 us (level)
    pallas_call x1, Pallas kernels: 2.41 us -> 2.82 us  [first_part(): pl.pallas_call(first_kernel, out_shape=(ROWS_SHAPE,) * 3 + (W_SHAPE, M_SH...]
    ppermute x1, starting transfers between devices: 2.71 us -> 2.3 us  [local(): from_a = lax.ppermute(send_a, 'row', far_side)]
    pallas_call x1, Pallas kernels: 5.18 us -> 4.81 us  [own_part(): pl.pallas_call(own_kernel, out_shape=(W_SHAPE, M_SHAPE) + tuple((in_vmem(...]
  transfers between devices with their start and end apart: 4 -> 4, of which waited for: 0 -> 0; matrix products, arithmetic and copies ran while one was open for 0% -> 0% of each run, Pallas kernels for 18% -> 17%
where the time goes in v8:
time: 34.6 us; the launch traced here: 34.1 us
  starting transfers between devices  19.8 us (57%)
  Pallas kernels  12.3 us (36%)
  blocking collectives  1.88 us (5%)
    ppermute x1, starting transfers between devices, local(): from_b = lax.ppermute(send_b, 'row', pairs(1, rows))  12.9 us
    pallas_call x1, Pallas kernels, own_part(): pl.pallas_call(own_kernel, out_shape=(W_SHAPE, M_SHAPE) + tuple((in_vmem(...  4.81 us
    ppermute x1, starting transfers between devices, local(): from_b = lax.ppermute(to_b, 'col', pairs(1, cols))  4 us
    pallas_call x1, Pallas kernels, first_part(): pl.pallas_call(first_kernel, out_shape=(ROWS_SHAPE,) * 3 + (W_SHAPE, M_SH...  2.82 us
    pallas_call x1, Pallas kernels, final_part(): pl.pallas_call(kernel, out_shape=(in_vmem((FR, 4, 16, C2), BF), ACC_SHAPE...  2.5 us
    ppermute x1, starting transfers between devices, local(): from_a = lax.ppermute(send_a, 'row', far_side)  2.3 us
    all_gather x1, blocking collectives, local(): lax.all_gather(to_a, 'col', axis_index_groups=[[i, i + 1] for i in range(...  1.88 us
    pallas_call x1, Pallas kernels, far_part(): pl.pallas_call(far_kernel, out_shape=(ACC_SHAPE, EDGE_SHAPE, STRIP_SHAPE,...  1.2 us
  transfers between devices with their start and end apart: 4, of which 0 were waited for; matrix products, arithmetic and copies ran while one was open for 0% of the time, Pallas kernels for 17%

profile of v8, /device:TPU:7, one launch (start us, length us, event | category | flops | bytes accessed | tf_op | source)
XLA Modules:
  0.0 34.1 jit_solution(16307861963132885773)
XLA Ops:
  0.0 2.8 %first_part.1 = (bf16[8,3,32,128]{3,2,1,0:T(8,128)(2,1)S(1)}, bf16[8,3,32,128]{3,2,1,0:T(8,128)(2,1)S(1)}, bf16[8,3,32,128]{3,2,1,0:T(8,128)(2,1)S(1)}, bf16[3,4...) custom-call(bf16[8,8,32,128]{3,2,1,0:T(8,128)(2,1)} %feat.3, ...), custom_call_target="tpu_custom_call" | custom-call | tf_op jit(solution)/shard_map/first_part/pallas_call | solution.py:514
  2.8 2.3 %collective-permute-start.2 = (bf16[8,3,32,128]{3,2,1,0:T(8,128)(2,1)S(1)}, bf16[8,3,32,128]{3,2,1,0:T(8,128)(2,1)S(1)}, u32[]{:S(2)}, u32[]{:S(2)}) collective-permute-start(bf16[8,3,32,128]{3,2,1,0:T(8,128)(2,1)S(1)} %get-tuple-element.33), channel_id=1, source_target_pairs={{0,8},{8,0},{128,136},{136,128},{256,264},{264,256},{384,392},{392... | collective-permute-start | bytes 589832 | tf_op jit(solution)/shard_map/ppermute | solution.py:611
  5.1 12.9 %collective-permute-start = (bf16[8,3,32,128]{3,2,1,0:T(8,128)(2,1)S(1)}, bf16[8,3,32,128]{3,2,1,0:T(8,128)(2,1)S(1)}, u32[]{:S(2)}, u32[]{:S(2)}) collective-permute-start(bf16[8,3,32,128]{3,2,1,0:T(8,128)(2,1)S(1)} %get-tuple-element.25), channel_id=1, source_target_pairs={{8,16},{16,8},{24,32},{32,24},{40,48},{48,40},{56,64},{64,56},{72,... | collective-permute-start | bytes 589832 | tf_op jit(solution)/shard_map/ppermute | solution.py:612
  18.0 0.7 %collective-permute-start.1 = (bf16[8,3,32,128]{3,2,1,0:T(8,128)(2,1)S(1)}, bf16[8,3,32,128]{3,2,1,0:T(8,128)(2,1)S(1)}, u32[]{:S(2)}, u32[]{:S(2)}) collective-permute-start(bf16[8,3,32,128]{3,2,1,0:T(8,128)(2,1)S(1)} %get-tuple-element.26), channel_id=1, source_target_pairs={{16,24},{24,16},{32,40},{40,32},{48,56},{56,48},{64,72},{72,64},{8... | collective-permute-start | bytes 589832 | tf_op jit(solution)/shard_map/ppermute | solution.py:613
  18.7 4.8 %own_part.1 = (bf16[3,4,512,256]{3,2,1,0:T(8,128)(2,1)S(1)}, bf16[512,256]{1,0:T(8,128)(2,1)S(1)}, bf16[8,8,32,128]{3,2,1,0:T(8,128)(2,1)S(1)}, bf16[3,3,3,128,1...) custom-call(bf16[8,8,32,128]{3,2,1,0:T(8,128)(2,1)} %feat.3, ...), custom_call_target="tpu_custom_call", output_to_operand_aliasing={{0}: (4, {}), {1}: (5, {}), {2}: (6, {}), {3}: (7, {})} | custom-call | tf_op jit(solution)/shard_map/own_part/pallas_call | solution.py:531
  23.5 0.0 collective-permute-done.2.got
  23.5 1.0 %near_part.1 = (f32[2,8,6,16,128]{4,3,2,1,0:T(8,128)S(1)}, f32[96,256]{1,0:T(8,128)S(1)}) custom-call(bf16[8,3,32,128]{3,2,1,0:T(8,128)(2,1)S(1)} %collective-permute-done.2.got, bf16[3,4,512,256]{3,2,1,0:T(8,128)(2,1)S(1)} %get-tuple-element.31.w, bf16[512,256]{1,0:T(8,128)(2,1)S(1)} %get-tuple-element.32.m, ...), custom_call_target="tpu_custom_call", output_to_operand_aliasing={{0}: (3, {}), {1}: (4, {})} | custom-call | tf_op jit(solution)/shard_map/near_part/pallas_call | solution.py:553
  24.5 0.0 collective-permute-done.got
  24.5 0.0 collective-permute-done.1.got_near
  24.5 1.2 %far_part.1 = (f32[2,8,6,16,128]{4,3,2,1,0:T(8,128)S(1)}, f32[96,256]{1,0:T(8,128)S(1)}, bf16[6,16,256]{2,1,0:T(8,128)(2,1)S(1)}, bf16[6,16,256]{2,1,0:T(8,128)(2,1)S(1)}) custom-call(bf16[8,3,32,128]{3,2,1,0:T(8,128)(2,1)S(1)} %collective-permute-done.got, ...), custom_call_target="tpu_custom_call", output_to_operand_aliasing={{0}: (4, {}), {1}: (5, {})} | custom-call | tf_op jit(solution)/shard_map/far_part/pallas_call | solution.py:566
  25.7 4.0 %collective-permute-start.3 = (bf16[6,16,256]{2,1,0:T(8,128)(2,1)S(1)}, bf16[6,16,256]{2,1,0:T(8,128)(2,1)S(1)}, u32[]{:S(2)}, u32[]{:S(2)}) collective-permute-start(bf16[6,16,256]{2,1,0:T(8,128)(2,1)S(1)} %get-tuple-element.38), channel_id=1, source_target_pairs={{1,2},{2,1},{3,4},{4,3},{5,6},{6,5},{9,10},{10,9},{11,12},{12,11},... | collective-permute-start | bytes 147464 | tf_op jit(solution)/shard_map/ppermute | solution.py:617
  29.7 1.9 %all-gather = bf16[12,16,256]{2,1,0:T(8,128)(2,1)S(1)} all-gather(bf16[6,16,256]{2,1,0:T(8,128)(2,1)S(1)} %get-tuple-element.39), channel_id=2, replica_groups={{0,1},{2,3},{4,5},{6,7},{8,9},{10,11},{12,13},{14,15},{16,17},{18,19},{..., dimensions={0}, use_global_device_ids=true | all-gather | bytes 147456 | tf_op jit(solution)/shard_map/all_gather | solution.py:618
  31.6 0.0 collective-permute-done.3.refs_0_
  31.6 2.5 %final_part.1 = (bf16[8,4,16,256]{3,2,1,0:T(8,128)(2,1)}, f32[2,8,6,16,128]{4,3,2,1,0:T(8,128)S(1)}, f32[2,512,128]{2,1,0:T(8,128)S(1)}) custom-call(bf16[6,16,256]{2,1,0:T(8,128)(2,1)S(1)} %collective-permute-done.3.refs_0_, bf16[2,6,16,256]{3,2,1,0:T(8,128)(2,1)S(1)} %bitcast.1, ...), custom_call_target="tpu_custom_call", output_to_operand_aliasing={{1}: (2, {}), {2}: (5, {})} | custom-call | tf_op jit(solution)/shard_map/final_part/pallas_call | solution.py:582
Async XLA Ops:
  2.8 20.7 %collective-permute-start.2 = (bf16[8,3,32,128]{3,2,1,0:T(8,128)(2,1)S(1)}, bf16[8,3,32,128]{3,2,1,0:T(8,128)(2,1)S(1)}, u32[]{:S(2)}, u32[]{:S(2)}) collective-permute-start(bf16[8,3,32,128]{3,2,1,0:T(8,128)(2,1)S(1)} %get-tuple-element.33), channel_id=1, source_target_pairs={{0,8},{8,0},{128,136},{136,128},{256,264},{264,256},{384,392},{392... | collective-permute-start | bytes 589832 | tf_op jit(solution)/shard_map/ppermute | solution.py:611
  5.1 19.4 %collective-permute-start = (bf16[8,3,32,128]{3,2,1,0:T(8,128)(2,1)S(1)}, bf16[8,3,32,128]{3,2,1,0:T(8,128)(2,1)S(1)}, u32[]{:S(2)}, u32[]{:S(2)}) collective-permute-start(bf16[8,3,32,128]{3,2,1,0:T(8,128)(2,1)S(1)} %get-tuple-element.25), channel_id=1, source_target_pairs={{8,16},{16,8},{24,32},{32,24},{40,48},{48,40},{56,64},{64,56},{72,... | collective-permute-start | bytes 589832 | tf_op jit(solution)/shard_map/ppermute | solution.py:612
  18.0 6.5 %collective-permute-start.1 = (bf16[8,3,32,128]{3,2,1,0:T(8,128)(2,1)S(1)}, bf16[8,3,32,128]{3,2,1,0:T(8,128)(2,1)S(1)}, u32[]{:S(2)}, u32[]{:S(2)}) collective-permute-start(bf16[8,3,32,128]{3,2,1,0:T(8,128)(2,1)S(1)} %get-tuple-element.26), channel_id=1, source_target_pairs={{16,24},{24,16},{32,40},{40,32},{48,56},{56,48},{64,72},{72,64},{8... | collective-permute-start | bytes 589832 | tf_op jit(solution)/shard_map/ppermute | solution.py:613
  25.7 5.9 %collective-permute-start.3 = (bf16[6,16,256]{2,1,0:T(8,128)(2,1)S(1)}, bf16[6,16,256]{2,1,0:T(8,128)(2,1)S(1)}, u32[]{:S(2)}, u32[]{:S(2)}) collective-permute-start(bf16[6,16,256]{2,1,0:T(8,128)(2,1)S(1)} %get-tuple-element.38), channel_id=1, source_target_pairs={{1,2},{2,1},{3,4},{4,3},{5,6},{6,5},{9,10},{10,9},{11,12},{12,11},... | collective-permute-start | bytes 147464 | tf_op jit(solution)/shard_map/ppermute | solution.py:617
